TPU v7x, 512 devices: a whole 4x8x8 slice. The times are simulated.
512 devices in a mesh: gx: 32 (over z_lo, y), gy: 16 (over z_hi, x, core).
Axes of the slice: x: 4, y: 8, z: 8 (z_hi: 2, z_lo: 4; z = z_hi * 4 + z_lo), core: 2. Of those that a mesh axis runs over, the one named last changes fastest.
Arguments:
- start_state: float32 [5, 256, 256, 256], P(None, 'gx', 'gy'), may hold values from -1.5 to 5.5, as said below
- section_state: float32 [5, 256, 256, 256], P(None, 'gx', 'gy'), may hold values from -1.5 to 5.5, as said below
- previous_speed: float32 [], replicated, may hold values from 1.2 to 2.4
Outputs:
- new_state: float32 [5, 256, 256, 256], P(None, 'gx', 'gy')
- next_speed: float32 [], replicated
Inputs may be any that keep to these rules, and one draw needn't show every extreme that they name: `start_state`: density (component 0) lies in 0.7 to 1.3 and the pressure 0.4 (E - |momentum|^2 / (2 density)) in 0.6 to 1.2 in every cell. `section_state`: density (component 0) lies in 0.7 to 1.3 and the pressure 0.4 (E - |momentum|^2 / (2 density)) in 0.6 to 1.2 in every cell.
All inputs are finite; a program needn't handle non-finite values.
Results may differ from a plain program's by a relative error of at most 0.00002.
Values sent between devices are 32-bit elements; how exact they have to be, the bound alone decides.
No kernel may reach another device: no remote copies, remote signals or barrier semaphores. Data moves between devices by JAX's collectives and lax.ppermute only.
A program may use at most 64 MiB of HBM per device.

v0:
```python
import jax
import jax.numpy as jnp
from jax import lax
from jax.sharding import Mesh
from jax.sharding import PartitionSpec as P

GX_GY = ("gx_0", "gx_1", "gy_0", "gy_1", "gy_2")
GX = ("gx_0", "gx_1")
GY = ("gy_0", "gy_1", "gy_2")


GAMMA = 1.4
COURANT = 0.3
VISCOSITY = 0.05
CONDUCTION = 0.07
FIRST = (0.8, -0.2, 4.0 / 105.0, -1.0 / 280.0)
SECOND = (1.6, -0.2, 8.0 / 315.0, -1.0 / 560.0)
CENTRE = -205.0 / 72.0


def extended(x, sides, width):
    edges = {}
    for axis, dim in sides:
        devices, length = (lax.axis_size(axis), x.shape[dim])
        up = [(i, (i + 1) % devices) for i in range(devices)]
        last = lax.slice_in_dim(x, length - width, length, axis=dim)
        initial = lax.slice_in_dim(x, 0, width, axis=dim)
        edges[dim] = (
            lax.ppermute(last, axis, up),
            lax.ppermute(initial, axis, [(b, a) for a, b in up]),
        )
    done = []
    for _, dim in sides:
        low, high = edges[dim]
        around = [(width, width) if d in done else (0, 0) for d in range(x.ndim)]
        x = jnp.concatenate([jnp.pad(low, around), x, jnp.pad(high, around)], axis=dim)
        done.append(dim)
    return x


def over_axes(x, axes):
    for axis in axes:
        x = lax.pmax(x, axis)
    return x


def primitive(conserved_variables):
    density = conserved_variables[0]
    flow_speed_vector = (
        conserved_variables[1] / density,
        conserved_variables[2] / density,
        conserved_variables[3] / density,
    )
    kinetic = 0.5 * (
        flow_speed_vector[0] * flow_speed_vector[0]
        + flow_speed_vector[1] * flow_speed_vector[1]
        + flow_speed_vector[2] * flow_speed_vector[2]
    )
    thermodynamic_load = (GAMMA - 1.0) * (conserved_variables[4] - density * kinetic)
    return (density, flow_speed_vector, kinetic, thermodynamic_load)


def wave_speed(conserved_variables):
    density, flow_speed_vector, kinetic, thermodynamic_load = primitive(conserved_variables)
    return jnp.sqrt(2.0 * kinetic) + jnp.sqrt(GAMMA * thermodynamic_load / density)


def flux_terms(conserved_variables, primitives, sweep_coordinate):
    density, flow_speed_vector, kinetic, thermodynamic_load = primitives
    transported_scalar = flow_speed_vector[sweep_coordinate]
    interface_transport = [conserved_variables[0] * transported_scalar]
    for variable_index in range(3):
        tendency_increment = conserved_variables[1 + variable_index] * transported_scalar
        if variable_index == sweep_coordinate:
            tendency_increment = tendency_increment + thermodynamic_load
        interface_transport.append(tendency_increment)
    interface_transport.append((conserved_variables[4] + thermodynamic_load) * transported_scalar)
    return interface_transport


def smooth_terms(primitives):
    density, flow_speed_vector, kinetic, thermodynamic_load = primitives
    return [
        flow_speed_vector[0],
        flow_speed_vector[1],
        flow_speed_vector[2],
        kinetic,
        thermodynamic_load / density,
    ]


def quantities(conserved_variables, sweep_coordinate):
    primitives = primitive(conserved_variables)
    return flux_terms(conserved_variables, primitives, sweep_coordinate) + smooth_terms(primitives)


def widened_terms(rim_state, middle_terms, along_axis, sweep_coordinate):
    extent = rim_state.shape[along_axis + 1]
    lower = quantities(lax.slice_in_dim(rim_state, 0, 4, axis=along_axis + 1), sweep_coordinate)
    upper = quantities(
        lax.slice_in_dim(rim_state, extent - 4, extent, axis=along_axis + 1), sweep_coordinate
    )
    return [
        jnp.concatenate([lower[index], middle_terms[index], upper[index]], axis=along_axis)
        for index in range(10)
    ]


def stencil(values, along_axis, extent):

    def shifted(source, offset):
        return lax.slice_in_dim(source, 4 + offset, 4 + offset + extent, axis=along_axis)

    firsts = []
    seconds = []
    for variable_index in range(10):
        source = values[variable_index]
        if variable_index < 5:
            result = FIRST[0] * (shifted(source, 1) - shifted(source, -1))
            for offset in range(1, 4):
                result = result + FIRST[offset] * (
                    shifted(source, offset + 1) - shifted(source, -offset - 1)
                )
            firsts.append(result)
        else:
            result = CENTRE * shifted(source, 0)
            for offset in range(4):
                result = result + SECOND[offset] * (
                    shifted(source, offset + 1) + shifted(source, -offset - 1)
                )
            seconds.append(result)
    return (firsts, seconds)


def wrapped_stencil(values):
    firsts = []
    seconds = []
    for variable_index in range(10):
        source = values[variable_index]
        if variable_index < 5:
            result = FIRST[0] * (jnp.roll(source, -1, 2) - jnp.roll(source, 1, 2))
            for offset in range(1, 4):
                result = result + FIRST[offset] * (
                    jnp.roll(source, -offset - 1, 2) - jnp.roll(source, offset + 1, 2)
                )
            firsts.append(result)
        else:
            result = CENTRE * source
            for offset in range(4):
                result = result + SECOND[offset] * (
                    jnp.roll(source, -offset - 1, 2) + jnp.roll(source, offset + 1, 2)
                )
            seconds.append(result)
    return (firsts, seconds)


def assemble(parts):
    rate = []
    for variable_index in range(5):
        rate.append(
            -(
                parts[0][0][variable_index]
                + parts[1][0][variable_index]
                + parts[2][0][variable_index]
            )
        )
    lap = [
        parts[0][1][variable_index] + parts[1][1][variable_index] + parts[2][1][variable_index]
        for variable_index in range(5)
    ]
    rate[1] = rate[1] + VISCOSITY * lap[0]
    rate[2] = rate[2] + VISCOSITY * lap[1]
    rate[3] = rate[3] + VISCOSITY * lap[2]
    rate[4] = rate[4] + VISCOSITY * lap[3] + CONDUCTION * lap[4]
    return jnp.stack(rate, 0)


def local(start_state, section_state, previous_speed):
    cells_x = section_state.shape[1]
    cells_y = section_state.shape[2]
    time_step = COURANT / previous_speed
    section_primitives = primitive(section_state)
    smooth = smooth_terms(section_primitives)
    x_middle = flux_terms(section_state, section_primitives, 0) + smooth
    y_middle = flux_terms(section_state, section_primitives, 1) + smooth
    z_middle = flux_terms(section_state, section_primitives, 2) + smooth
    padded = extended(start_state, ((GX, 1), (GY, 2)), 4)
    x_start = padded[:, :, 4 : 4 + cells_y]
    y_start = padded[:, 4 : 4 + cells_x]
    x_parts = stencil(widened_terms(x_start, x_middle, 0, 0), 0, cells_x)
    y_parts = stencil(widened_terms(y_start, y_middle, 1, 1), 1, cells_y)
    z_parts = wrapped_stencil(z_middle)
    rate = assemble((x_parts, y_parts, z_parts))
    new_state = 0.75 * start_state + 0.25 * (section_state + time_step * rate)
    newest = over_axes(jnp.max(wave_speed(new_state)), GX_GY)
    return (new_state, newest)


def solution(mesh):
    split = Mesh(mesh.devices.reshape(4, 8, 2, 4, 2), ("gx_0", "gx_1", "gy_0", "gy_1", "gy_2"))
    in_specs = (P(None, GX, GY, None), P(None, GX, GY, None), P())
    out_specs = (P(None, GX, GY, None), P())
    return jax.shard_map(local, mesh=split, in_specs=in_specs, out_specs=out_specs, check_vma=False)
```

profile of v0, /device:TPU:1, one launch (start us, length us, event | category | flops | bytes accessed | tf_op | source)
XLA Modules:
  0.0 137.5 jit_solution(4243412491353572183)
XLA Ops:
  0.6 2.0 %fusion.533 = (f32[5,4,16,256]{3,2,1,0:T(8,128)}, f32[5,4,16,256]{3,2,1,0:T(8,128)}) fusion(f32[5,8,16,256]{3,2,1,0:T(8,128)} %param.3), kind=kLoop, calls=%fused_computation.903 | loop fusion | bytes 1310720 | tf_op jit(solution)/shard_map/slice | solution.py:27
  2.7 11.5 %collective-permute-start = (f32[5,4,16,256]{3,2,1,0:T(8,128)}, f32[5,4,16,256]{3,2,1,0:T(8,128)S(1)}, u32[]{:S(2)}, u32[]{:S(2)}) collective-permute-start(f32[5,4,16,256]{3,2,1,0:T(8,128)} %get-tuple-element.51), channel_id=1, source_target_pairs={{16,0},{32,16},{48,32},{64,48},{80,64},{96,80},{112,96},{128,112},... | collective-permute-start | bytes 983048 | tf_op jit(solution)/shard_map/ppermute | solution.py:30
  14.1 1.9 %collective-permute-start.1 = (f32[5,4,16,256]{3,2,1,0:T(8,128)}, f32[5,4,16,256]{3,2,1,0:T(8,128)S(1)}, u32[]{:S(2)}, u32[]{:S(2)}) collective-permute-start(f32[5,4,16,256]{3,2,1,0:T(8,128)} %get-tuple-element.52), channel_id=1, source_target_pairs={{0,16},{16,32},{32,48},{48,64},{64,80},{80,96},{96,112},{112,128},... | collective-permute-start | bytes 983048 | tf_op jit(solution)/shard_map/ppermute | solution.py:29
  16.1 0.8 fusion.532
  16.9 2.9 %collective-permute-start.2 = (f32[5,8,4,256]{3,2,1,0:T(4,128)}, f32[5,8,4,256]{3,2,1,0:T(4,128)S(1)}, u32[]{:S(2)}, u32[]{:S(2)}) collective-permute-start(f32[5,8,4,256]{3,2,1,0:T(4,128)} %get-tuple-element.49), channel_id=1, source_target_pairs={{1,0},{2,1},{3,2},{4,3},{5,4},{6,5},{7,6},{8,7},{9,8},{10,9},{11,1... | collective-permute-start | bytes 491528 | tf_op jit(solution)/shard_map/ppermute | solution.py:30
  19.7 3.0 %collective-permute-start.3 = (f32[5,8,4,256]{3,2,1,0:T(4,128)}, f32[5,8,4,256]{3,2,1,0:T(4,128)S(1)}, u32[]{:S(2)}, u32[]{:S(2)}) collective-permute-start(f32[5,8,4,256]{3,2,1,0:T(4,128)} %get-tuple-element.50), channel_id=1, source_target_pairs={{0,1},{1,2},{2,3},{3,4},{4,5},{5,6},{6,7},{7,8},{8,9},{9,10},{10,1... | collective-permute-start | bytes 491528 | tf_op jit(solution)/shard_map/ppermute | solution.py:29
  22.9 1.1 fusion.518
  24.0 0.8 fusion.607
  24.7 0.8 fusion.609
  29.9 0.9 fusion.583
  30.8 0.9 fusion.585
  31.6 0.9 fusion.587
  32.5 0.9 fusion.589
  33.4 0.8 fusion.582
  34.2 0.8 fusion.584
  35.0 0.8 fusion.586
  35.7 0.8 fusion.588
  36.5 0.9 fusion.575
  37.4 0.9 fusion.577
  38.3 0.9 fusion.579
  39.2 0.9 fusion.581
  40.1 0.8 fusion.574
  41.6 0.8 fusion.578
  43.2 0.9 fusion.535
  44.1 0.9 fusion.537
  45.0 0.9 fusion.539
  45.9 0.9 fusion.541
  46.8 0.8 fusion.534
  48.3 0.8 fusion.538
  49.1 0.8 fusion.540
  49.8 0.9 fusion.551
  50.7 0.9 fusion.553
  51.6 0.9 fusion.555
  52.5 0.9 fusion.557
  53.4 0.8 fusion.550
  54.2 0.8 fusion.552
  55.7 0.8 fusion.556
  57.2 0.8 fusion.549
  66.0 2.6 %fusion.259 = f32[5,8,16,256]{3,2,1,0:T(8,128)S(1)} fusion(f32[5,8,16,256]{3,2,1,0:T(8,128)S(1)} %fusion.329, f32[8,16,256]{2,1,0:T(8,128)S(1)} %get-tuple-element.6, f32[8,16,256]{2,1,0:T(8,128)S(1)} %copy-done.7, f32[8,16,256]{2,1,0:T(8,128)S(1)} %copy-done.6, f32[4,16,256]{2,1,0:T(8,128)S(1)} %get-tuple-element.31, ...), kind=kLoop, calls=%fused_computation.500 | loop fusion | flops 4096000 | bytes 3092480
  69.4 1.9 %fusion.188 = f32[5,8,16,256]{3,2,1,0:T(8,128)S(1)} fusion(f32[5,8,16,256]{3,2,1,0:T(8,128)S(1)} %fusion.259, f32[8,16,256]{2,1,0:T(8,128)S(1)} %get-tuple-element.7, f32[8,16,256]{2,1,0:T(8,128)S(1)} %copy-done.4, f32[8,16,256]{2,1,0:T(8,128)S(1)} %copy-done.5, f32[4,16,256]{2,1,0:T(8,128)S(1)} %get-tuple-element.29, ...), kind=kLoop, calls=%fused_computation.429 | loop fusion | flops 4096000 | bytes 3612672
  71.3 0.8 copy-done.92
  72.5 3.1 %fusion.117 = f32[5,8,16,256]{3,2,1,0:T(8,128)S(1)} fusion(f32[5,8,16,256]{3,2,1,0:T(8,128)S(1)} %fusion.188, f32[8,16,256]{2,1,0:T(8,128)S(1)} %get-tuple-element.5, f32[8,16,256]{2,1,0:T(8,128)S(1)} %get-tuple-element.39, f32[8,16,256]{2,1,0:T(8,128)S(1)} %copy-done.3, f32[4,16,256]{2,1,0:T(8,128)S(1)} %get-tuple-element.30, ...), kind=kLoop, calls=%fused_computation.358 | loop fusion | flops 4096000 | bytes 3078144
  76.4 3.1 %fusion.10 = f32[5,8,16,256]{3,2,1,0:T(8,128)S(1)} fusion(f32[5,8,16,256]{3,2,1,0:T(8,128)S(1)} %fusion.117, f32[8,16,256]{2,1,0:T(8,128)S(1)} %get-tuple-element.41, f32[8,16,256]{2,1,0:T(8,128)S(1)} %broadcast_multiply_fusion, f32[8,16,256]{2,1,0:T(8,128)S(1)} %get-tuple-element.37, f32[8,16,256]{2,1,0:T(8,128)S(1)} %get-tuple-element.32, ...), kind=kLoop, calls=%fused_computation.251 | loop fusion | flops 6225920 | bytes 5707776 | tf_op jit(solution)/shard_map/stack | solution.py:175
  80.5 7.2 %pmax.35 = f32[]{:T(128)} all-reduce(f32[]{:T(128)} %fusion.487), channel_id=1, replica_groups=mesh['gx_0'=4,'gx_1'=8,'gy_0'=2,'gy_1'=4,'gy_2'=2] {'gx_0'}, use_global_device_ids=true, to_apply=%region_1.2 | all-reduce | flops 1 | bytes 8 | tf_op jit(solution)/shard_map/pmax | solution.py:43
  87.7 17.2 %pmax.36 = f32[]{:T(128)} all-reduce(f32[]{:T(128)} %pmax.35), channel_id=1, replica_groups=mesh['gx_0'=4,'gx_1'=8,'gy_0'=2,'gy_1'=4,'gy_2'=2] {'gx_1'}, use_global_device_ids=true, to_apply=%region_2.3 | all-reduce | flops 1 | bytes 8 | tf_op jit(solution)/shard_map/pmax | solution.py:43
  104.9 9.2 %pmax.37 = f32[]{:T(128)} all-reduce(f32[]{:T(128)} %pmax.36), channel_id=1, replica_groups=mesh['gx_0'=4,'gx_1'=8,'gy_0'=2,'gy_1'=4,'gy_2'=2] {'gy_0'}, use_global_device_ids=true, to_apply=%region_3.4 | all-reduce | flops 1 | bytes 8 | tf_op jit(solution)/shard_map/pmax | solution.py:43
  114.1 14.5 %pmax.38 = f32[]{:T(128)} all-reduce(f32[]{:T(128)} %pmax.37), channel_id=1, replica_groups=mesh['gx_0'=4,'gx_1'=8,'gy_0'=2,'gy_1'=4,'gy_2'=2] {'gy_1'}, use_global_device_ids=true, to_apply=%region_4.5 | all-reduce | flops 1 | bytes 8 | tf_op jit(solution)/shard_map/pmax | solution.py:43
  128.6 8.9 %pmax.39 = f32[]{:T(128)} all-reduce(f32[]{:T(128)} %pmax.38), channel_id=1, replica_groups=mesh['gx_0'=4,'gx_1'=8,'gy_0'=2,'gy_1'=4,'gy_2'=2] {'gy_2'}, use_global_device_ids=true, to_apply=%region_5.6 | all-reduce | flops 1 | bytes 8 | tf_op jit(solution)/shard_map/pmax | solution.py:43
  (237 shorter events, 17.2 us)
Async XLA Ops:
  0.6 15.4 %copy-start.1 = (f32[5,8,16,256]{3,2,1,0:T(8,128)S(1)}, f32[5,8,16,256]{3,2,1,0:T(8,128)}, u32[]{:S(2)}) copy-start(f32[5,8,16,256]{3,2,1,0:T(8,128)} %param.3) | copy-start | bytes 1966084
  2.7 20.1 %copy-start = (f32[5,8,16,256]{3,2,1,0:T(8,128)S(1)}, f32[5,8,16,256]{3,2,1,0:T(8,128)}, u32[]{:S(2)}) copy-start(f32[5,8,16,256]{3,2,1,0:T(8,128)} %param.4) | copy-start | bytes 1966084
  2.7 59.9 %collective-permute-start = (f32[5,4,16,256]{3,2,1,0:T(8,128)}, f32[5,4,16,256]{3,2,1,0:T(8,128)S(1)}, u32[]{:S(2)}, u32[]{:S(2)}) collective-permute-start(f32[5,4,16,256]{3,2,1,0:T(8,128)} %get-tuple-element.51), channel_id=1, source_target_pairs={{16,0},{32,16},{48,32},{64,48},{80,64},{96,80},{112,96},{128,112},... | collective-permute-start | bytes 983048 | tf_op jit(solution)/shard_map/ppermute | solution.py:30
  14.1 48.5 %collective-permute-start.1 = (f32[5,4,16,256]{3,2,1,0:T(8,128)}, f32[5,4,16,256]{3,2,1,0:T(8,128)S(1)}, u32[]{:S(2)}, u32[]{:S(2)}) collective-permute-start(f32[5,4,16,256]{3,2,1,0:T(8,128)} %get-tuple-element.52), channel_id=1, source_target_pairs={{0,16},{16,32},{32,48},{48,64},{64,80},{80,96},{96,112},{112,128},... | collective-permute-start | bytes 983048 | tf_op jit(solution)/shard_map/ppermute | solution.py:29
  16.9 45.5 %collective-permute-start.2 = (f32[5,8,4,256]{3,2,1,0:T(4,128)}, f32[5,8,4,256]{3,2,1,0:T(4,128)S(1)}, u32[]{:S(2)}, u32[]{:S(2)}) collective-permute-start(f32[5,8,4,256]{3,2,1,0:T(4,128)} %get-tuple-element.49), channel_id=1, source_target_pairs={{1,0},{2,1},{3,2},{4,3},{5,4},{6,5},{7,6},{8,7},{9,8},{10,9},{11,1... | collective-permute-start | bytes 491528 | tf_op jit(solution)/shard_map/ppermute | solution.py:30
  19.7 42.7 %collective-permute-start.3 = (f32[5,8,4,256]{3,2,1,0:T(4,128)}, f32[5,8,4,256]{3,2,1,0:T(4,128)S(1)}, u32[]{:S(2)}, u32[]{:S(2)}) collective-permute-start(f32[5,8,4,256]{3,2,1,0:T(4,128)} %get-tuple-element.50), channel_id=1, source_target_pairs={{0,1},{1,2},{2,3},{3,4},{4,5},{5,6},{6,7},{7,8},{8,9},{9,10},{10,1... | collective-permute-start | bytes 491528 | tf_op jit(solution)/shard_map/ppermute | solution.py:29
  65.7 2.8 %copy-start.44 = (f32[8,16,253]{2,1,0:T(8,128)S(1)}, f32[8,16,253]{2,1,0:T(8,128)}, u32[]{:S(2)}) copy-start(f32[8,16,253]{2,1,0:T(8,128)} %get-tuple-element.175) | copy-start | bytes 388612
  65.7 2.8 %copy-start.45 = (f32[8,16,253]{2,1,0:T(8,128)S(1)}, f32[8,16,253]{2,1,0:T(8,128)}, u32[]{:S(2)}) copy-start(f32[8,16,253]{2,1,0:T(8,128)} %get-tuple-element.176) | copy-start | bytes 388612
  65.8 2.8 %copy-start.46 = (f32[8,16,254]{2,1,0:T(8,128)S(1)}, f32[8,16,254]{2,1,0:T(8,128)}, u32[]{:S(2)}) copy-start(f32[8,16,254]{2,1,0:T(8,128)} %get-tuple-element.179) | copy-start | bytes 390148
  72.1 3.4 %copy-start.10 = (f32[8,16,254]{2,1,0:T(8,128)S(1)}, f32[8,16,254]{2,1,0:T(8,128)}, u32[]{:S(2)}) copy-start(f32[8,16,254]{2,1,0:T(8,128)} %get-tuple-element.99) | copy-start | bytes 390148
  72.1 3.4 %copy-start.11 = (f32[8,16,254]{2,1,0:T(8,128)S(1)}, f32[8,16,254]{2,1,0:T(8,128)}, u32[]{:S(2)}) copy-start(f32[8,16,254]{2,1,0:T(8,128)} %get-tuple-element.100) | copy-start | bytes 390148
  72.1 3.4 %copy-start.12 = (f32[8,16,255]{2,1,0:T(8,128)S(1)}, f32[8,16,255]{2,1,0:T(8,128)}, u32[]{:S(2)}) copy-start(f32[8,16,255]{2,1,0:T(8,128)} %get-tuple-element.103) | copy-start | bytes 391684
  72.1 3.4 %copy-start.13 = (f32[8,16,255]{2,1,0:T(8,128)S(1)}, f32[8,16,255]{2,1,0:T(8,128)}, u32[]{:S(2)}) copy-start(f32[8,16,255]{2,1,0:T(8,128)} %get-tuple-element.104) | copy-start | bytes 391684
  72.1 3.4 %copy-start.14 = (f32[8,16,252]{2,1,0:T(8,128)S(1)}, f32[8,16,252]{2,1,0:T(8,128)}, u32[]{:S(2)}) copy-start(f32[8,16,252]{2,1,0:T(8,128)} %get-tuple-element.91) | copy-start | bytes 387076
  72.1 3.4 %copy-start.15 = (f32[8,16,252]{2,1,0:T(8,128)S(1)}, f32[8,16,252]{2,1,0:T(8,128)}, u32[]{:S(2)}) copy-start(f32[8,16,252]{2,1,0:T(8,128)} %get-tuple-element.92) | copy-start | bytes 387076
  72.1 3.4 %copy-start.16 = (f32[8,16,253]{2,1,0:T(8,128)S(1)}, f32[8,16,253]{2,1,0:T(8,128)}, u32[]{:S(2)}) copy-start(f32[8,16,253]{2,1,0:T(8,128)} %get-tuple-element.95) | copy-start | bytes 388612
  72.2 3.4 %copy-start.17 = (f32[8,16,253]{2,1,0:T(8,128)S(1)}, f32[8,16,253]{2,1,0:T(8,128)}, u32[]{:S(2)}) copy-start(f32[8,16,253]{2,1,0:T(8,128)} %get-tuple-element.96) | copy-start | bytes 388612
  72.2 3.4 %copy-start.26 = (f32[8,16,252]{2,1,0:T(8,128)S(1)}, f32[8,16,252]{2,1,0:T(8,128)}, u32[]{:S(2)}) copy-start(f32[8,16,252]{2,1,0:T(8,128)} %get-tuple-element.75) | copy-start | bytes 387076
  72.2 3.4 %copy-start.27 = (f32[8,16,252]{2,1,0:T(8,128)S(1)}, f32[8,16,252]{2,1,0:T(8,128)}, u32[]{:S(2)}) copy-start(f32[8,16,252]{2,1,0:T(8,128)} %get-tuple-element.76) | copy-start | bytes 387076
  72.2 3.4 %copy-start.28 = (f32[8,16,253]{2,1,0:T(8,128)S(1)}, f32[8,16,253]{2,1,0:T(8,128)}, u32[]{:S(2)}) copy-start(f32[8,16,253]{2,1,0:T(8,128)} %get-tuple-element.79) | copy-start | bytes 388612
  72.2 3.4 %copy-start.29 = (f32[8,16,253]{2,1,0:T(8,128)S(1)}, f32[8,16,253]{2,1,0:T(8,128)}, u32[]{:S(2)}) copy-start(f32[8,16,253]{2,1,0:T(8,128)} %get-tuple-element.80) | copy-start | bytes 388612
  72.2 3.4 %copy-start.30 = (f32[8,16,254]{2,1,0:T(8,128)S(1)}, f32[8,16,254]{2,1,0:T(8,128)}, u32[]{:S(2)}) copy-start(f32[8,16,254]{2,1,0:T(8,128)} %get-tuple-element.83) | copy-start | bytes 390148
  72.2 3.4 %copy-start.31 = (f32[8,16,254]{2,1,0:T(8,128)S(1)}, f32[8,16,254]{2,1,0:T(8,128)}, u32[]{:S(2)}) copy-start(f32[8,16,254]{2,1,0:T(8,128)} %get-tuple-element.84) | copy-start | bytes 390148
  72.2 3.4 %copy-start.32 = (f32[8,16,255]{2,1,0:T(8,128)S(1)}, f32[8,16,255]{2,1,0:T(8,128)}, u32[]{:S(2)}) copy-start(f32[8,16,255]{2,1,0:T(8,128)} %get-tuple-element.87) | copy-start | bytes 391684
  72.2 3.4 %copy-start.33 = (f32[8,16,255]{2,1,0:T(8,128)S(1)}, f32[8,16,255]{2,1,0:T(8,128)}, u32[]{:S(2)}) copy-start(f32[8,16,255]{2,1,0:T(8,128)} %get-tuple-element.88) | copy-start | bytes 391684
  72.2 3.4 %copy-start.34 = (f32[8,16,252]{2,1,0:T(8,128)S(1)}, f32[8,16,252]{2,1,0:T(8,128)}, u32[]{:S(2)}) copy-start(f32[8,16,252]{2,1,0:T(8,128)} %get-tuple-element.107) | copy-start | bytes 387076
  72.3 3.4 %copy-start.35 = (f32[8,16,252]{2,1,0:T(8,128)S(1)}, f32[8,16,252]{2,1,0:T(8,128)}, u32[]{:S(2)}) copy-start(f32[8,16,252]{2,1,0:T(8,128)} %get-tuple-element.108) | copy-start | bytes 387076
  72.3 3.4 %copy-start.36 = (f32[8,16,253]{2,1,0:T(8,128)S(1)}, f32[8,16,253]{2,1,0:T(8,128)}, u32[]{:S(2)}) copy-start(f32[8,16,253]{2,1,0:T(8,128)} %get-tuple-element.111) | copy-start | bytes 388612
  72.3 3.4 %copy-start.37 = (f32[8,16,253]{2,1,0:T(8,128)S(1)}, f32[8,16,253]{2,1,0:T(8,128)}, u32[]{:S(2)}) copy-start(f32[8,16,253]{2,1,0:T(8,128)} %get-tuple-element.112) | copy-start | bytes 388612
  72.3 3.4 %copy-start.38 = (f32[8,16,254]{2,1,0:T(8,128)S(1)}, f32[8,16,254]{2,1,0:T(8,128)}, u32[]{:S(2)}) copy-start(f32[8,16,254]{2,1,0:T(8,128)} %get-tuple-element.115) | copy-start | bytes 390148
  72.3 3.4 %copy-start.39 = (f32[8,16,254]{2,1,0:T(8,128)S(1)}, f32[8,16,254]{2,1,0:T(8,128)}, u32[]{:S(2)}) copy-start(f32[8,16,254]{2,1,0:T(8,128)} %get-tuple-element.116) | copy-start | bytes 390148
  72.3 3.4 %copy-start.40 = (f32[8,16,255]{2,1,0:T(8,128)S(1)}, f32[8,16,255]{2,1,0:T(8,128)}, u32[]{:S(2)}) copy-start(f32[8,16,255]{2,1,0:T(8,128)} %get-tuple-element.119) | copy-start | bytes 391684
  72.3 3.4 %copy-start.41 = (f32[8,16,255]{2,1,0:T(8,128)S(1)}, f32[8,16,255]{2,1,0:T(8,128)}, u32[]{:S(2)}) copy-start(f32[8,16,255]{2,1,0:T(8,128)} %get-tuple-element.120) | copy-start | bytes 391684
  72.3 3.4 %copy-start.69 = (f32[8,16,4]{2,1,0:T(8,128)S(1)}, f32[8,16,4]{2,1,0:T(8,128)}, u32[]{:S(2)}) copy-start(f32[8,16,4]{2,1,0:T(8,128)} %get-tuple-element.89) | copy-start | bytes 6148
  72.3 3.4 %copy-start.70 = (f32[8,16,4]{2,1,0:T(8,128)S(1)}, f32[8,16,4]{2,1,0:T(8,128)}, u32[]{:S(2)}) copy-start(f32[8,16,4]{2,1,0:T(8,128)} %get-tuple-element.90) | copy-start | bytes 6148
  72.3 3.4 %copy-start.71 = (f32[8,16,3]{2,1,0:T(8,128)S(1)}, f32[8,16,3]{2,1,0:T(8,128)}, u32[]{:S(2)}) copy-start(f32[8,16,3]{2,1,0:T(8,128)} %get-tuple-element.93) | copy-start | bytes 4612
  72.4 3.4 %copy-start.72 = (f32[8,16,3]{2,1,0:T(8,128)S(1)}, f32[8,16,3]{2,1,0:T(8,128)}, u32[]{:S(2)}) copy-start(f32[8,16,3]{2,1,0:T(8,128)} %get-tuple-element.94) | copy-start | bytes 4612
  72.4 3.4 %copy-start.73 = (f32[8,16,4]{2,1,0:T(8,128)S(1)}, f32[8,16,4]{2,1,0:T(8,128)}, u32[]{:S(2)}) copy-start(f32[8,16,4]{2,1,0:T(8,128)} %get-tuple-element.73) | copy-start | bytes 6148
  72.4 3.4 %copy-start.74 = (f32[8,16,4]{2,1,0:T(8,128)S(1)}, f32[8,16,4]{2,1,0:T(8,128)}, u32[]{:S(2)}) copy-start(f32[8,16,4]{2,1,0:T(8,128)} %get-tuple-element.74) | copy-start | bytes 6148
  72.4 3.4 %copy-start.75 = (f32[8,16,3]{2,1,0:T(8,128)S(1)}, f32[8,16,3]{2,1,0:T(8,128)}, u32[]{:S(2)}) copy-start(f32[8,16,3]{2,1,0:T(8,128)} %get-tuple-element.77) | copy-start | bytes 4612
  72.4 3.4 %copy-start.76 = (f32[8,16,3]{2,1,0:T(8,128)S(1)}, f32[8,16,3]{2,1,0:T(8,128)}, u32[]{:S(2)}) copy-start(f32[8,16,3]{2,1,0:T(8,128)} %get-tuple-element.78) | copy-start | bytes 4612
  72.4 3.4 %copy-start.77 = (f32[8,16,2]{2,1,0:T(8,128)S(1)}, f32[8,16,2]{2,1,0:T(8,128)}, u32[]{:S(2)}) copy-start(f32[8,16,2]{2,1,0:T(8,128)} %get-tuple-element.81) | copy-start | bytes 3076
  72.4 3.4 %copy-start.78 = (f32[8,16,2]{2,1,0:T(8,128)S(1)}, f32[8,16,2]{2,1,0:T(8,128)}, u32[]{:S(2)}) copy-start(f32[8,16,2]{2,1,0:T(8,128)} %get-tuple-element.82) | copy-start | bytes 3076
  72.4 3.4 %copy-start.79 = (f32[8,16,1]{2,1,0:T(8,128)S(1)}, f32[8,16,1]{2,1,0:T(8,128)}, u32[]{:S(2)}) copy-start(f32[8,16,1]{2,1,0:T(8,128)} %get-tuple-element.85) | copy-start | bytes 1540
  72.4 3.4 %copy-start.80 = (f32[8,16,1]{2,1,0:T(8,128)S(1)}, f32[8,16,1]{2,1,0:T(8,128)}, u32[]{:S(2)}) copy-start(f32[8,16,1]{2,1,0:T(8,128)} %get-tuple-element.86) | copy-start | bytes 1540
  72.4 3.4 %copy-start.81 = (f32[8,16,4]{2,1,0:T(8,128)S(1)}, f32[8,16,4]{2,1,0:T(8,128)}, u32[]{:S(2)}) copy-start(f32[8,16,4]{2,1,0:T(8,128)} %get-tuple-element.105) | copy-start | bytes 6148
  72.5 3.4 %copy-start.82 = (f32[8,16,4]{2,1,0:T(8,128)S(1)}, f32[8,16,4]{2,1,0:T(8,128)}, u32[]{:S(2)}) copy-start(f32[8,16,4]{2,1,0:T(8,128)} %get-tuple-element.106) | copy-start | bytes 6148
  79.7 57.8 %copy-start.2 = (f32[5,8,16,256]{3,2,1,0:T(8,128)}, f32[5,8,16,256]{3,2,1,0:T(8,128)S(1)}, u32[]{:S(2)}) copy-start(f32[5,8,16,256]{3,2,1,0:T(8,128)S(1)} %multiply_add_fusion) | copy-start | bytes 1966084
  (58 other events, 104.4 us)
where the time goes:
time: 138 us
  blocking collectives  57 us (41%)
  local copies, waits for them, and re-layouts  44.9 us (33%)
  starting transfers between devices  19.3 us (14%)
  other arithmetic  13.6 us (10%)
  between operations  2.75 us (2%)
    pmax x5, blocking collectives, over_axes(): x = lax.pmax(x, axis)  57 us
    slice x42, local copies, waits for them, and re-layouts, wrapped_stencil(): jnp.roll(source, offset + 1, 2)  32.9 us
    ppermute x2, starting transfers between devices, extended(): lax.ppermute(initial, axis, [(b, a) for a, b in up])  14.3 us
    unnamed x4, other arithmetic  7.97 us
    ppermute x2, starting transfers between devices, extended(): lax.ppermute(last, axis, up)  4.94 us
    slice x6, local copies, waits for them, and re-layouts, wrapped_stencil(): result = FIRST[0] * (jnp.roll(source, -1, 2) - jnp.roll(source, 1, 2))  4.78 us
    unnamed x204, local copies, waits for them, and re-layouts  4.38 us
    another operation x1, other arithmetic, assemble(): return jnp.stack(rate, 0)  3.11 us
  transfers between devices with their start and end apart: 4, of which 0 were waited for; matrix products, arithmetic and copies ran while one was open for 29% of the time, Pallas kernels for 0%

commit v1 on v0

v1 whole, which is shorter than its diff:
```python
import jax
import jax.numpy as jnp
from jax import lax
from jax.experimental import pallas as pl
from jax.experimental.pallas import tpu as pltpu
from jax.sharding import PartitionSpec as P

GAMMA = 1.4
COURANT = 0.3
VISCOSITY = 0.05
CONDUCTION = 0.07
FIRST = (0.8, -0.2, 4.0 / 105.0, -1.0 / 280.0)
SECOND = (1.6, -0.2, 8.0 / 315.0, -1.0 / 560.0)
CENTRE = -205.0 / 72.0
VMEM = pltpu.VMEM
SMEM = pltpu.SMEM


def primitive(q):
    inverse = 1.0 / q[0]
    u, v, w = q[1] * inverse, q[2] * inverse, q[3] * inverse
    kinetic = 0.5 * (u * u + v * v + w * w)
    pressure = (GAMMA - 1.0) * (q[4] - q[0] * kinetic)
    return inverse, (u, v, w), kinetic, pressure


def flux(q, velocity, pressure, d):
    s = velocity[d]
    out = [q[1 + d], q[1] * s, q[2] * s, q[3] * s, (q[4] + pressure) * s]
    out[1 + d] = out[1 + d] + pressure
    return out


def smooth(inverse, velocity, kinetic, pressure):
    heat = VISCOSITY * kinetic + CONDUCTION * (pressure * inverse)
    return [None] + [VISCOSITY * s for s in velocity] + [heat]


def sides(f, g, m):
    first = FIRST[m - 1] * f
    if g is None:
        return -first, first
    second = SECOND[m - 1] * g
    return second - first, second + first


def pack_kernel(start, x_low, x_high, y_low, y_high):
    x_low[...] = start[:, 0:4]
    x_high[...] = start[:, 4:8]
    first = lax.broadcasted_iota(jnp.int32, (8, 256), 0) < 4
    for c in range(5):
        for j in range(4):
            even, odd = start[c, 2 * j, 0:8], start[c, 2 * j + 1, 0:8]
            y_low[c, j] = jnp.where(first, even, pltpu.roll(odd, 4, 0))
            even, odd = start[c, 2 * j, 8:16], start[c, 2 * j + 1, 8:16]
            y_high[c, j] = jnp.where(first, pltpu.roll(odd, 4, 0), even)


def inner_kernel(speed, start, section, out, fluxes, smooths):
    rows = lax.broadcasted_iota(jnp.int32, (16, 256), 0)

    def layer(i, carry):
        q = [section[c, i] for c in range(5)]
        inverse, velocity, kinetic, pressure = primitive(q)
        g = smooth(inverse, velocity, kinetic, pressure)
        fx = flux(q, velocity, pressure, 0)
        fy = flux(q, velocity, pressure, 1)
        fz = flux(q, velocity, pressure, 2)
        for c in range(5):
            fluxes[c, i] = fx[c]
            total = jnp.zeros((16, 256), jnp.float32)
            if c:
                smooths[c - 1, i] = g[c]
                total = (3.0 * CENTRE) * g[c]
            for m in range(1, 5):
                up, down = sides(fz[c], g[c], m)
                total = total + pltpu.roll(up, 256 - m, 1) + pltpu.roll(down, m, 1)
                up, down = sides(fy[c], g[c], m)
                total = total + jnp.where(rows < 16 - m, pltpu.roll(up, 16 - m, 0), 0.0)
                total = total + jnp.where(rows >= m, pltpu.roll(down, m, 0), 0.0)
            out[c, i] = total
        return carry

    lax.fori_loop(0, 8, layer, 0)
    factor = (0.25 * COURANT) / jnp.full((16, 256), speed[0], jnp.float32)
    for c in range(5):
        for i in range(8):
            total = out[c, i]
            for m in range(1, 5):
                for j, sign in ((i + m, -1.0), (i - m, 1.0)):
                    if 0 <= j < 8:
                        total = total + (sign * FIRST[m - 1]) * fluxes[c, j]
                        if c:
                            total = total + SECOND[m - 1] * smooths[c - 1, j]
            out[c, i] = 0.75 * start[c, i] + 0.25 * section[c, i] + factor * total


def rim_kernel(speed, inner, x_low, x_high, y_low, y_high, out, peak, fluxes, smooths, sums):
    rows = lax.broadcasted_iota(jnp.int32, (8, 256), 0)
    first = rows < 4

    def x_rim(i, carry):
        for k, side in enumerate((x_low, x_high)):
            q = [side[c, i] for c in range(5)]
            inverse, velocity, kinetic, pressure = primitive(q)
            g = smooth(inverse, velocity, kinetic, pressure)
            f = flux(q, velocity, pressure, 0)
            for c in range(5):
                fluxes[k, c, i] = f[c]
                if c:
                    smooths[k, c - 1, i] = g[c]
        return carry

    def y_rim(j, carry):
        for odd in range(2):
            q = []
            for c in range(5):
                low, high = y_low[c, j], y_high[c, j]
                q.append(jnp.where(first, low, high) if odd else jnp.where(first, high, low))
            inverse, velocity, kinetic, pressure = primitive(q)
            g = smooth(inverse, velocity, kinetic, pressure)
            f = flux(q, velocity, pressure, 1)
            turn = 4 * odd
            for c in range(5):
                lower = jnp.zeros((8, 256), jnp.float32)
                upper = jnp.zeros((8, 256), jnp.float32)
                for m in range(1, 5):
                    up, down = sides(f[c], g[c], m)
                    lower = lower + jnp.where(rows < m, pltpu.roll(down, (m + turn) % 8, 0), 0.0)
                    upper = upper + jnp.where(rows >= 8 - m, pltpu.roll(up, (8 - m + turn) % 8, 0), 0.0)
                sums[c, 2 * j + odd, 0:8] = lower
                sums[c, 2 * j + odd, 8:16] = upper
        return carry

    lax.fori_loop(0, 4, x_rim, 0)
    lax.fori_loop(0, 4, y_rim, 0)
    factor = (0.25 * COURANT) / jnp.full((16, 256), speed[0], jnp.float32)
    most = jnp.zeros((16, 256), jnp.float32)
    for i in range(8):
        new = []
        for c in range(5):
            total = sums[c, i]
            for m in range(1, 5):
                for k, j, sign in ((0, i - m, 1.0), (1, i + m - 8, -1.0)):
                    j = j + 4 if k == 0 else j
                    if (k == 0 and i - m < 0) or (k == 1 and i + m > 7):
                        total = total + (sign * FIRST[m - 1]) * fluxes[k, c, j]
                        if c:
                            total = total + SECOND[m - 1] * smooths[k, c - 1, j]
            value = inner[c, i] + factor * total
            out[c, i] = value
            new.append(value)
        inverse, velocity, kinetic, pressure = primitive(new)
        most = jnp.maximum(most, jnp.sqrt(2.0 * kinetic) + jnp.sqrt(GAMMA * pressure * inverse))
    peak[...] = jnp.full(peak.shape, jnp.max(most), jnp.float32)


def shape(*sizes):
    return jax.ShapeDtypeStruct(sizes, jnp.float32)


def in_vmem(n):
    return [pl.BlockSpec(memory_space=VMEM)] * n


def call(kernel, outs, n_in, scratch, speed, *arrays):
    specs = in_vmem(n_in)
    if speed is not None:
        specs = [pl.BlockSpec(memory_space=SMEM)] + specs
        arrays = (speed,) + arrays
    return pl.pallas_call(
        kernel,
        out_shape=outs,
        in_specs=specs,
        out_specs=tuple(in_vmem(len(outs))),
        scratch_shapes=scratch,
        compiler_params=pltpu.CompilerParams(vmem_limit_bytes=24 << 20),
    )(*arrays)


def shift(x, axis, by):
    n = lax.axis_size(axis)
    return lax.ppermute(x, axis, [(i, (i + by) % n) for i in range(n)])


def local(start, section, previous_speed):
    speed = previous_speed.reshape(1)
    devices = lax.axis_size(("gx", "gy"))
    x_low, x_high, y_low, y_high = call(
        pack_kernel,
        (shape(5, 4, 16, 256), shape(5, 4, 16, 256), shape(5, 4, 8, 256), shape(5, 4, 8, 256)),
        1,
        [],
        None,
        start,
    )
    from_high_x, from_low_x = shift(x_low, "gx", -1), shift(x_high, "gx", 1)
    from_high_y, from_low_y = shift(y_low, "gy", -1), shift(y_high, "gy", 1)
    (inner,) = call(
        inner_kernel,
        (shape(5, 8, 16, 256),),
        2,
        [VMEM((5, 8, 16, 256), jnp.float32), VMEM((4, 8, 16, 256), jnp.float32)],
        speed,
        start,
        section,
    )
    new, peak = call(
        rim_kernel,
        (shape(5, 8, 16, 256), shape(devices, 128)),
        5,
        [
            VMEM((2, 5, 4, 16, 256), jnp.float32),
            VMEM((2, 4, 4, 16, 256), jnp.float32),
            VMEM((5, 8, 16, 256), jnp.float32),
        ],
        speed,
        inner,
        from_low_x,
        from_high_x,
        from_low_y,
        from_high_y,
    )
    peaks = lax.all_to_all(peak, ("gx", "gy"), 0, 0, tiled=True)
    return new, jnp.max(peaks)


def solution(mesh):
    spec = P(None, "gx", "gy", None)
    return jax.shard_map(
        local, mesh=mesh, in_specs=(spec, spec, P()), out_specs=(spec, P()), check_vma=False
    )
```

time: 138 us -> 68 us (0.49)
  local copies, waits for them, and re-layouts: 44.9 us -> 2.17 us
  blocking collectives: 57 us -> 37.8 us
  other arithmetic: 13.6 us -> 1.14 us
  Pallas kernels: 0 us -> 4.58 us
    pmax x5 -> x0, blocking collectives: 57 us -> none  [over_axes(): x = lax.pmax(x, axis)]
    slice x50 -> x0, local copies, waits for them, and re-layouts: 40.5 us -> none  [the longest x42 32.9 us: wrapped_stencil(): jnp.roll(source, offset + 1, 2)]
    all_to_all x0 -> x1, blocking collectives: none -> 37.8 us  [local(): peaks = lax.all_to_all(peak, ('gx', 'gy'), 0, 0, tiled=True)]
    unnamed x4 -> x0, other arithmetic: 7.97 us -> none
    pallas_call x0 -> x3, Pallas kernels: none -> 4.58 us  [call(): pl.pallas_call(kernel, out_shape=outs, in_specs=specs, out_specs=tuple(in...]
    another operation x1 -> x0, other arithmetic: 3.11 us -> none  [assemble(): return jnp.stack(rate, 0)]
    unnamed x204 -> x6, local copies, waits for them, and re-layouts: 4.38 us -> 2.17 us
    mul x7 -> x0, other arithmetic: 1.41 us -> none  [the longest x6 1.4 us: flux_terms(): (conserved_variables[4] + thermodynamic_load) * transported_scalar]
  transfers between devices with their start and end apart: 4 -> 4, of which waited for: 0 -> 0; matrix products, arithmetic and copies ran while one was open for 29% -> 0% of each run, Pallas kernels for 0% -> 4%
where the time goes in v1:
time: 68 us; the launch traced here: 67.7 us
  blocking collectives  37.8 us (56%)
  starting transfers between devices  20.6 us (30%)
  Pallas kernels  4.58 us (7%)
  local copies, waits for them, and re-layouts  2.17 us (3%)
  between operations  1.38 us (2%)
  other arithmetic  1.14 us (2%)
    all_to_all x1, blocking collectives, local(): peaks = lax.all_to_all(peak, ('gx', 'gy'), 0, 0, tiled=True)  37.8 us
    ppermute x4, starting transfers between devices, shift(): return lax.ppermute(x, axis, [(i, (i + by) % n) for i in range(n)])  20.6 us
    pallas_call x3, Pallas kernels, call(): pl.pallas_call(kernel, out_shape=outs, in_specs=specs, out_specs=tuple(in...  4.58 us
    unnamed x6, local copies, waits for them, and re-layouts  2.17 us
  transfers between devices with their start and end apart: 4, of which 0 were waited for; matrix products, arithmetic and copies ran while one was open for 0% of the time, Pallas kernels for 4%

profile of v1, /device:TPU:1, one launch (start us, length us, event | category | flops | bytes accessed | tf_op | source)
XLA Modules:
  0.0 67.7 jit_solution(2823154316698817510)
XLA Ops:
  0.6 0.0 copy-start
  0.6 1.1 %copy-done = f32[5,8,16,256]{3,2,1,0:T(8,128)S(1)} copy-done((f32[5,8,16,256]{3,2,1,0:T(8,128)S(1)}, f32[5,8,16,256]{3,2,1,0:T(8,128)}, u32[]{:S(2)}) %copy-start) | copy-done | bytes 655384
  1.7 0.0 copy-start.1
  1.7 0.1 shard_map.51
  1.8 4.2 %collective-permute-start = (f32[5,4,16,256]{3,2,1,0:T(8,128)S(1)}, f32[5,4,16,256]{3,2,1,0:T(8,128)S(1)}, u32[]{:S(2)}, u32[]{:S(2)}) collective-permute-start(f32[5,4,16,256]{3,2,1,0:T(8,128)S(1)} %get-tuple-element.8), channel_id=1, source_target_pairs={{0,16},{16,32},{32,48},{48,64},{64,80},{80,96},{96,112},{112,128},... | collective-permute-start | bytes 983048 | tf_op jit(solution)/shard_map/ppermute | solution.py:183
  6.0 9.2 %collective-permute-start.1 = (f32[5,4,16,256]{3,2,1,0:T(8,128)S(1)}, f32[5,4,16,256]{3,2,1,0:T(8,128)S(1)}, u32[]{:S(2)}, u32[]{:S(2)}) collective-permute-start(f32[5,4,16,256]{3,2,1,0:T(8,128)S(1)} %get-tuple-element.9), channel_id=1, source_target_pairs={{0,496},{16,0},{32,16},{48,32},{64,48},{80,64},{96,80},{112,96},{1... | collective-permute-start | bytes 983048 | tf_op jit(solution)/shard_map/ppermute | solution.py:183
  15.2 4.0 %collective-permute-start.2 = (f32[5,4,8,256]{3,2,1,0:T(8,128)S(1)}, f32[5,4,8,256]{3,2,1,0:T(8,128)S(1)}, u32[]{:S(2)}, u32[]{:S(2)}) collective-permute-start(f32[5,4,8,256]{3,2,1,0:T(8,128)S(1)} %get-tuple-element.10), channel_id=1, source_target_pairs={{0,1},{1,2},{2,3},{3,4},{4,5},{5,6},{6,7},{7,8},{8,9},{9,10},{10,1... | collective-permute-start | bytes 491528 | tf_op jit(solution)/shard_map/ppermute | solution.py:183
  19.2 3.2 %collective-permute-start.3 = (f32[5,4,8,256]{3,2,1,0:T(8,128)S(1)}, f32[5,4,8,256]{3,2,1,0:T(8,128)S(1)}, u32[]{:S(2)}, u32[]{:S(2)}) collective-permute-start(f32[5,4,8,256]{3,2,1,0:T(8,128)S(1)} %get-tuple-element.11), channel_id=1, source_target_pairs={{0,15},{1,0},{2,1},{3,2},{4,3},{5,4},{6,5},{7,6},{8,7},{9,8},{10,9... | collective-permute-start | bytes 491528 | tf_op jit(solution)/shard_map/ppermute | solution.py:183
  23.1 0.0 copy-done.1
  23.1 0.0 copy-start.2
  23.1 1.1 %copy-done.2 = f32[5,8,16,256]{3,2,1,0:T(8,128)S(1)} copy-done((f32[5,8,16,256]{3,2,1,0:T(8,128)S(1)}, f32[5,8,16,256]{3,2,1,0:T(8,128)}, u32[]{:S(2)}) %copy-start.2) | copy-done | bytes 655384
  24.2 2.7 %shard_map.50.inner = f32[5,8,16,256]{3,2,1,0:T(8,128)S(1)} custom-call(f32[1]{0:T(128)} %bitcast.4.speed, f32[5,8,16,256]{3,2,1,0:T(8,128)S(1)} %copy-done.1, f32[5,8,16,256]{3,2,1,0:T(8,128)S(1)} %copy-done.2), custom_call_target="tpu_custom_call" | custom-call | tf_op jit(solution)/shard_map/pallas_call | solution.py:171
  26.9 0.0 collective-permute-done.2.y_low
  26.9 0.0 collective-permute-done.3.y_high
  26.9 0.0 collective-permute-done.x_low
  26.9 0.0 collective-permute-done.1.x_high
  26.9 1.8 %shard_map.52 = (f32[5,8,16,256]{3,2,1,0:T(8,128)}, f32[512,128]{1,0:T(8,128)S(1)}) custom-call(f32[1]{0:T(128)} %bitcast.5.speed, f32[5,8,16,256]{3,2,1,0:T(8,128)S(1)} %shard_map.50.inner, f32[5,4,16,256]{3,2,1,0:T(8,128)S(1)} %collective-permute-done.x_low, f32[5,4,16,256]{3,2,1,0:T(8,128)S(1)} %collective-permute-done.1.x_high, ...), custom_call_target="tpu_custom_call" | custom-call | tf_op jit(solution)/shard_map/pallas_call | solution.py:171
  28.7 37.8 %all_to_all.9 = f32[512,1,128]{2,1,0:T(1,128)S(1)} all-to-all(f32[512,1,128]{2,1,0:T(1,128)S(1)} %bitcast.6), channel_id=1, replica_groups=mesh['gx'=32,'gy'=16] {'gx','gy'}, dimensions={0} | all-to-all | bytes 524288 | tf_op jit(solution)/shard_map/all_to_all | solution.py:224
  66.5 1.1 %reduce_max.9 = f32[]{:T(128)} reduce(f32[512,1,128]{2,1,0:T(1,128)S(1)} %all_to_all.9, f32[]{:T(128)} %constant.0.clone.1), dimensions={0,1,2}, to_apply=%region_0.0 | reduce | flops 65535 | bytes 262152 | tf_op jit(solution)/shard_map/reduce_max | solution.py:225
Async XLA Ops:
  0.6 1.1 %copy-start = (f32[5,8,16,256]{3,2,1,0:T(8,128)S(1)}, f32[5,8,16,256]{3,2,1,0:T(8,128)}, u32[]{:S(2)}) copy-start(f32[5,8,16,256]{3,2,1,0:T(8,128)} %start.3) | copy-start | bytes 1966084
  1.7 21.3 %copy-start.1 = (f32[5,8,16,256]{3,2,1,0:T(8,128)S(1)}, f32[5,8,16,256]{3,2,1,0:T(8,128)}, u32[]{:S(2)}) copy-start(f32[5,8,16,256]{3,2,1,0:T(8,128)} %start.3) | copy-start | bytes 1966084
  1.8 25.1 %collective-permute-start = (f32[5,4,16,256]{3,2,1,0:T(8,128)S(1)}, f32[5,4,16,256]{3,2,1,0:T(8,128)S(1)}, u32[]{:S(2)}, u32[]{:S(2)}) collective-permute-start(f32[5,4,16,256]{3,2,1,0:T(8,128)S(1)} %get-tuple-element.8), channel_id=1, source_target_pairs={{0,16},{16,32},{32,48},{48,64},{64,80},{80,96},{96,112},{112,128},... | collective-permute-start | bytes 983048 | tf_op jit(solution)/shard_map/ppermute | solution.py:183
  6.0 20.9 %collective-permute-start.1 = (f32[5,4,16,256]{3,2,1,0:T(8,128)S(1)}, f32[5,4,16,256]{3,2,1,0:T(8,128)S(1)}, u32[]{:S(2)}, u32[]{:S(2)}) collective-permute-start(f32[5,4,16,256]{3,2,1,0:T(8,128)S(1)} %get-tuple-element.9), channel_id=1, source_target_pairs={{0,496},{16,0},{32,16},{48,32},{64,48},{80,64},{96,80},{112,96},{1... | collective-permute-start | bytes 983048 | tf_op jit(solution)/shard_map/ppermute | solution.py:183
  15.2 11.7 %collective-permute-start.2 = (f32[5,4,8,256]{3,2,1,0:T(8,128)S(1)}, f32[5,4,8,256]{3,2,1,0:T(8,128)S(1)}, u32[]{:S(2)}, u32[]{:S(2)}) collective-permute-start(f32[5,4,8,256]{3,2,1,0:T(8,128)S(1)} %get-tuple-element.10), channel_id=1, source_target_pairs={{0,1},{1,2},{2,3},{3,4},{4,5},{5,6},{6,7},{7,8},{8,9},{9,10},{10,1... | collective-permute-start | bytes 491528 | tf_op jit(solution)/shard_map/ppermute | solution.py:183
  19.2 7.7 %collective-permute-start.3 = (f32[5,4,8,256]{3,2,1,0:T(8,128)S(1)}, f32[5,4,8,256]{3,2,1,0:T(8,128)S(1)}, u32[]{:S(2)}, u32[]{:S(2)}) collective-permute-start(f32[5,4,8,256]{3,2,1,0:T(8,128)S(1)} %get-tuple-element.11), channel_id=1, source_target_pairs={{0,15},{1,0},{2,1},{3,2},{4,3},{5,4},{6,5},{7,6},{8,7},{9,8},{10,9... | collective-permute-start | bytes 491528 | tf_op jit(solution)/shard_map/ppermute | solution.py:183
  23.1 1.1 %copy-start.2 = (f32[5,8,16,256]{3,2,1,0:T(8,128)S(1)}, f32[5,8,16,256]{3,2,1,0:T(8,128)}, u32[]{:S(2)}) copy-start(f32[5,8,16,256]{3,2,1,0:T(8,128)} %section.1) | copy-start | bytes 1966084

commit v2 on v1

--- a/solution.py
+++ b/solution.py
@@ -44,16 +44,24 @@
     return second - first, second + first
 
 
-def pack_kernel(start, x_low, x_high, y_low, y_high):
-    x_low[...] = start[:, 0:4]
-    x_high[...] = start[:, 4:8]
+def odd(axis):
+    return lax.rem(lax.axis_index(axis), 2)
+
+
+def pack_kernel(start, x_even, x_odd, y_even, y_odd):
+    side = odd("gx")
+    x_even[...] = start[:, pl.ds(4 - 4 * side, 4)]
+    x_odd[...] = start[:, pl.ds(4 * side, 4)]
     first = lax.broadcasted_iota(jnp.int32, (8, 256), 0) < 4
+    upper = odd("gy") == 0
     for c in range(5):
         for j in range(4):
-            even, odd = start[c, 2 * j, 0:8], start[c, 2 * j + 1, 0:8]
-            y_low[c, j] = jnp.where(first, even, pltpu.roll(odd, 4, 0))
-            even, odd = start[c, 2 * j, 8:16], start[c, 2 * j + 1, 8:16]
-            y_high[c, j] = jnp.where(first, pltpu.roll(odd, 4, 0), even)
+            a, b = start[c, 2 * j, 0:8], start[c, 2 * j + 1, 0:8]
+            low = jnp.where(first, a, pltpu.roll(b, 4, 0))
+            a, b = start[c, 2 * j, 8:16], start[c, 2 * j + 1, 8:16]
+            high = jnp.where(first, pltpu.roll(b, 4, 0), a)
+            y_even[c, j] = jnp.where(upper, high, low)
+            y_odd[c, j] = jnp.where(upper, low, high)
 
 
 def inner_kernel(speed, start, section, out, fluxes, smooths):
@@ -95,12 +103,13 @@
             out[c, i] = 0.75 * start[c, i] + 0.25 * section[c, i] + factor * total
 
 
-def rim_kernel(speed, inner, x_low, x_high, y_low, y_high, out, peak, fluxes, smooths, sums):
+def rim_kernel(speed, inner, x_even, x_odd, y_even, y_odd, out, peak, fluxes, smooths, sums):
     rows = lax.broadcasted_iota(jnp.int32, (8, 256), 0)
-    first = rows < 4
+    even_first = (rows // 4) == odd("gy")
+    below = odd("gx")
 
     def x_rim(i, carry):
-        for k, side in enumerate((x_low, x_high)):
+        for k, side in ((1 - below, x_even), (below, x_odd)):
             q = [side[c, i] for c in range(5)]
             inverse, velocity, kinetic, pressure = primitive(q)
             g = smooth(inverse, velocity, kinetic, pressure)
@@ -112,15 +121,15 @@
         return carry
 
     def y_rim(j, carry):
-        for odd in range(2):
+        for second in range(2):
             q = []
             for c in range(5):
-                low, high = y_low[c, j], y_high[c, j]
-                q.append(jnp.where(first, low, high) if odd else jnp.where(first, high, low))
+                a, b = (y_odd, y_even) if second else (y_even, y_odd)
+                q.append(jnp.where(even_first, a[c, j], b[c, j]))
             inverse, velocity, kinetic, pressure = primitive(q)
             g = smooth(inverse, velocity, kinetic, pressure)
             f = flux(q, velocity, pressure, 1)
-            turn = 4 * odd
+            turn = 4 * second
             for c in range(5):
                 lower = jnp.zeros((8, 256), jnp.float32)
                 upper = jnp.zeros((8, 256), jnp.float32)
@@ -128,8 +137,8 @@
                     up, down = sides(f[c], g[c], m)
                     lower = lower + jnp.where(rows < m, pltpu.roll(down, (m + turn) % 8, 0), 0.0)
                     upper = upper + jnp.where(rows >= 8 - m, pltpu.roll(up, (8 - m + turn) % 8, 0), 0.0)
-                sums[c, 2 * j + odd, 0:8] = lower
-                sums[c, 2 * j + odd, 8:16] = upper
+                sums[c, 2 * j + second, 0:8] = lower
+                sums[c, 2 * j + second, 8:16] = upper
         return carry
 
     lax.fori_loop(0, 4, x_rim, 0)
@@ -178,15 +187,16 @@
     )(*arrays)
 
 
-def shift(x, axis, by):
+def swap(x, axis, offset):
     n = lax.axis_size(axis)
-    return lax.ppermute(x, axis, [(i, (i + by) % n) for i in range(n)])
+    pairs = [((i + offset) % n, (i + 1 + offset) % n) for i in range(0, n, 2)]
+    return lax.ppermute(x, axis, pairs + [(b, a) for a, b in pairs])
 
 
 def local(start, section, previous_speed):
     speed = previous_speed.reshape(1)
     devices = lax.axis_size(("gx", "gy"))
-    x_low, x_high, y_low, y_high = call(
+    x_even, x_odd, y_even, y_odd = call(
         pack_kernel,
         (shape(5, 4, 16, 256), shape(5, 4, 16, 256), shape(5, 4, 8, 256), shape(5, 4, 8, 256)),
         1,
@@ -194,8 +204,12 @@
         None,
         start,
     )
-    from_high_x, from_low_x = shift(x_low, "gx", -1), shift(x_high, "gx", 1)
-    from_high_y, from_low_y = shift(y_low, "gy", -1), shift(y_high, "gy", 1)
+    received = (
+        swap(x_even, "gx", 0),
+        swap(x_odd, "gx", 1),
+        swap(y_even, "gy", 0),
+        swap(y_odd, "gy", 1),
+    )
     (inner,) = call(
         inner_kernel,
         (shape(5, 8, 16, 256),),
@@ -216,10 +230,7 @@
         ],
         speed,
         inner,
-        from_low_x,
-        from_high_x,
-        from_low_y,
-        from_high_y,
+        *received,
     )
     peaks = lax.all_to_all(peak, ("gx", "gy"), 0, 0, tiled=True)
     return new, jnp.max(peaks)

time: 68 us -> 65 us (0.956)
  blocking collectives: 37.8 us -> 34.7 us
    all_to_all x1, blocking collectives: 37.8 us -> 34.7 us  [local(): peaks = lax.all_to_all(peak, ('gx', 'gy'), 0, 0, tiled=True)]
where the time goes in v2:
time: 65 us; the launch traced here: 64.7 us
  blocking collectives  34.7 us (53%)
  starting transfers between devices  20.6 us (32%)
  Pallas kernels  4.62 us (7%)
  local copies, waits for them, and re-layouts  2.17 us (3%)
  between operations  1.38 us (2%)
  other arithmetic  1.14 us (2%)
    all_to_all x1, blocking collectives, local(): peaks = lax.all_to_all(peak, ('gx', 'gy'), 0, 0, tiled=True)  34.7 us
    ppermute x4, starting transfers between devices, swap(): return lax.ppermute(x, axis, pairs + [(b, a) for a, b in pairs])  20.6 us
    pallas_call x3, Pallas kernels, call(): pl.pallas_call(kernel, out_shape=outs, in_specs=specs, out_specs=tuple(in...  4.62 us
    unnamed x6, local copies, waits for them, and re-layouts  2.17 us
  transfers between devices with their start and end apart: 4, of which 0 were waited for; matrix products, arithmetic and copies ran while one was open for 0% of the time, Pallas kernels for 4%

profile of v2, /device:TPU:1, one launch (start us, length us, event | category | flops | bytes accessed | tf_op | source)
XLA Modules:
  0.0 64.7 jit_solution(18044796314258565731)
XLA Ops:
  0.6 0.0 copy-start
  0.6 1.1 %copy-done = f32[5,8,16,256]{3,2,1,0:T(8,128)S(1)} copy-done((f32[5,8,16,256]{3,2,1,0:T(8,128)S(1)}, f32[5,8,16,256]{3,2,1,0:T(8,128)}, u32[]{:S(2)}) %copy-start) | copy-done | bytes 655384
  1.7 0.0 copy-start.1
  1.7 0.1 shard_map.51
  1.8 4.2 %collective-permute-start = (f32[5,4,16,256]{3,2,1,0:T(8,128)S(1)}, f32[5,4,16,256]{3,2,1,0:T(8,128)S(1)}, u32[]{:S(2)}, u32[]{:S(2)}) collective-permute-start(f32[5,4,16,256]{3,2,1,0:T(8,128)S(1)} %get-tuple-element.8), channel_id=1, source_target_pairs={{0,16},{32,48},{64,80},{96,112},{128,144},{160,176},{192,208},{224... | collective-permute-start | bytes 983048 | tf_op jit(solution)/shard_map/ppermute | solution.py:193
  6.0 10.3 %collective-permute-start.1 = (f32[5,4,16,256]{3,2,1,0:T(8,128)S(1)}, f32[5,4,16,256]{3,2,1,0:T(8,128)S(1)}, u32[]{:S(2)}, u32[]{:S(2)}) collective-permute-start(f32[5,4,16,256]{3,2,1,0:T(8,128)S(1)} %get-tuple-element.9), channel_id=1, source_target_pairs={{16,32},{48,64},{80,96},{112,128},{144,160},{176,192},{208,224},{2... | collective-permute-start | bytes 983048 | tf_op jit(solution)/shard_map/ppermute | solution.py:193
  16.3 3.1 %collective-permute-start.2 = (f32[5,4,8,256]{3,2,1,0:T(8,128)S(1)}, f32[5,4,8,256]{3,2,1,0:T(8,128)S(1)}, u32[]{:S(2)}, u32[]{:S(2)}) collective-permute-start(f32[5,4,8,256]{3,2,1,0:T(8,128)S(1)} %get-tuple-element.10), channel_id=1, source_target_pairs={{0,1},{2,3},{4,5},{6,7},{8,9},{10,11},{12,13},{14,15},{1,0},{3,2},... | collective-permute-start | bytes 491528 | tf_op jit(solution)/shard_map/ppermute | solution.py:193
  19.4 3.0 %collective-permute-start.3 = (f32[5,4,8,256]{3,2,1,0:T(8,128)S(1)}, f32[5,4,8,256]{3,2,1,0:T(8,128)S(1)}, u32[]{:S(2)}, u32[]{:S(2)}) collective-permute-start(f32[5,4,8,256]{3,2,1,0:T(8,128)S(1)} %get-tuple-element.11), channel_id=1, source_target_pairs={{1,2},{3,4},{5,6},{7,8},{9,10},{11,12},{13,14},{15,0},{2,1},{4,3},... | collective-permute-start | bytes 491528 | tf_op jit(solution)/shard_map/ppermute | solution.py:193
  23.1 0.0 copy-done.1
  23.1 0.0 copy-start.2
  23.1 1.1 %copy-done.2 = f32[5,8,16,256]{3,2,1,0:T(8,128)S(1)} copy-done((f32[5,8,16,256]{3,2,1,0:T(8,128)S(1)}, f32[5,8,16,256]{3,2,1,0:T(8,128)}, u32[]{:S(2)}) %copy-start.2) | copy-done | bytes 655384
  24.2 2.7 %shard_map.50.inner = f32[5,8,16,256]{3,2,1,0:T(8,128)S(1)} custom-call(f32[1]{0:T(128)} %bitcast.4.speed, f32[5,8,16,256]{3,2,1,0:T(8,128)S(1)} %copy-done.1, f32[5,8,16,256]{3,2,1,0:T(8,128)S(1)} %copy-done.2), custom_call_target="tpu_custom_call" | custom-call | tf_op jit(solution)/shard_map/pallas_call | solution.py:180
  26.9 0.0 collective-permute-done.2.y_even
  26.9 0.0 collective-permute-done.3.y_odd
  26.9 0.0 collective-permute-done.x_even
  26.9 0.0 collective-permute-done.1.x_odd
  26.9 1.8 %shard_map.52 = (f32[5,8,16,256]{3,2,1,0:T(8,128)}, f32[512,128]{1,0:T(8,128)S(1)}) custom-call(f32[1]{0:T(128)} %bitcast.5.speed, f32[5,8,16,256]{3,2,1,0:T(8,128)S(1)} %shard_map.50.inner, f32[5,4,16,256]{3,2,1,0:T(8,128)S(1)} %collective-permute-done.x_even, f32[5,4,16,256]{3,2,1,0:T(8,128)S(1)} %collective-permute-done.1.x_odd, ...), custom_call_target="tpu_custom_call" | custom-call | tf_op jit(solution)/shard_map/pallas_call | solution.py:180
  28.8 34.7 %all_to_all.9 = f32[512,1,128]{2,1,0:T(1,128)S(1)} all-to-all(f32[512,1,128]{2,1,0:T(1,128)S(1)} %bitcast.6), channel_id=1, replica_groups=mesh['gx'=32,'gy'=16] {'gx','gy'}, dimensions={0} | all-to-all | bytes 524288 | tf_op jit(solution)/shard_map/all_to_all | solution.py:235
  63.5 1.1 %reduce_max.9 = f32[]{:T(128)} reduce(f32[512,1,128]{2,1,0:T(1,128)S(1)} %all_to_all.9, f32[]{:T(128)} %constant.0.clone.1), dimensions={0,1,2}, to_apply=%region_0.0 | reduce | flops 65535 | bytes 262152 | tf_op jit(solution)/shard_map/reduce_max | solution.py:236
Async XLA Ops:
  0.6 1.1 %copy-start = (f32[5,8,16,256]{3,2,1,0:T(8,128)S(1)}, f32[5,8,16,256]{3,2,1,0:T(8,128)}, u32[]{:S(2)}) copy-start(f32[5,8,16,256]{3,2,1,0:T(8,128)} %start.3) | copy-start | bytes 1966084
  1.7 21.4 %copy-start.1 = (f32[5,8,16,256]{3,2,1,0:T(8,128)S(1)}, f32[5,8,16,256]{3,2,1,0:T(8,128)}, u32[]{:S(2)}) copy-start(f32[5,8,16,256]{3,2,1,0:T(8,128)} %start.3) | copy-start | bytes 1966084
  1.8 25.1 %collective-permute-start = (f32[5,4,16,256]{3,2,1,0:T(8,128)S(1)}, f32[5,4,16,256]{3,2,1,0:T(8,128)S(1)}, u32[]{:S(2)}, u32[]{:S(2)}) collective-permute-start(f32[5,4,16,256]{3,2,1,0:T(8,128)S(1)} %get-tuple-element.8), channel_id=1, source_target_pairs={{0,16},{32,48},{64,80},{96,112},{128,144},{160,176},{192,208},{224... | collective-permute-start | bytes 983048 | tf_op jit(solution)/shard_map/ppermute | solution.py:193
  6.0 21.0 %collective-permute-start.1 = (f32[5,4,16,256]{3,2,1,0:T(8,128)S(1)}, f32[5,4,16,256]{3,2,1,0:T(8,128)S(1)}, u32[]{:S(2)}, u32[]{:S(2)}) collective-permute-start(f32[5,4,16,256]{3,2,1,0:T(8,128)S(1)} %get-tuple-element.9), channel_id=1, source_target_pairs={{16,32},{48,64},{80,96},{112,128},{144,160},{176,192},{208,224},{2... | collective-permute-start | bytes 983048 | tf_op jit(solution)/shard_map/ppermute | solution.py:193
  16.3 10.6 %collective-permute-start.2 = (f32[5,4,8,256]{3,2,1,0:T(8,128)S(1)}, f32[5,4,8,256]{3,2,1,0:T(8,128)S(1)}, u32[]{:S(2)}, u32[]{:S(2)}) collective-permute-start(f32[5,4,8,256]{3,2,1,0:T(8,128)S(1)} %get-tuple-element.10), channel_id=1, source_target_pairs={{0,1},{2,3},{4,5},{6,7},{8,9},{10,11},{12,13},{14,15},{1,0},{3,2},... | collective-permute-start | bytes 491528 | tf_op jit(solution)/shard_map/ppermute | solution.py:193
  19.4 7.5 %collective-permute-start.3 = (f32[5,4,8,256]{3,2,1,0:T(8,128)S(1)}, f32[5,4,8,256]{3,2,1,0:T(8,128)S(1)}, u32[]{:S(2)}, u32[]{:S(2)}) collective-permute-start(f32[5,4,8,256]{3,2,1,0:T(8,128)S(1)} %get-tuple-element.11), channel_id=1, source_target_pairs={{1,2},{3,4},{5,6},{7,8},{9,10},{11,12},{13,14},{15,0},{2,1},{4,3},... | collective-permute-start | bytes 491528 | tf_op jit(solution)/shard_map/ppermute | solution.py:193
  23.1 1.1 %copy-start.2 = (f32[5,8,16,256]{3,2,1,0:T(8,128)S(1)}, f32[5,8,16,256]{3,2,1,0:T(8,128)}, u32[]{:S(2)}) copy-start(f32[5,8,16,256]{3,2,1,0:T(8,128)} %section.1) | copy-start | bytes 1966084

commit v3 on v2

--- a/solution.py
+++ b/solution.py
@@ -103,7 +103,7 @@
             out[c, i] = 0.75 * start[c, i] + 0.25 * section[c, i] + factor * total
 
 
-def rim_kernel(speed, inner, x_even, x_odd, y_even, y_odd, out, peak, fluxes, smooths, sums):
+def rim_kernel(speed, inner, y_odd, x_odd, x_even, y_even, out, peak, fluxes, smooths, sums):
     rows = lax.broadcasted_iota(jnp.int32, (8, 256), 0)
     even_first = (rows // 4) == odd("gy")
     below = odd("gx")
@@ -205,10 +205,10 @@
         start,
     )
     received = (
+        swap(y_odd, "gy", 1),
+        swap(x_odd, "gx", 1),
         swap(x_even, "gx", 0),
-        swap(x_odd, "gx", 1),
         swap(y_even, "gy", 0),
-        swap(y_odd, "gy", 1),
     )
     (inner,) = call(
         inner_kernel,

time: 65 us -> 62 us (0.954)
  blocking collectives: 34.7 us -> 26.5 us
  starting transfers between devices: 20.6 us -> 25.8 us
    all_to_all x1, blocking collectives: 34.7 us -> 26.5 us  [local(): peaks = lax.all_to_all(peak, ('gx', 'gy'), 0, 0, tiled=True)]
    ppermute x4, starting transfers between devices: 20.6 us -> 25.8 us  [swap(): return lax.ppermute(x, axis, pairs + [(b, a) for a, b in pairs])]
where the time goes in v3:
time: 62 us; the launch traced here: 61.6 us
  blocking collectives  26.5 us (43%)
  starting transfers between devices  25.8 us (42%)
  Pallas kernels  4.62 us (7%)
  local copies, waits for them, and re-layouts  2.17 us (4%)
  between operations  1.38 us (2%)
  other arithmetic  1.14 us (2%)
    all_to_all x1, blocking collectives, local(): peaks = lax.all_to_all(peak, ('gx', 'gy'), 0, 0, tiled=True)  26.5 us
    ppermute x4, starting transfers between devices, swap(): return lax.ppermute(x, axis, pairs + [(b, a) for a, b in pairs])  25.8 us
    pallas_call x3, Pallas kernels, call(): pl.pallas_call(kernel, out_shape=outs, in_specs=specs, out_specs=tuple(in...  4.62 us
    unnamed x6, local copies, waits for them, and re-layouts  2.17 us
  transfers between devices with their start and end apart: 4, of which 0 were waited for; matrix products, arithmetic and copies ran while one was open for 0% of the time, Pallas kernels for 4%

profile of v3, /device:TPU:1, one launch (start us, length us, event | category | flops | bytes accessed | tf_op | source)
XLA Modules:
  0.0 61.6 jit_solution(2197304264921189269)
XLA Ops:
  0.6 0.0 copy-start
  0.6 1.1 %copy-done = f32[5,8,16,256]{3,2,1,0:T(8,128)S(1)} copy-done((f32[5,8,16,256]{3,2,1,0:T(8,128)S(1)}, f32[5,8,16,256]{3,2,1,0:T(8,128)}, u32[]{:S(2)}) %copy-start) | copy-done | bytes 655384
  1.7 0.0 copy-start.1
  1.7 0.1 shard_map.51
  1.8 11.5 %collective-permute-start.1 = (f32[5,4,16,256]{3,2,1,0:T(8,128)S(1)}, f32[5,4,16,256]{3,2,1,0:T(8,128)S(1)}, u32[]{:S(2)}, u32[]{:S(2)}) collective-permute-start(f32[5,4,16,256]{3,2,1,0:T(8,128)S(1)} %get-tuple-element.9), channel_id=1, source_target_pairs={{16,32},{48,64},{80,96},{112,128},{144,160},{176,192},{208,224},{2... | collective-permute-start | bytes 983048 | tf_op jit(solution)/shard_map/ppermute | solution.py:193
  13.3 1.9 %collective-permute-start.2 = (f32[5,4,16,256]{3,2,1,0:T(8,128)S(1)}, f32[5,4,16,256]{3,2,1,0:T(8,128)S(1)}, u32[]{:S(2)}, u32[]{:S(2)}) collective-permute-start(f32[5,4,16,256]{3,2,1,0:T(8,128)S(1)} %get-tuple-element.10), channel_id=1, source_target_pairs={{0,16},{32,48},{64,80},{96,112},{128,144},{160,176},{192,208},{224... | collective-permute-start | bytes 983048 | tf_op jit(solution)/shard_map/ppermute | solution.py:193
  15.2 4.0 %collective-permute-start = (f32[5,4,8,256]{3,2,1,0:T(8,128)S(1)}, f32[5,4,8,256]{3,2,1,0:T(8,128)S(1)}, u32[]{:S(2)}, u32[]{:S(2)}) collective-permute-start(f32[5,4,8,256]{3,2,1,0:T(8,128)S(1)} %get-tuple-element.8), channel_id=1, source_target_pairs={{1,2},{3,4},{5,6},{7,8},{9,10},{11,12},{13,14},{15,0},{2,1},{4,3},... | collective-permute-start | bytes 491528 | tf_op jit(solution)/shard_map/ppermute | solution.py:193
  19.2 8.5 %collective-permute-start.3 = (f32[5,4,8,256]{3,2,1,0:T(8,128)S(1)}, f32[5,4,8,256]{3,2,1,0:T(8,128)S(1)}, u32[]{:S(2)}, u32[]{:S(2)}) collective-permute-start(f32[5,4,8,256]{3,2,1,0:T(8,128)S(1)} %get-tuple-element.11), channel_id=1, source_target_pairs={{0,1},{2,3},{4,5},{6,7},{8,9},{10,11},{12,13},{14,15},{1,0},{3,2},... | collective-permute-start | bytes 491528 | tf_op jit(solution)/shard_map/ppermute | solution.py:193
  28.3 0.0 copy-done.1
  28.3 0.0 copy-start.2
  28.3 1.1 %copy-done.2 = f32[5,8,16,256]{3,2,1,0:T(8,128)S(1)} copy-done((f32[5,8,16,256]{3,2,1,0:T(8,128)S(1)}, f32[5,8,16,256]{3,2,1,0:T(8,128)}, u32[]{:S(2)}) %copy-start.2) | copy-done | bytes 655384
  29.4 2.7 %shard_map.50.inner = f32[5,8,16,256]{3,2,1,0:T(8,128)S(1)} custom-call(f32[1]{0:T(128)} %bitcast.4.speed, f32[5,8,16,256]{3,2,1,0:T(8,128)S(1)} %copy-done.1, f32[5,8,16,256]{3,2,1,0:T(8,128)S(1)} %copy-done.2), custom_call_target="tpu_custom_call" | custom-call | tf_op jit(solution)/shard_map/pallas_call | solution.py:180
  32.1 0.0 collective-permute-done.y_odd
  32.1 0.0 collective-permute-done.3.y_even
  32.1 0.0 collective-permute-done.1.x_odd
  32.2 0.0 collective-permute-done.2.x_even
  32.2 1.8 %shard_map.52 = (f32[5,8,16,256]{3,2,1,0:T(8,128)}, f32[512,128]{1,0:T(8,128)S(1)}) custom-call(f32[1]{0:T(128)} %bitcast.5.speed, f32[5,8,16,256]{3,2,1,0:T(8,128)S(1)} %shard_map.50.inner, f32[5,4,8,256]{3,2,1,0:T(8,128)S(1)} %collective-permute-done.y_odd, f32[5,4,16,256]{3,2,1,0:T(8,128)S(1)} %collective-permute-done.1.x_odd, ...), custom_call_target="tpu_custom_call" | custom-call | tf_op jit(solution)/shard_map/pallas_call | solution.py:180
  34.0 26.5 %all_to_all.9 = f32[512,1,128]{2,1,0:T(1,128)S(1)} all-to-all(f32[512,1,128]{2,1,0:T(1,128)S(1)} %bitcast.6), channel_id=1, replica_groups=mesh['gx'=32,'gy'=16] {'gx','gy'}, dimensions={0} | all-to-all | bytes 524288 | tf_op jit(solution)/shard_map/all_to_all | solution.py:235
  60.5 1.1 %reduce_max.9 = f32[]{:T(128)} reduce(f32[512,1,128]{2,1,0:T(1,128)S(1)} %all_to_all.9, f32[]{:T(128)} %constant.0.clone.1), dimensions={0,1,2}, to_apply=%region_0.0 | reduce | flops 65535 | bytes 262152 | tf_op jit(solution)/shard_map/reduce_max | solution.py:236
Async XLA Ops:
  0.6 1.1 %copy-start = (f32[5,8,16,256]{3,2,1,0:T(8,128)S(1)}, f32[5,8,16,256]{3,2,1,0:T(8,128)}, u32[]{:S(2)}) copy-start(f32[5,8,16,256]{3,2,1,0:T(8,128)} %start.3) | copy-start | bytes 1966084
  1.7 26.6 %copy-start.1 = (f32[5,8,16,256]{3,2,1,0:T(8,128)S(1)}, f32[5,8,16,256]{3,2,1,0:T(8,128)}, u32[]{:S(2)}) copy-start(f32[5,8,16,256]{3,2,1,0:T(8,128)} %start.3) | copy-start | bytes 1966084
  1.8 30.3 %collective-permute-start.1 = (f32[5,4,16,256]{3,2,1,0:T(8,128)S(1)}, f32[5,4,16,256]{3,2,1,0:T(8,128)S(1)}, u32[]{:S(2)}, u32[]{:S(2)}) collective-permute-start(f32[5,4,16,256]{3,2,1,0:T(8,128)S(1)} %get-tuple-element.9), channel_id=1, source_target_pairs={{16,32},{48,64},{80,96},{112,128},{144,160},{176,192},{208,224},{2... | collective-permute-start | bytes 983048 | tf_op jit(solution)/shard_map/ppermute | solution.py:193
  13.3 18.9 %collective-permute-start.2 = (f32[5,4,16,256]{3,2,1,0:T(8,128)S(1)}, f32[5,4,16,256]{3,2,1,0:T(8,128)S(1)}, u32[]{:S(2)}, u32[]{:S(2)}) collective-permute-start(f32[5,4,16,256]{3,2,1,0:T(8,128)S(1)} %get-tuple-element.10), channel_id=1, source_target_pairs={{0,16},{32,48},{64,80},{96,112},{128,144},{160,176},{192,208},{224... | collective-permute-start | bytes 983048 | tf_op jit(solution)/shard_map/ppermute | solution.py:193
  15.2 16.9 %collective-permute-start = (f32[5,4,8,256]{3,2,1,0:T(8,128)S(1)}, f32[5,4,8,256]{3,2,1,0:T(8,128)S(1)}, u32[]{:S(2)}, u32[]{:S(2)}) collective-permute-start(f32[5,4,8,256]{3,2,1,0:T(8,128)S(1)} %get-tuple-element.8), channel_id=1, source_target_pairs={{1,2},{3,4},{5,6},{7,8},{9,10},{11,12},{13,14},{15,0},{2,1},{4,3},... | collective-permute-start | bytes 491528 | tf_op jit(solution)/shard_map/ppermute | solution.py:193
  19.2 12.9 %collective-permute-start.3 = (f32[5,4,8,256]{3,2,1,0:T(8,128)S(1)}, f32[5,4,8,256]{3,2,1,0:T(8,128)S(1)}, u32[]{:S(2)}, u32[]{:S(2)}) collective-permute-start(f32[5,4,8,256]{3,2,1,0:T(8,128)S(1)} %get-tuple-element.11), channel_id=1, source_target_pairs={{0,1},{2,3},{4,5},{6,7},{8,9},{10,11},{12,13},{14,15},{1,0},{3,2},... | collective-permute-start | bytes 491528 | tf_op jit(solution)/shard_map/ppermute | solution.py:193
  28.3 1.1 %copy-start.2 = (f32[5,8,16,256]{3,2,1,0:T(8,128)S(1)}, f32[5,8,16,256]{3,2,1,0:T(8,128)}, u32[]{:S(2)}) copy-start(f32[5,8,16,256]{3,2,1,0:T(8,128)} %section.1) | copy-start | bytes 1966084

commit v4 on v3

v4 whole, which is shorter than its diff:
```python
import jax
import jax.numpy as jnp
from jax import lax
from jax.experimental import pallas as pl
from jax.experimental.pallas import tpu as pltpu
from jax.sharding import PartitionSpec as P

GAMMA = 1.4
COURANT = 0.3
VISCOSITY = 0.05
CONDUCTION = 0.07
FIRST = (0.8, -0.2, 4.0 / 105.0, -1.0 / 280.0)
SECOND = (1.6, -0.2, 8.0 / 315.0, -1.0 / 560.0)
CENTRE = -205.0 / 72.0
VMEM = pltpu.VMEM
SMEM = pltpu.SMEM
INNER_COST, ODD_COST, EVEN_COST = 1 << 20, 8 << 20, 1 << 20


def primitive(q):
    inverse = 1.0 / q[0]
    u, v, w = q[1] * inverse, q[2] * inverse, q[3] * inverse
    kinetic = 0.5 * (u * u + v * v + w * w)
    pressure = (GAMMA - 1.0) * (q[4] - q[0] * kinetic)
    return inverse, (u, v, w), kinetic, pressure


def flux(q, velocity, pressure, d):
    s = velocity[d]
    out = [q[1 + d], q[1] * s, q[2] * s, q[3] * s, (q[4] + pressure) * s]
    out[1 + d] = out[1 + d] + pressure
    return out


def smooth(inverse, velocity, kinetic, pressure):
    heat = VISCOSITY * kinetic + CONDUCTION * (pressure * inverse)
    return [None] + [VISCOSITY * s for s in velocity] + [heat]


def sides(f, g, m):
    first = FIRST[m - 1] * f
    if g is None:
        return -first, first
    second = SECOND[m - 1] * g
    return second - first, second + first


def odd(axis):
    return lax.rem(lax.axis_index(axis), 2)


def pack_kernel(start, x_odd, y_odd, x_even, y_even):
    side = odd("gx")
    x_even[...] = start[:, pl.ds(4 - 4 * side, 4)]
    x_odd[...] = start[:, pl.ds(4 * side, 4)]
    first = lax.broadcasted_iota(jnp.int32, (8, 256), 0) < 4
    upper = odd("gy") == 0
    for c in range(5):
        for j in range(4):
            a, b = start[c, 2 * j, 0:8], start[c, 2 * j + 1, 0:8]
            low = jnp.where(first, a, pltpu.roll(b, 4, 0))
            a, b = start[c, 2 * j, 8:16], start[c, 2 * j + 1, 8:16]
            high = jnp.where(first, pltpu.roll(b, 4, 0), a)
            y_even[c, j] = jnp.where(upper, high, low)
            y_odd[c, j] = jnp.where(upper, low, high)


def inner_kernel(speed, start, section_far, out, step, section, fluxes, smooths, sems):
    copies = [
        pltpu.make_async_copy(section_far.at[:, i], section.at[:, i], sems.at[i]) for i in range(8)
    ]
    for copy in copies:
        copy.start()
    rows = lax.broadcasted_iota(jnp.int32, (16, 256), 0)

    def layer(i, carry):
        pltpu.make_async_copy(section_far.at[:, i], section.at[:, i], sems.at[i]).wait()
        q = [section[c, i] for c in range(5)]
        inverse, velocity, kinetic, pressure = primitive(q)
        g = smooth(inverse, velocity, kinetic, pressure)
        fx = flux(q, velocity, pressure, 0)
        fy = flux(q, velocity, pressure, 1)
        fz = flux(q, velocity, pressure, 2)
        for c in range(5):
            fluxes[c, i] = fx[c]
            total = jnp.zeros((16, 256), jnp.float32)
            if c:
                smooths[c - 1, i] = g[c]
                total = (3.0 * CENTRE) * g[c]
            for m in range(1, 5):
                up, down = sides(fz[c], g[c], m)
                total = total + pltpu.roll(up, 256 - m, 1) + pltpu.roll(down, m, 1)
                up, down = sides(fy[c], g[c], m)
                total = total + jnp.where(rows < 16 - m, pltpu.roll(up, 16 - m, 0), 0.0)
                total = total + jnp.where(rows >= m, pltpu.roll(down, m, 0), 0.0)
            out[c, i] = total
        return carry

    lax.fori_loop(0, 8, layer, 0)
    factor = (0.25 * COURANT) / jnp.broadcast_to(speed[...], (8, 128))
    step[...] = factor
    factor = jnp.tile(factor, (2, 2))
    for c in range(5):
        for i in range(8):
            total = out[c, i]
            for m in range(1, 5):
                for j, sign in ((i + m, -1.0), (i - m, 1.0)):
                    if 0 <= j < 8:
                        total = total + (sign * FIRST[m - 1]) * fluxes[c, j]
                        if c:
                            total = total + SECOND[m - 1] * smooths[c - 1, j]
            out[c, i] = 0.75 * start[c, i] + 0.25 * section[c, i] + factor * total


def y_side(rim, sums, below):
    rows = lax.broadcasted_iota(jnp.int32, (8, 256), 0)

    def pair(j, carry):
        q = [rim[c, j] for c in range(5)]
        inverse, velocity, kinetic, pressure = primitive(q)
        g = smooth(inverse, velocity, kinetic, pressure)
        f = flux(q, velocity, pressure, 1)
        for c in range(5):
            totals = [None, None]
            for m in range(1, 5):
                up, down = sides(f[c], g[c], m)
                for second in range(2):
                    if below:
                        part = jnp.where(rows < m, pltpu.roll(down, (m + 4 * second) % 8, 0), 0.0)
                    else:
                        part = jnp.where(rows >= 8 - m, pltpu.roll(up, (8 - m + 4 * second) % 8, 0), 0.0)
                    totals[second] = part if totals[second] is None else totals[second] + part
            sums[c, 2 * j] = totals[0]
            sums[c, 2 * j + 1] = totals[1]
        return carry

    lax.fori_loop(0, 4, pair, 0)


def rim_terms(x_below, y_below, x_rim, y_rim, fluxes, smooths, sums):
    @pl.when(y_below == 1)
    def _():
        y_side(y_rim, sums, True)

    @pl.when(y_below == 0)
    def _():
        y_side(y_rim, sums, False)

    sign = jnp.where(x_below == 1, 1.0, -1.0)

    def x_layer(d, carry):
        i = jnp.where(x_below == 1, 3 - d, d)
        q = [x_rim[c, i] for c in range(5)]
        inverse, velocity, kinetic, pressure = primitive(q)
        g = smooth(inverse, velocity, kinetic, pressure)
        f = flux(q, velocity, pressure, 0)
        for c in range(5):
            fluxes[c, d] = sign * f[c]
            if c:
                smooths[c - 1, d] = g[c]
        return carry

    lax.fori_loop(0, 4, x_layer, 0)


def rim_layer(t, x_below, y_below, inner, step, fluxes, smooths, sums):
    i = jnp.where(x_below == 1, t, 7 - t)
    factor = jnp.tile(step[...], (1, 2))
    low = jnp.where(y_below == 1, factor, 0.0)
    edge = jnp.concatenate([low, factor - low], axis=0)
    factor = jnp.concatenate([factor, factor], axis=0)
    values = []
    for c in range(5):
        part = sums[c, i]
        value = inner[c, i] + edge * jnp.concatenate([part, part], axis=0)
        total = None
        for d in range(4 - t):
            term = FIRST[d + t] * fluxes[c, d]
            if c:
                term = term + SECOND[d + t] * smooths[c - 1, d]
            total = term if total is None else total + term
        if total is not None:
            value = value + factor * total
        values.append(value)
    return i, values


def odd_kernel(inner, step, x_rim, y_rim, out, fluxes, smooths, sums):
    x_below, y_below = 1 - odd("gx"), 1 - odd("gy")
    rim_terms(x_below, y_below, x_rim, y_rim, fluxes, smooths, sums)
    for t in range(8):
        i, values = rim_layer(t, x_below, y_below, inner, step, fluxes, smooths, sums)
        for c in range(5):
            out[c, i] = values[c]


def even_kernel(inner, step, x_rim, y_rim, out, peak, fluxes, smooths, sums):
    x_below, y_below = odd("gx"), odd("gy")
    rim_terms(x_below, y_below, x_rim, y_rim, fluxes, smooths, sums)
    most = None
    for t in range(8):
        i, values = rim_layer(t, x_below, y_below, inner, step, fluxes, smooths, sums)
        for c in range(5):
            out[c, i] = values[c]
        inverse, velocity, kinetic, pressure = primitive(values)
        speed = jnp.sqrt(2.0 * kinetic) + jnp.sqrt(GAMMA * pressure * inverse)
        most = speed if most is None else jnp.maximum(most, speed)
    peak[...] = jnp.full(peak.shape, jnp.max(most), jnp.float32)


def most_kernel(peaks, out):
    out[0] = jnp.max(peaks[...])


def in_vmem(*sizes):
    return VMEM(sizes, jnp.float32)


def call(kernel, outs, in_specs, scratch, cost, *arrays, out_space=VMEM):
    estimate = pl.CostEstimate(flops=cost * 300, bytes_accessed=cost, transcendentals=0) if cost else None
    return pl.pallas_call(
        kernel,
        out_shape=outs,
        in_specs=[pl.BlockSpec(memory_space=m) for m in in_specs],
        out_specs=tuple(pl.BlockSpec(memory_space=out_space) for _ in outs),
        scratch_shapes=scratch,
        cost_estimate=estimate,
        compiler_params=pltpu.CompilerParams(vmem_limit_bytes=24 << 20),
    )(*arrays)


def far(x):
    return pltpu.with_memory_space_constraint(x, pltpu.HBM)


def swap(x, axis, offset):
    n = lax.axis_size(axis)
    pairs = [((i + offset) % n, (i + 1 + offset) % n) for i in range(0, n, 2)]
    return lax.ppermute(x, axis, pairs + [(b, a) for a, b in pairs])


def local(start, section, previous_speed):
    devices = lax.axis_size(("gx", "gy"))
    x_odd, y_odd, x_even, y_even = call(
        pack_kernel,
        (in_vmem(5, 4, 16, 256), in_vmem(5, 4, 8, 256)) * 2,
        [VMEM],
        [],
        0,
        start,
    )
    x_odd, y_odd = swap(x_odd, "gx", 1), swap(y_odd, "gy", 1)
    y_even, x_even = swap(y_even, "gy", 0), swap(x_even, "gx", 0)
    state = in_vmem(5, 8, 16, 256)
    inner, step = call(
        inner_kernel,
        (state, in_vmem(8, 128)),
        [VMEM, VMEM, pltpu.HBM],
        [
            state,
            state,
            in_vmem(4, 8, 16, 256),
            pltpu.SemaphoreType.DMA((8,)),
        ],
        INNER_COST,
        previous_speed.reshape(1, 1),
        start,
        far(section),
    )
    rims = [in_vmem(5, 4, 16, 256), in_vmem(4, 4, 16, 256), in_vmem(5, 8, 8, 256)]
    (inner,) = call(odd_kernel, (state,), [VMEM] * 4, rims, ODD_COST, inner, step, x_odd, y_odd)
    new, peak = call(
        even_kernel,
        (state, in_vmem(devices, 128)),
        [VMEM] * 4,
        rims,
        EVEN_COST,
        inner,
        step,
        x_even,
        y_even,
    )
    peaks = lax.all_to_all(peak, ("gx", "gy"), 0, 0, tiled=True)
    (most,) = call(
        most_kernel, (SMEM((1,), jnp.float32),), [VMEM], [], 0, peaks, out_space=SMEM
    )
    return new, most.reshape(())


def solution(mesh):
    spec = P(None, "gx", "gy", None)
    return jax.shard_map(
        local, mesh=mesh, in_specs=(spec, spec, P()), out_specs=(spec, P()), check_vma=False
    )
```

time: 62 us -> 60.1 us (0.969)
  blocking collectives: 26.5 us -> 0 us
  waiting for transfers between devices: 0.01 us -> 15.8 us
  starting transfers between devices: 25.8 us -> 34.2 us
  Pallas kernels: 4.62 us -> 5.96 us
  other arithmetic: 1.14 us -> 0 us
    all_to_all x1 -> x0, blocking collectives: 26.5 us -> none  [local(): peaks = lax.all_to_all(peak, ('gx', 'gy'), 0, 0, tiled=True)]
    all_to_all x0 -> x1, waiting for transfers between devices: none -> 15.8 us  [local(): peaks = lax.all_to_all(peak, ('gx', 'gy'), 0, 0, tiled=True)]
    all_to_all x0 -> x1, starting transfers between devices: none -> 8.34 us  [local(): peaks = lax.all_to_all(peak, ('gx', 'gy'), 0, 0, tiled=True)]
    pallas_call x3 -> x5, Pallas kernels: 4.62 us -> 5.96 us  [call(): pl.pallas_call(kernel, out_shape=outs, in_specs=[pl.BlockSpec(memory_spac...]
    reduce_max x1 -> x0, other arithmetic: 1.14 us -> none  [local(): return (new, jnp.max(peaks))]
    unnamed x6 -> x5, local copies, waits for them, and re-layouts: 2.17 us -> 1.92 us
  transfers between devices with their start and end apart: 4 -> 5, of which waited for: 0 -> 1; matrix products, arithmetic and copies ran while one was open for 0% -> 1% of each run, Pallas kernels for 4% -> 7%
where the time goes in v4:
time: 60.1 us; the launch traced here: 59.8 us
  starting transfers between devices  34.2 us (57%)
  waiting for transfers between devices  15.8 us (26%)
  Pallas kernels  5.96 us (10%)
  local copies, waits for them, and re-layouts  1.92 us (3%)
  between operations  1.9 us (3%)
    ppermute x4, starting transfers between devices, swap(): return lax.ppermute(x, axis, pairs + [(b, a) for a, b in pairs])  25.8 us
    all_to_all x1, waiting for transfers between devices, local(): peaks = lax.all_to_all(peak, ('gx', 'gy'), 0, 0, tiled=True)  15.8 us
    all_to_all x1, starting transfers between devices, local(): peaks = lax.all_to_all(peak, ('gx', 'gy'), 0, 0, tiled=True)  8.34 us
    pallas_call x5, Pallas kernels, call(): pl.pallas_call(kernel, out_shape=outs, in_specs=[pl.BlockSpec(memory_spac...  5.96 us
    unnamed x5, local copies, waits for them, and re-layouts  1.92 us
  transfers between devices with their start and end apart: 5, of which 1 were waited for; matrix products, arithmetic and copies ran while one was open for 1% of the time, Pallas kernels for 7%

profile of v4, /device:TPU:1, one launch (start us, length us, event | category | flops | bytes accessed | tf_op | source)
XLA Modules:
  0.0 59.8 jit_solution(2887002914804483743)
XLA Ops:
  0.6 0.0 copy-start
  0.6 1.1 %copy-done = f32[5,8,16,256]{3,2,1,0:T(8,128)S(1)} copy-done((f32[5,8,16,256]{3,2,1,0:T(8,128)S(1)}, f32[5,8,16,256]{3,2,1,0:T(8,128)}, u32[]{:S(2)}) %copy-start) | copy-done | bytes 655384
  1.7 0.0 copy-start.1
  1.7 0.1 shard_map.51
  1.8 11.5 %collective-permute-start = (f32[5,4,16,256]{3,2,1,0:T(8,128)S(1)}, f32[5,4,16,256]{3,2,1,0:T(8,128)S(1)}, u32[]{:S(2)}, u32[]{:S(2)}) collective-permute-start(f32[5,4,16,256]{3,2,1,0:T(8,128)S(1)} %get-tuple-element.12), channel_id=1, source_target_pairs={{16,32},{48,64},{80,96},{112,128},{144,160},{176,192},{208,224},{2... | collective-permute-start | bytes 983048 | tf_op jit(solution)/shard_map/ppermute | solution.py:239
  13.3 4.0 %collective-permute-start.1 = (f32[5,4,8,256]{3,2,1,0:T(8,128)S(1)}, f32[5,4,8,256]{3,2,1,0:T(8,128)S(1)}, u32[]{:S(2)}, u32[]{:S(2)}) collective-permute-start(f32[5,4,8,256]{3,2,1,0:T(8,128)S(1)} %get-tuple-element.13), channel_id=1, source_target_pairs={{1,2},{3,4},{5,6},{7,8},{9,10},{11,12},{13,14},{15,0},{2,1},{4,3},... | collective-permute-start | bytes 491528 | tf_op jit(solution)/shard_map/ppermute | solution.py:239
  17.3 1.9 %collective-permute-start.2 = (f32[5,4,16,256]{3,2,1,0:T(8,128)S(1)}, f32[5,4,16,256]{3,2,1,0:T(8,128)S(1)}, u32[]{:S(2)}, u32[]{:S(2)}) collective-permute-start(f32[5,4,16,256]{3,2,1,0:T(8,128)S(1)} %get-tuple-element.14), channel_id=1, source_target_pairs={{0,16},{32,48},{64,80},{96,112},{128,144},{160,176},{192,208},{224... | collective-permute-start | bytes 983048 | tf_op jit(solution)/shard_map/ppermute | solution.py:239
  19.2 8.5 %collective-permute-start.3 = (f32[5,4,8,256]{3,2,1,0:T(8,128)S(1)}, f32[5,4,8,256]{3,2,1,0:T(8,128)S(1)}, u32[]{:S(2)}, u32[]{:S(2)}) collective-permute-start(f32[5,4,8,256]{3,2,1,0:T(8,128)S(1)} %get-tuple-element.15), channel_id=1, source_target_pairs={{0,1},{2,3},{4,5},{6,7},{8,9},{10,11},{12,13},{14,15},{1,0},{3,2},... | collective-permute-start | bytes 491528 | tf_op jit(solution)/shard_map/ppermute | solution.py:239
  28.3 0.0 copy-done.1
  28.3 3.7 %shard_map.50 = (f32[5,8,16,256]{3,2,1,0:T(8,128)S(1)}, f32[8,128]{1,0:T(8,128)S(1)}) custom-call(f32[1,1]{1,0:T(1,128)} %bitcast.6.speed, f32[5,8,16,256]{3,2,1,0:T(8,128)S(1)} %copy-done.1, f32[5,8,16,256]{3,2,1,0:T(8,128)} %section_far.1), custom_call_target="tpu_custom_call" | custom-call | flops 314572800 | bytes 1048576 | tf_op jit(solution)/shard_map/pallas_call | solution.py:221
  32.1 0.0 collective-permute-done.1.y_rim
  32.1 0.0 collective-permute-done.x_rim
  32.1 0.5 shard_map.52.inner
  32.6 0.0 collective-permute-done.3.y_rim
  32.6 0.0 collective-permute-done.2.x_rim
  32.6 1.5 %shard_map.53 = (f32[5,8,16,256]{3,2,1,0:T(8,128)S(1)}, f32[512,128]{1,0:T(8,128)}) custom-call(f32[5,8,16,256]{3,2,1,0:T(8,128)S(1)} %shard_map.52.inner, f32[8,128]{1,0:T(8,128)S(1)} %get-tuple-element.11.step, f32[5,4,16,256]{3,2,1,0:T(8,128)S(1)} %collective-permute-done.2.x_rim, f32[5,4,8,256]{3,2,1,0:T(8,128)S(1)} %collective-permute-done.3.y_rim), custom_call_target="tpu_custom_call" | custom-call | flops 314572800 | bytes 1048576 | tf_op jit(solution)/shard_map/pallas_call | solution.py:221
  34.1 8.3 %all-to-all-start = ((f32[512,1,128]{2,1,0:T(1,128)}), f32[512,1,128]{2,1,0:T(1,128)S(1)}, u32[]{:S(2)}, u32[]{:S(2)}) async-start(f32[512,1,128]{2,1,0:T(1,128)} %bitcast.2), calls=%async_computation | async-start | bytes 524288 | tf_op jit(solution)/shard_map/all_to_all | solution.py:283
  42.5 0.8 %copy.6 = f32[5,8,16,256]{3,2,1,0:T(8,128)} copy(f32[5,8,16,256]{3,2,1,0:T(8,128)S(1)} %get-tuple-element.18) | data formatting | bytes 1310720
  43.3 15.8 %all-to-all-done = f32[512,1,128]{2,1,0:T(1,128)S(1)} async-done(((f32[512,1,128]{2,1,0:T(1,128)}), f32[512,1,128]{2,1,0:T(1,128)S(1)}, u32[]{:S(2)}, u32[]{:S(2)}) %all-to-all-start) | async-done | bytes 262176 | tf_op jit(solution)/shard_map/all_to_all | solution.py:283
  59.1 0.1 shard_map.54
Async XLA Ops:
  0.6 1.1 %copy-start = (f32[5,8,16,256]{3,2,1,0:T(8,128)S(1)}, f32[5,8,16,256]{3,2,1,0:T(8,128)}, u32[]{:S(2)}) copy-start(f32[5,8,16,256]{3,2,1,0:T(8,128)} %start.3) | copy-start | bytes 1966084
  1.7 26.6 %copy-start.1 = (f32[5,8,16,256]{3,2,1,0:T(8,128)S(1)}, f32[5,8,16,256]{3,2,1,0:T(8,128)}, u32[]{:S(2)}) copy-start(f32[5,8,16,256]{3,2,1,0:T(8,128)} %start.3) | copy-start | bytes 1966084
  1.8 30.3 %collective-permute-start = (f32[5,4,16,256]{3,2,1,0:T(8,128)S(1)}, f32[5,4,16,256]{3,2,1,0:T(8,128)S(1)}, u32[]{:S(2)}, u32[]{:S(2)}) collective-permute-start(f32[5,4,16,256]{3,2,1,0:T(8,128)S(1)} %get-tuple-element.12), channel_id=1, source_target_pairs={{16,32},{48,64},{80,96},{112,128},{144,160},{176,192},{208,224},{2... | collective-permute-start | bytes 983048 | tf_op jit(solution)/shard_map/ppermute | solution.py:239
  13.3 18.8 %collective-permute-start.1 = (f32[5,4,8,256]{3,2,1,0:T(8,128)S(1)}, f32[5,4,8,256]{3,2,1,0:T(8,128)S(1)}, u32[]{:S(2)}, u32[]{:S(2)}) collective-permute-start(f32[5,4,8,256]{3,2,1,0:T(8,128)S(1)} %get-tuple-element.13), channel_id=1, source_target_pairs={{1,2},{3,4},{5,6},{7,8},{9,10},{11,12},{13,14},{15,0},{2,1},{4,3},... | collective-permute-start | bytes 491528 | tf_op jit(solution)/shard_map/ppermute | solution.py:239
  17.3 15.4 %collective-permute-start.2 = (f32[5,4,16,256]{3,2,1,0:T(8,128)S(1)}, f32[5,4,16,256]{3,2,1,0:T(8,128)S(1)}, u32[]{:S(2)}, u32[]{:S(2)}) collective-permute-start(f32[5,4,16,256]{3,2,1,0:T(8,128)S(1)} %get-tuple-element.14), channel_id=1, source_target_pairs={{0,16},{32,48},{64,80},{96,112},{128,144},{160,176},{192,208},{224... | collective-permute-start | bytes 983048 | tf_op jit(solution)/shard_map/ppermute | solution.py:239
  19.2 13.4 %collective-permute-start.3 = (f32[5,4,8,256]{3,2,1,0:T(8,128)S(1)}, f32[5,4,8,256]{3,2,1,0:T(8,128)S(1)}, u32[]{:S(2)}, u32[]{:S(2)}) collective-permute-start(f32[5,4,8,256]{3,2,1,0:T(8,128)S(1)} %get-tuple-element.15), channel_id=1, source_target_pairs={{0,1},{2,3},{4,5},{6,7},{8,9},{10,11},{12,13},{14,15},{1,0},{3,2},... | collective-permute-start | bytes 491528 | tf_op jit(solution)/shard_map/ppermute | solution.py:239
  34.1 25.0 %all-to-all-start = ((f32[512,1,128]{2,1,0:T(1,128)}), f32[512,1,128]{2,1,0:T(1,128)S(1)}, u32[]{:S(2)}, u32[]{:S(2)}) async-start(f32[512,1,128]{2,1,0:T(1,128)} %bitcast.2), calls=%async_computation | async-start | bytes 524288 | tf_op jit(solution)/shard_map/all_to_all | solution.py:283

commit v5 on v4

--- a/solution.py
+++ b/solution.py
@@ -3,6 +3,7 @@
 from jax import lax
 from jax.experimental import pallas as pl
 from jax.experimental.pallas import tpu as pltpu
+from jax.sharding import Mesh
 from jax.sharding import PartitionSpec as P
 
 GAMMA = 1.4
@@ -12,6 +13,10 @@
 FIRST = (0.8, -0.2, 4.0 / 105.0, -1.0 / 280.0)
 SECOND = (1.6, -0.2, 8.0 / 315.0, -1.0 / 560.0)
 CENTRE = -205.0 / 72.0
+AXES = ("z_lo", "y", "z_hi", "x", "core")
+SIZES = (4, 8, 2, 4, 2)
+GX, GY = AXES[:2], AXES[2:]
+NEAR, FAR = ("y", "core"), ("z_lo", "z_hi", "x")
 VMEM = pltpu.VMEM
 SMEM = pltpu.SMEM
 INNER_COST, ODD_COST, EVEN_COST = 1 << 20, 8 << 20, 1 << 20
@@ -49,13 +54,22 @@
     return lax.rem(lax.axis_index(axis), 2)
 
 
-def pack_kernel(start, x_odd, y_odd, x_even, y_even):
-    side = odd("gx")
-    x_even[...] = start[:, pl.ds(4 - 4 * side, 4)]
-    x_odd[...] = start[:, pl.ds(4 * side, 4)]
+def pack_kernel(far_start, x_odd, y_odd, x_even, y_even, start, sems):
+    copies = [
+        pltpu.make_async_copy(far_start.at[c, rows], start.at[c, rows], sems.at[c, k])
+        for c in range(5)
+        for k, rows in enumerate((pl.ds(0, 4), pl.ds(4, 4)))
+    ]
+    for copy in copies:
+        copy.start()
+    side = odd("y")
     first = lax.broadcasted_iota(jnp.int32, (8, 256), 0) < 4
-    upper = odd("gy") == 0
+    upper = odd("core") == 0
     for c in range(5):
+        copies[2 * c].wait()
+        copies[2 * c + 1].wait()
+        x_even[c] = start[c, pl.ds(4 - 4 * side, 4)]
+        x_odd[c] = start[c, pl.ds(4 * side, 4)]
         for j in range(4):
             a, b = start[c, 2 * j, 0:8], start[c, 2 * j + 1, 0:8]
             low = jnp.where(first, a, pltpu.roll(b, 4, 0))
@@ -186,7 +200,7 @@
 
 
 def odd_kernel(inner, step, x_rim, y_rim, out, fluxes, smooths, sums):
-    x_below, y_below = 1 - odd("gx"), 1 - odd("gy")
+    x_below, y_below = 1 - odd("y"), 1 - odd("core")
     rim_terms(x_below, y_below, x_rim, y_rim, fluxes, smooths, sums)
     for t in range(8):
         i, values = rim_layer(t, x_below, y_below, inner, step, fluxes, smooths, sums)
@@ -195,7 +209,7 @@
 
 
 def even_kernel(inner, step, x_rim, y_rim, out, peak, fluxes, smooths, sums):
-    x_below, y_below = odd("gx"), odd("gy")
+    x_below, y_below = odd("y"), odd("core")
     rim_terms(x_below, y_below, x_rim, y_rim, fluxes, smooths, sums)
     most = None
     for t in range(8):
@@ -205,7 +219,16 @@
         inverse, velocity, kinetic, pressure = primitive(values)
         speed = jnp.sqrt(2.0 * kinetic) + jnp.sqrt(GAMMA * pressure * inverse)
         most = speed if most is None else jnp.maximum(most, speed)
-    peak[...] = jnp.full(peak.shape, jnp.max(most), jnp.float32)
+    most = jnp.maximum(most[:, :128], most[:, 128:])
+    spread(most, peak)
+
+
+def spread(values, out):
+    out[...] = jnp.broadcast_to(jnp.max(values, axis=0, keepdims=True), out.shape)
+
+
+def pass_kernel(peaks, out):
+    spread(peaks[...], out)
 
 
 def most_kernel(peaks, out):
@@ -240,17 +263,16 @@
 
 
 def local(start, section, previous_speed):
-    devices = lax.axis_size(("gx", "gy"))
     x_odd, y_odd, x_even, y_even = call(
         pack_kernel,
         (in_vmem(5, 4, 16, 256), in_vmem(5, 4, 8, 256)) * 2,
-        [VMEM],
-        [],
+        [pltpu.HBM],
+        [in_vmem(5, 8, 16, 256), pltpu.SemaphoreType.DMA((5, 2))],
         0,
-        start,
-    )
-    x_odd, y_odd = swap(x_odd, "gx", 1), swap(y_odd, "gy", 1)
-    y_even, x_even = swap(y_even, "gy", 0), swap(x_even, "gx", 0)
+        far(start),
+    )
+    x_odd, y_odd = swap(x_odd, GX, 1), swap(y_odd, GY, 1)
+    y_even, x_even = swap(y_even, GY, 0), swap(x_even, GX, 0)
     state = in_vmem(5, 8, 16, 256)
     inner, step = call(
         inner_kernel,
@@ -271,7 +293,7 @@
     (inner,) = call(odd_kernel, (state,), [VMEM] * 4, rims, ODD_COST, inner, step, x_odd, y_odd)
     new, peak = call(
         even_kernel,
-        (state, in_vmem(devices, 128)),
+        (state, in_vmem(lax.axis_size(NEAR), 128)),
         [VMEM] * 4,
         rims,
         EVEN_COST,
@@ -280,7 +302,9 @@
         x_even,
         y_even,
     )
-    peaks = lax.all_to_all(peak, ("gx", "gy"), 0, 0, tiled=True)
+    peaks = lax.all_to_all(peak, NEAR, 0, 0, tiled=True)
+    (peak,) = call(pass_kernel, (in_vmem(lax.axis_size(FAR), 128),), [VMEM], [], 0, peaks)
+    peaks = lax.all_to_all(peak, FAR, 0, 0, tiled=True)
     (most,) = call(
         most_kernel, (SMEM((1,), jnp.float32),), [VMEM], [], 0, peaks, out_space=SMEM
     )
@@ -288,7 +312,8 @@
 
 
 def solution(mesh):
-    spec = P(None, "gx", "gy", None)
+    split = Mesh(mesh.devices.reshape(SIZES), AXES)
+    spec = P(None, GX, GY, None)
     return jax.shard_map(
-        local, mesh=mesh, in_specs=(spec, spec, P()), out_specs=(spec, P()), check_vma=False
-    )
+        local, mesh=split, in_specs=(spec, spec, P()), out_specs=(spec, P()), check_vma=False
+    )

time: 60.1 us -> 58.8 us (0.978)
  blocking collectives: 0 us -> 10.2 us
  waiting for transfers between devices: 15.8 us -> 7.83 us
  starting transfers between devices: 34.2 us -> 30.8 us
  local copies, waits for them, and re-layouts: 1.92 us -> 0.84 us
  Pallas kernels: 5.96 us -> 6.91 us
    all_to_all x0 -> x1, blocking collectives: none -> 10.2 us  [local(): peaks = lax.all_to_all(peak, NEAR, 0, 0, tiled=True)]
    all_to_all x1, waiting for transfers between devices: 15.8 us -> 7.82 us  [local(): peaks = lax.all_to_all(peak, FAR, 0, 0, tiled=True)]
    all_to_all x1, starting transfers between devices: 8.34 us -> 5.04 us  [local(): peaks = lax.all_to_all(peak, FAR, 0, 0, tiled=True)]
    unnamed x5 -> x3, local copies, waits for them, and re-layouts: 1.92 us -> 0.84 us
    pallas_call x5 -> x6, Pallas kernels: 5.96 us -> 6.91 us  [call(): pl.pallas_call(kernel, out_shape=outs, in_specs=[pl.BlockSpec(memory_spac...]
where the time goes in v5:
time: 58.8 us; the launch traced here: 58.5 us
  starting transfers between devices  30.8 us (52%)
  blocking collectives  10.2 us (17%)
  waiting for transfers between devices  7.83 us (13%)
  Pallas kernels  6.91 us (12%)
  between operations  1.91 us (3%)
  local copies, waits for them, and re-layouts  0.84 us (1%)
    ppermute x4, starting transfers between devices, swap(): return lax.ppermute(x, axis, pairs + [(b, a) for a, b in pairs])  25.7 us
    all_to_all x1, blocking collectives, local(): peaks = lax.all_to_all(peak, NEAR, 0, 0, tiled=True)  10.2 us
    all_to_all x1, waiting for transfers between devices, local(): peaks = lax.all_to_all(peak, FAR, 0, 0, tiled=True)  7.82 us
    pallas_call x6, Pallas kernels, call(): pl.pallas_call(kernel, out_shape=outs, in_specs=[pl.BlockSpec(memory_spac...  6.91 us
    all_to_all x1, starting transfers between devices, local(): peaks = lax.all_to_all(peak, FAR, 0, 0, tiled=True)  5.04 us
  transfers between devices with their start and end apart: 5, of which 1 were waited for; matrix products, arithmetic and copies ran while one was open for 1% of the time, Pallas kernels for 7%

profile of v5, /device:TPU:1, one launch (start us, length us, event | category | flops | bytes accessed | tf_op | source)
XLA Modules:
  0.0 58.5 jit_solution(3044903905823717987)
XLA Ops:
  0.6 0.0 copy-start
  0.6 1.3 %shard_map.51 = (f32[5,4,16,256]{3,2,1,0:T(8,128)S(1)}, f32[5,4,8,256]{3,2,1,0:T(8,128)S(1)}, f32[5,4,16,256]{3,2,1,0:T(8,128)S(1)}, f32[5,4,8,256]{3,2,1,0:T(8,128)S(1)}) custom-call(f32[5,8,16,256]{3,2,1,0:T(8,128)} %far_start.1), custom_call_target="tpu_custom_call" | custom-call | tf_op jit(solution)/shard_map/pallas_call | solution.py:244
  1.9 11.4 %collective-permute-start = (f32[5,4,16,256]{3,2,1,0:T(8,128)S(1)}, f32[5,4,16,256]{3,2,1,0:T(8,128)S(1)}, u32[]{:S(2)}, u32[]{:S(2)}) collective-permute-start(f32[5,4,16,256]{3,2,1,0:T(8,128)S(1)} %get-tuple-element.12), channel_id=1, source_target_pairs={{16,32},{48,64},{80,96},{112,128},{144,160},{176,192},{208,224},{2... | collective-permute-start | bytes 983048 | tf_op jit(solution)/shard_map/ppermute | solution.py:262
  13.3 4.0 %collective-permute-start.1 = (f32[5,4,8,256]{3,2,1,0:T(8,128)S(1)}, f32[5,4,8,256]{3,2,1,0:T(8,128)S(1)}, u32[]{:S(2)}, u32[]{:S(2)}) collective-permute-start(f32[5,4,8,256]{3,2,1,0:T(8,128)S(1)} %get-tuple-element.13), channel_id=1, source_target_pairs={{1,2},{3,4},{5,6},{7,8},{9,10},{11,12},{13,14},{15,0},{2,1},{4,3},... | collective-permute-start | bytes 491528 | tf_op jit(solution)/shard_map/ppermute | solution.py:262
  17.3 1.9 %collective-permute-start.2 = (f32[5,4,16,256]{3,2,1,0:T(8,128)S(1)}, f32[5,4,16,256]{3,2,1,0:T(8,128)S(1)}, u32[]{:S(2)}, u32[]{:S(2)}) collective-permute-start(f32[5,4,16,256]{3,2,1,0:T(8,128)S(1)} %get-tuple-element.14), channel_id=1, source_target_pairs={{0,16},{32,48},{64,80},{96,112},{128,144},{160,176},{192,208},{224... | collective-permute-start | bytes 983048 | tf_op jit(solution)/shard_map/ppermute | solution.py:262
  19.2 8.5 %collective-permute-start.3 = (f32[5,4,8,256]{3,2,1,0:T(8,128)S(1)}, f32[5,4,8,256]{3,2,1,0:T(8,128)S(1)}, u32[]{:S(2)}, u32[]{:S(2)}) collective-permute-start(f32[5,4,8,256]{3,2,1,0:T(8,128)S(1)} %get-tuple-element.15), channel_id=1, source_target_pairs={{0,1},{2,3},{4,5},{6,7},{8,9},{10,11},{12,13},{14,15},{1,0},{3,2},... | collective-permute-start | bytes 491528 | tf_op jit(solution)/shard_map/ppermute | solution.py:262
  28.3 0.0 copy-done
  28.3 3.7 %shard_map.50 = (f32[5,8,16,256]{3,2,1,0:T(8,128)S(1)}, f32[8,128]{1,0:T(8,128)S(1)}) custom-call(f32[1,1]{1,0:T(1,128)} %bitcast.10.speed, f32[5,8,16,256]{3,2,1,0:T(8,128)S(1)} %copy-done, f32[5,8,16,256]{3,2,1,0:T(8,128)} %section_far.1), custom_call_target="tpu_custom_call" | custom-call | flops 314572800 | bytes 1048576 | tf_op jit(solution)/shard_map/pallas_call | solution.py:244
  32.1 0.0 collective-permute-done.1.y_rim
  32.1 0.0 collective-permute-done.x_rim
  32.1 0.5 shard_map.52.inner
  32.6 0.0 collective-permute-done.3.y_rim
  32.6 0.0 collective-permute-done.2.x_rim
  32.6 0.7 %shard_map.53 = (f32[5,8,16,256]{3,2,1,0:T(8,128)S(1)}, f32[16,128]{1,0:T(8,128)S(1)}) custom-call(f32[5,8,16,256]{3,2,1,0:T(8,128)S(1)} %shard_map.52.inner, f32[8,128]{1,0:T(8,128)S(1)} %get-tuple-element.11.step, f32[5,4,16,256]{3,2,1,0:T(8,128)S(1)} %collective-permute-done.2.x_rim, f32[5,4,8,256]{3,2,1,0:T(8,128)S(1)} %collective-permute-done.3.y_rim), custom_call_target="tpu_custom_call" | custom-call | flops 314572800 | bytes 1048576 | tf_op jit(solution)/shard_map/pallas_call | solution.py:244
  33.3 10.2 %all_to_all.22 = f32[16,1,128]{2,1,0:T(1,128)S(1)} all-to-all(f32[16,1,128]{2,1,0:T(1,128)S(1)} %bitcast.13), channel_id=1, replica_groups=mesh['z_lo'=4,'y'=8,'z_hi'=2,'x'=4,'core'=2] {'y','core'}, dimensions={0} | all-to-all | bytes 16384 | tf_op jit(solution)/shard_map/all_to_all | solution.py:305
  43.5 0.6 %shard_map.54 = f32[32,128]{1,0:T(8,128)} custom-call(f32[16,128]{1,0:T(8,128)S(1)} %bitcast.12), custom_call_target="tpu_custom_call" | custom-call | tf_op jit(solution)/shard_map/pallas_call | solution.py:244
  44.1 5.0 %all-to-all-start.1 = ((f32[32,1,128]{2,1,0:T(1,128)}), f32[32,1,128]{2,1,0:T(1,128)S(1)}, u32[]{:S(2)}, u32[]{:S(2)}) async-start(f32[32,1,128]{2,1,0:T(1,128)} %bitcast.5), calls=%async_computation.1 | async-start | bytes 32768 | tf_op jit(solution)/shard_map/all_to_all | solution.py:307
  49.2 0.8 %copy.7 = f32[5,8,16,256]{3,2,1,0:T(8,128)} copy(f32[5,8,16,256]{3,2,1,0:T(8,128)S(1)} %get-tuple-element.18) | data formatting | bytes 1310720
  50.0 7.8 %all-to-all-done.1 = f32[32,1,128]{2,1,0:T(1,128)S(1)} async-done(((f32[32,1,128]{2,1,0:T(1,128)}), f32[32,1,128]{2,1,0:T(1,128)S(1)}, u32[]{:S(2)}, u32[]{:S(2)}) %all-to-all-start.1) | async-done | bytes 16416 | tf_op jit(solution)/shard_map/all_to_all | solution.py:307
  57.8 0.1 shard_map.55
Async XLA Ops:
  0.6 27.7 %copy-start = (f32[5,8,16,256]{3,2,1,0:T(8,128)S(1)}, f32[5,8,16,256]{3,2,1,0:T(8,128)}, u32[]{:S(2)}) copy-start(f32[5,8,16,256]{3,2,1,0:T(8,128)} %far_start.1) | copy-start | bytes 1966084
  1.9 30.2 %collective-permute-start = (f32[5,4,16,256]{3,2,1,0:T(8,128)S(1)}, f32[5,4,16,256]{3,2,1,0:T(8,128)S(1)}, u32[]{:S(2)}, u32[]{:S(2)}) collective-permute-start(f32[5,4,16,256]{3,2,1,0:T(8,128)S(1)} %get-tuple-element.12), channel_id=1, source_target_pairs={{16,32},{48,64},{80,96},{112,128},{144,160},{176,192},{208,224},{2... | collective-permute-start | bytes 983048 | tf_op jit(solution)/shard_map/ppermute | solution.py:262
  13.3 18.8 %collective-permute-start.1 = (f32[5,4,8,256]{3,2,1,0:T(8,128)S(1)}, f32[5,4,8,256]{3,2,1,0:T(8,128)S(1)}, u32[]{:S(2)}, u32[]{:S(2)}) collective-permute-start(f32[5,4,8,256]{3,2,1,0:T(8,128)S(1)} %get-tuple-element.13), channel_id=1, source_target_pairs={{1,2},{3,4},{5,6},{7,8},{9,10},{11,12},{13,14},{15,0},{2,1},{4,3},... | collective-permute-start | bytes 491528 | tf_op jit(solution)/shard_map/ppermute | solution.py:262
  17.3 15.4 %collective-permute-start.2 = (f32[5,4,16,256]{3,2,1,0:T(8,128)S(1)}, f32[5,4,16,256]{3,2,1,0:T(8,128)S(1)}, u32[]{:S(2)}, u32[]{:S(2)}) collective-permute-start(f32[5,4,16,256]{3,2,1,0:T(8,128)S(1)} %get-tuple-element.14), channel_id=1, source_target_pairs={{0,16},{32,48},{64,80},{96,112},{128,144},{160,176},{192,208},{224... | collective-permute-start | bytes 983048 | tf_op jit(solution)/shard_map/ppermute | solution.py:262
  19.2 13.4 %collective-permute-start.3 = (f32[5,4,8,256]{3,2,1,0:T(8,128)S(1)}, f32[5,4,8,256]{3,2,1,0:T(8,128)S(1)}, u32[]{:S(2)}, u32[]{:S(2)}) collective-permute-start(f32[5,4,8,256]{3,2,1,0:T(8,128)S(1)} %get-tuple-element.15), channel_id=1, source_target_pairs={{0,1},{2,3},{4,5},{6,7},{8,9},{10,11},{12,13},{14,15},{1,0},{3,2},... | collective-permute-start | bytes 491528 | tf_op jit(solution)/shard_map/ppermute | solution.py:262
  44.1 13.7 %all-to-all-start.1 = ((f32[32,1,128]{2,1,0:T(1,128)}), f32[32,1,128]{2,1,0:T(1,128)S(1)}, u32[]{:S(2)}, u32[]{:S(2)}) async-start(f32[32,1,128]{2,1,0:T(1,128)} %bitcast.5), calls=%async_computation.1 | async-start | bytes 32768 | tf_op jit(solution)/shard_map/all_to_all | solution.py:307

commit v6 on v5

--- a/solution.py
+++ b/solution.py
@@ -54,7 +54,56 @@
     return lax.rem(lax.axis_index(axis), 2)
 
 
-def pack_kernel(far_start, x_odd, y_odd, x_even, y_even, start, sems):
+def early():
+    return (lax.axis_index("z_hi") == 0) & (lax.axis_index("z_lo") < 3)
+
+
+def inner_work(start, section_far, base, rate, section, fluxes, smooths, sems):
+    def copy(i):
+        return pltpu.make_async_copy(section_far.at[:, i], section.at[:, i], sems.at[i])
+
+    for i in range(8):
+        copy(i).start()
+    rows = lax.broadcasted_iota(jnp.int32, (16, 256), 0)
+
+    def layer(i, carry):
+        copy(i).wait()
+        q = [section[c, i] for c in range(5)]
+        inverse, velocity, kinetic, pressure = primitive(q)
+        g = smooth(inverse, velocity, kinetic, pressure)
+        fx = flux(q, velocity, pressure, 0)
+        fy = flux(q, velocity, pressure, 1)
+        fz = flux(q, velocity, pressure, 2)
+        for c in range(5):
+            fluxes[c, i] = fx[c]
+            base[c, i] = 0.75 * start[c, i] + 0.25 * q[c]
+            total = jnp.zeros((16, 256), jnp.float32)
+            if c:
+                smooths[c - 1, i] = g[c]
+                total = (3.0 * CENTRE) * g[c]
+            for m in range(1, 5):
+                up, down = sides(fz[c], g[c], m)
+                total = total + pltpu.roll(up, 256 - m, 1) + pltpu.roll(down, m, 1)
+                up, down = sides(fy[c], g[c], m)
+                total = total + jnp.where(rows < 16 - m, pltpu.roll(up, 16 - m, 0), 0.0)
+                total = total + jnp.where(rows >= m, pltpu.roll(down, m, 0), 0.0)
+            rate[c, i] = total
+        return carry
+
+    lax.fori_loop(0, 8, layer, 0)
+    for c in range(5):
+        for i in range(8):
+            total = rate[c, i]
+            for m in range(1, 5):
+                for j, sign in ((i + m, -1.0), (i - m, 1.0)):
+                    if 0 <= j < 8:
+                        total = total + (sign * FIRST[m - 1]) * fluxes[c, j]
+                        if c:
+                            total = total + SECOND[m - 1] * smooths[c - 1, j]
+            rate[c, i] = total
+
+
+def pack_kernel(far_start, section_far, x_odd, y_odd, x_even, y_even, start, rate, sems, *work):
     copies = [
         pltpu.make_async_copy(far_start.at[c, rows], start.at[c, rows], sems.at[c, k])
         for c in range(5)
@@ -78,52 +127,22 @@
             y_even[c, j] = jnp.where(upper, high, low)
             y_odd[c, j] = jnp.where(upper, low, high)
 
-
-def inner_kernel(speed, start, section_far, out, step, section, fluxes, smooths, sems):
-    copies = [
-        pltpu.make_async_copy(section_far.at[:, i], section.at[:, i], sems.at[i]) for i in range(8)
-    ]
-    for copy in copies:
-        copy.start()
-    rows = lax.broadcasted_iota(jnp.int32, (16, 256), 0)
-
-    def layer(i, carry):
-        pltpu.make_async_copy(section_far.at[:, i], section.at[:, i], sems.at[i]).wait()
-        q = [section[c, i] for c in range(5)]
-        inverse, velocity, kinetic, pressure = primitive(q)
-        g = smooth(inverse, velocity, kinetic, pressure)
-        fx = flux(q, velocity, pressure, 0)
-        fy = flux(q, velocity, pressure, 1)
-        fz = flux(q, velocity, pressure, 2)
-        for c in range(5):
-            fluxes[c, i] = fx[c]
-            total = jnp.zeros((16, 256), jnp.float32)
-            if c:
-                smooths[c - 1, i] = g[c]
-                total = (3.0 * CENTRE) * g[c]
-            for m in range(1, 5):
-                up, down = sides(fz[c], g[c], m)
-                total = total + pltpu.roll(up, 256 - m, 1) + pltpu.roll(down, m, 1)
-                up, down = sides(fy[c], g[c], m)
-                total = total + jnp.where(rows < 16 - m, pltpu.roll(up, 16 - m, 0), 0.0)
-                total = total + jnp.where(rows >= m, pltpu.roll(down, m, 0), 0.0)
-            out[c, i] = total
-        return carry
-
-    lax.fori_loop(0, 8, layer, 0)
-    factor = (0.25 * COURANT) / jnp.broadcast_to(speed[...], (8, 128))
-    step[...] = factor
-    factor = jnp.tile(factor, (2, 2))
-    for c in range(5):
-        for i in range(8):
-            total = out[c, i]
-            for m in range(1, 5):
-                for j, sign in ((i + m, -1.0), (i - m, 1.0)):
-                    if 0 <= j < 8:
-                        total = total + (sign * FIRST[m - 1]) * fluxes[c, j]
-                        if c:
-                            total = total + SECOND[m - 1] * smooths[c - 1, j]
-            out[c, i] = 0.75 * start[c, i] + 0.25 * section[c, i] + factor * total
+    @pl.when(early())
+    def _():
+        inner_work(start, section_far, start, rate, *work)
+
+
+def inner_kernel(speed, start, section_far, early_rate, step, base, rate, *work):
+    step[...] = (0.25 * COURANT) / jnp.broadcast_to(speed[...], (8, 128))
+
+    @pl.when(early())
+    def _():
+        base[...] = start[...]
+        rate[...] = early_rate[...]
+
+    @pl.when(jnp.logical_not(early()))
+    def _():
+        inner_work(start, section_far, base, rate, *work)
 
 
 def y_side(rim, sums, below):
@@ -177,7 +196,7 @@
     lax.fori_loop(0, 4, x_layer, 0)
 
 
-def rim_layer(t, x_below, y_below, inner, step, fluxes, smooths, sums):
+def rim_layer(t, x_below, y_below, base, rate, step, fluxes, smooths, sums):
     i = jnp.where(x_below == 1, t, 7 - t)
     factor = jnp.tile(step[...], (1, 2))
     low = jnp.where(y_below == 1, factor, 0.0)
@@ -186,8 +205,8 @@
     values = []
     for c in range(5):
         part = sums[c, i]
-        value = inner[c, i] + edge * jnp.concatenate([part, part], axis=0)
-        total = None
+        value = base[c, i] + edge * jnp.concatenate([part, part], axis=0)
+        total = None if rate is None else rate[c, i]
         for d in range(4 - t):
             term = FIRST[d + t] * fluxes[c, d]
             if c:
@@ -199,21 +218,21 @@
     return i, values
 
 
-def odd_kernel(inner, step, x_rim, y_rim, out, fluxes, smooths, sums):
+def odd_kernel(base, rate, step, x_rim, y_rim, out, fluxes, smooths, sums):
     x_below, y_below = 1 - odd("y"), 1 - odd("core")
     rim_terms(x_below, y_below, x_rim, y_rim, fluxes, smooths, sums)
     for t in range(8):
-        i, values = rim_layer(t, x_below, y_below, inner, step, fluxes, smooths, sums)
+        i, values = rim_layer(t, x_below, y_below, base, rate, step, fluxes, smooths, sums)
         for c in range(5):
             out[c, i] = values[c]
 
 
-def even_kernel(inner, step, x_rim, y_rim, out, peak, fluxes, smooths, sums):
+def even_kernel(base, step, x_rim, y_rim, out, peak, fluxes, smooths, sums):
     x_below, y_below = odd("y"), odd("core")
     rim_terms(x_below, y_below, x_rim, y_rim, fluxes, smooths, sums)
     most = None
     for t in range(8):
-        i, values = rim_layer(t, x_below, y_below, inner, step, fluxes, smooths, sums)
+        i, values = rim_layer(t, x_below, y_below, base, None, step, fluxes, smooths, sums)
         for c in range(5):
             out[c, i] = values[c]
         inverse, velocity, kinetic, pressure = primitive(values)
@@ -248,7 +267,7 @@
         out_specs=tuple(pl.BlockSpec(memory_space=out_space) for _ in outs),
         scratch_shapes=scratch,
         cost_estimate=estimate,
-        compiler_params=pltpu.CompilerParams(vmem_limit_bytes=24 << 20),
+        compiler_params=pltpu.CompilerParams(vmem_limit_bytes=8 << 20),
     )(*arrays)
 
 
@@ -263,41 +282,41 @@
 
 
 def local(start, section, previous_speed):
-    x_odd, y_odd, x_even, y_even = call(
+    state = in_vmem(5, 8, 16, 256)
+    work = [state, state, in_vmem(4, 8, 16, 256), pltpu.SemaphoreType.DMA((8,))]
+    x_odd, y_odd, x_even, y_even, start, rate = call(
         pack_kernel,
-        (in_vmem(5, 4, 16, 256), in_vmem(5, 4, 8, 256)) * 2,
-        [pltpu.HBM],
-        [in_vmem(5, 8, 16, 256), pltpu.SemaphoreType.DMA((5, 2))],
+        (in_vmem(5, 4, 16, 256), in_vmem(5, 4, 8, 256)) * 2 + (state,) * 2,
+        [pltpu.HBM] * 2,
+        [pltpu.SemaphoreType.DMA((5, 2))] + work,
         0,
         far(start),
+        far(section),
     )
     x_odd, y_odd = swap(x_odd, GX, 1), swap(y_odd, GY, 1)
     y_even, x_even = swap(y_even, GY, 0), swap(x_even, GX, 0)
-    state = in_vmem(5, 8, 16, 256)
-    inner, step = call(
+    step, base, rate = call(
         inner_kernel,
-        (state, in_vmem(8, 128)),
-        [VMEM, VMEM, pltpu.HBM],
-        [
-            state,
-            state,
-            in_vmem(4, 8, 16, 256),
-            pltpu.SemaphoreType.DMA((8,)),
-        ],
+        (in_vmem(8, 128), state, state),
+        [VMEM, VMEM, pltpu.HBM, VMEM],
+        work,
         INNER_COST,
         previous_speed.reshape(1, 1),
         start,
         far(section),
+        rate,
     )
     rims = [in_vmem(5, 4, 16, 256), in_vmem(4, 4, 16, 256), in_vmem(5, 8, 8, 256)]
-    (inner,) = call(odd_kernel, (state,), [VMEM] * 4, rims, ODD_COST, inner, step, x_odd, y_odd)
+    (base,) = call(
+        odd_kernel, (state,), [VMEM] * 5, rims, ODD_COST, base, rate, step, x_odd, y_odd
+    )
     new, peak = call(
         even_kernel,
         (state, in_vmem(lax.axis_size(NEAR), 128)),
         [VMEM] * 4,
         rims,
         EVEN_COST,
-        inner,
+        base,
         step,
         x_even,
         y_even,

time: 58.8 us -> 58.9 us (level)
  blocking collectives: 10.2 us -> 13.3 us
  starting transfers between devices: 30.8 us -> 27.8 us
    ppermute x4, starting transfers between devices: 25.7 us -> 22.2 us  [swap(): return lax.ppermute(x, axis, pairs + [(b, a) for a, b in pairs])]
    all_to_all x1, blocking collectives: 10.2 us -> 13.3 us  [local(): peaks = lax.all_to_all(peak, NEAR, 0, 0, tiled=True)]
  transfers between devices with their start and end apart: 5 -> 5, of which waited for: 1 -> 1; matrix products, arithmetic and copies ran while one was open for 1% -> 1% of each run, Pallas kernels for 7% -> 1%
where the time goes in v6:
time: 58.9 us; the launch traced here: 58.5 us
  starting transfers between devices  27.8 us (47%)
  blocking collectives  13.3 us (23%)
  waiting for transfers between devices  7.83 us (13%)
  Pallas kernels  6.87 us (12%)
  between operations  1.89 us (3%)
  local copies, waits for them, and re-layouts  0.84 us (1%)
    ppermute x4, starting transfers between devices, swap(): return lax.ppermute(x, axis, pairs + [(b, a) for a, b in pairs])  22.2 us
    all_to_all x1, blocking collectives, local(): peaks = lax.all_to_all(peak, NEAR, 0, 0, tiled=True)  13.3 us
    all_to_all x1, waiting for transfers between devices, local(): peaks = lax.all_to_all(peak, FAR, 0, 0, tiled=True)  7.82 us
    pallas_call x6, Pallas kernels, call(): pl.pallas_call(kernel, out_shape=outs, in_specs=[pl.BlockSpec(memory_spac...  6.87 us
    all_to_all x1, starting transfers between devices, local(): peaks = lax.all_to_all(peak, FAR, 0, 0, tiled=True)  5.53 us
  transfers between devices with their start and end apart: 5, of which 1 were waited for; matrix products, arithmetic and copies ran while one was open for 1% of the time, Pallas kernels for 1%

profile of v6, /device:TPU:1, one launch (start us, length us, event | category | flops | bytes accessed | tf_op | source)
XLA Modules:
  0.0 58.5 jit_solution(15351211893238555720)
XLA Ops:
  0.6 4.8 %shard_map.50 = (f32[5,4,16,256]{3,2,1,0:T(8,128)S(1)}, f32[5,4,8,256]{3,2,1,0:T(8,128)S(1)}, f32[5,4,16,256]{3,2,1,0:T(8,128)S(1)}, f32[5,4,8,256]{3,2,1,0:T(8,...) custom-call(f32[5,8,16,256]{3,2,1,0:T(8,128)} %far_start.1, f32[5,8,16,256]{3,2,1,0:T(8,128)} %section_far.3), custom_call_target="tpu_custom_call" | custom-call | tf_op jit(solution)/shard_map/pallas_call | solution.py:263
  5.4 7.9 %collective-permute-start = (f32[5,4,16,256]{3,2,1,0:T(8,128)S(1)}, f32[5,4,16,256]{3,2,1,0:T(8,128)S(1)}, u32[]{:S(2)}, u32[]{:S(2)}) collective-permute-start(f32[5,4,16,256]{3,2,1,0:T(8,128)S(1)} %get-tuple-element.18), channel_id=1, source_target_pairs={{16,32},{48,64},{80,96},{112,128},{144,160},{176,192},{208,224},{2... | collective-permute-start | bytes 983048 | tf_op jit(solution)/shard_map/ppermute | solution.py:281
  13.3 4.0 %collective-permute-start.1 = (f32[5,4,8,256]{3,2,1,0:T(8,128)S(1)}, f32[5,4,8,256]{3,2,1,0:T(8,128)S(1)}, u32[]{:S(2)}, u32[]{:S(2)}) collective-permute-start(f32[5,4,8,256]{3,2,1,0:T(8,128)S(1)} %get-tuple-element.19), channel_id=1, source_target_pairs={{1,2},{3,4},{5,6},{7,8},{9,10},{11,12},{13,14},{15,0},{2,1},{4,3},... | collective-permute-start | bytes 491528 | tf_op jit(solution)/shard_map/ppermute | solution.py:281
  17.3 1.9 %collective-permute-start.2 = (f32[5,4,16,256]{3,2,1,0:T(8,128)S(1)}, f32[5,4,16,256]{3,2,1,0:T(8,128)S(1)}, u32[]{:S(2)}, u32[]{:S(2)}) collective-permute-start(f32[5,4,16,256]{3,2,1,0:T(8,128)S(1)} %get-tuple-element.20), channel_id=1, source_target_pairs={{0,16},{32,48},{64,80},{96,112},{128,144},{160,176},{192,208},{224... | collective-permute-start | bytes 983048 | tf_op jit(solution)/shard_map/ppermute | solution.py:281
  19.2 8.5 %collective-permute-start.3 = (f32[5,4,8,256]{3,2,1,0:T(8,128)S(1)}, f32[5,4,8,256]{3,2,1,0:T(8,128)S(1)}, u32[]{:S(2)}, u32[]{:S(2)}) collective-permute-start(f32[5,4,8,256]{3,2,1,0:T(8,128)S(1)} %get-tuple-element.21), channel_id=1, source_target_pairs={{0,1},{2,3},{4,5},{6,7},{8,9},{10,11},{12,13},{14,15},{1,0},{3,2},... | collective-permute-start | bytes 491528 | tf_op jit(solution)/shard_map/ppermute | solution.py:281
  28.3 0.2 shard_map.51
  28.5 0.0 collective-permute-done.1.y_rim
  28.5 0.0 collective-permute-done.x_rim
  28.5 0.6 shard_map.52.base
  29.1 0.0 collective-permute-done.3.y_rim
  29.1 0.0 collective-permute-done.2.x_rim
  29.1 0.6 %shard_map.53 = (f32[5,8,16,256]{3,2,1,0:T(8,128)S(1)}, f32[16,128]{1,0:T(8,128)S(1)}) custom-call(f32[5,8,16,256]{3,2,1,0:T(8,128)S(1)} %shard_map.52.base, f32[8,128]{1,0:T(8,128)S(1)} %get-tuple-element.17.step, f32[5,4,16,256]{3,2,1,0:T(8,128)S(1)} %collective-permute-done.2.x_rim, f32[5,4,8,256]{3,2,1,0:T(8,128)S(1)} %collective-permute-done.3.y_rim), custom_call_target="tpu_custom_call" | custom-call | flops 314572800 | bytes 1048576 | tf_op jit(solution)/shard_map/pallas_call | solution.py:263
  29.8 13.3 %all_to_all.22 = f32[16,1,128]{2,1,0:T(1,128)S(1)} all-to-all(f32[16,1,128]{2,1,0:T(1,128)S(1)} %bitcast.13), channel_id=1, replica_groups=mesh['z_lo'=4,'y'=8,'z_hi'=2,'x'=4,'core'=2] {'y','core'}, dimensions={0} | all-to-all | bytes 16384 | tf_op jit(solution)/shard_map/all_to_all | solution.py:324
  43.0 0.6 %shard_map.54 = f32[32,128]{1,0:T(8,128)} custom-call(f32[16,128]{1,0:T(8,128)S(1)} %bitcast.12), custom_call_target="tpu_custom_call" | custom-call | tf_op jit(solution)/shard_map/pallas_call | solution.py:263
  43.6 5.5 %all-to-all-start.1 = ((f32[32,1,128]{2,1,0:T(1,128)}), f32[32,1,128]{2,1,0:T(1,128)S(1)}, u32[]{:S(2)}, u32[]{:S(2)}) async-start(f32[32,1,128]{2,1,0:T(1,128)} %bitcast.5), calls=%async_computation.1 | async-start | bytes 32768 | tf_op jit(solution)/shard_map/all_to_all | solution.py:326
  49.2 0.8 %copy.7 = f32[5,8,16,256]{3,2,1,0:T(8,128)} copy(f32[5,8,16,256]{3,2,1,0:T(8,128)S(1)} %get-tuple-element.24) | data formatting | bytes 1310720
  50.0 7.8 %all-to-all-done.1 = f32[32,1,128]{2,1,0:T(1,128)S(1)} async-done(((f32[32,1,128]{2,1,0:T(1,128)}), f32[32,1,128]{2,1,0:T(1,128)S(1)}, u32[]{:S(2)}, u32[]{:S(2)}) %all-to-all-start.1) | async-done | bytes 16416 | tf_op jit(solution)/shard_map/all_to_all | solution.py:326
  57.8 0.1 shard_map.55
Async XLA Ops:
  5.4 23.1 %collective-permute-start = (f32[5,4,16,256]{3,2,1,0:T(8,128)S(1)}, f32[5,4,16,256]{3,2,1,0:T(8,128)S(1)}, u32[]{:S(2)}, u32[]{:S(2)}) collective-permute-start(f32[5,4,16,256]{3,2,1,0:T(8,128)S(1)} %get-tuple-element.18), channel_id=1, source_target_pairs={{16,32},{48,64},{80,96},{112,128},{144,160},{176,192},{208,224},{2... | collective-permute-start | bytes 983048 | tf_op jit(solution)/shard_map/ppermute | solution.py:281
  13.3 15.2 %collective-permute-start.1 = (f32[5,4,8,256]{3,2,1,0:T(8,128)S(1)}, f32[5,4,8,256]{3,2,1,0:T(8,128)S(1)}, u32[]{:S(2)}, u32[]{:S(2)}) collective-permute-start(f32[5,4,8,256]{3,2,1,0:T(8,128)S(1)} %get-tuple-element.19), channel_id=1, source_target_pairs={{1,2},{3,4},{5,6},{7,8},{9,10},{11,12},{13,14},{15,0},{2,1},{4,3},... | collective-permute-start | bytes 491528 | tf_op jit(solution)/shard_map/ppermute | solution.py:281
  17.3 11.9 %collective-permute-start.2 = (f32[5,4,16,256]{3,2,1,0:T(8,128)S(1)}, f32[5,4,16,256]{3,2,1,0:T(8,128)S(1)}, u32[]{:S(2)}, u32[]{:S(2)}) collective-permute-start(f32[5,4,16,256]{3,2,1,0:T(8,128)S(1)} %get-tuple-element.20), channel_id=1, source_target_pairs={{0,16},{32,48},{64,80},{96,112},{128,144},{160,176},{192,208},{224... | collective-permute-start | bytes 983048 | tf_op jit(solution)/shard_map/ppermute | solution.py:281
  19.2 9.9 %collective-permute-start.3 = (f32[5,4,8,256]{3,2,1,0:T(8,128)S(1)}, f32[5,4,8,256]{3,2,1,0:T(8,128)S(1)}, u32[]{:S(2)}, u32[]{:S(2)}) collective-permute-start(f32[5,4,8,256]{3,2,1,0:T(8,128)S(1)} %get-tuple-element.21), channel_id=1, source_target_pairs={{0,1},{2,3},{4,5},{6,7},{8,9},{10,11},{12,13},{14,15},{1,0},{3,2},... | collective-permute-start | bytes 491528 | tf_op jit(solution)/shard_map/ppermute | solution.py:281
  43.6 14.2 %all-to-all-start.1 = ((f32[32,1,128]{2,1,0:T(1,128)}), f32[32,1,128]{2,1,0:T(1,128)S(1)}, u32[]{:S(2)}, u32[]{:S(2)}) async-start(f32[32,1,128]{2,1,0:T(1,128)} %bitcast.5), calls=%async_computation.1 | async-start | bytes 32768 | tf_op jit(solution)/shard_map/all_to_all | solution.py:326

commit v7 on v6

--- a/solution.py
+++ b/solution.py
@@ -19,7 +19,8 @@
 NEAR, FAR = ("y", "core"), ("z_lo", "z_hi", "x")
 VMEM = pltpu.VMEM
 SMEM = pltpu.SMEM
-INNER_COST, ODD_COST, EVEN_COST = 1 << 20, 8 << 20, 1 << 20
+INNER_COST, ODD_COST, EVEN_COST = 1 << 20, 1 << 18, 1 << 20
+Y_COST = 7 << 20
 
 
 def primitive(q):
@@ -170,19 +171,11 @@
     lax.fori_loop(0, 4, pair, 0)
 
 
-def rim_terms(x_below, y_below, x_rim, y_rim, fluxes, smooths, sums):
-    @pl.when(y_below == 1)
-    def _():
-        y_side(y_rim, sums, True)
-
-    @pl.when(y_below == 0)
-    def _():
-        y_side(y_rim, sums, False)
-
-    sign = jnp.where(x_below == 1, 1.0, -1.0)
-
-    def x_layer(d, carry):
-        i = jnp.where(x_below == 1, 3 - d, d)
+def x_side(x_rim, below, fluxes, smooths):
+    sign = jnp.where(below == 1, 1.0, -1.0)
+
+    def layer(d, carry):
+        i = jnp.where(below == 1, 3 - d, d)
         q = [x_rim[c, i] for c in range(5)]
         inverse, velocity, kinetic, pressure = primitive(q)
         g = smooth(inverse, velocity, kinetic, pressure)
@@ -193,53 +186,82 @@
                 smooths[c - 1, d] = g[c]
         return carry
 
-    lax.fori_loop(0, 4, x_layer, 0)
-
-
-def rim_layer(t, x_below, y_below, base, rate, step, fluxes, smooths, sums):
-    i = jnp.where(x_below == 1, t, 7 - t)
-    factor = jnp.tile(step[...], (1, 2))
-    low = jnp.where(y_below == 1, factor, 0.0)
-    edge = jnp.concatenate([low, factor - low], axis=0)
-    factor = jnp.concatenate([factor, factor], axis=0)
-    values = []
-    for c in range(5):
-        part = sums[c, i]
-        value = base[c, i] + edge * jnp.concatenate([part, part], axis=0)
-        total = None if rate is None else rate[c, i]
-        for d in range(4 - t):
-            term = FIRST[d + t] * fluxes[c, d]
-            if c:
-                term = term + SECOND[d + t] * smooths[c - 1, d]
-            total = term if total is None else total + term
-        if total is not None:
-            value = value + factor * total
-        values.append(value)
-    return i, values
-
-
-def odd_kernel(base, rate, step, x_rim, y_rim, out, fluxes, smooths, sums):
-    x_below, y_below = 1 - odd("y"), 1 - odd("core")
-    rim_terms(x_below, y_below, x_rim, y_rim, fluxes, smooths, sums)
-    for t in range(8):
-        i, values = rim_layer(t, x_below, y_below, base, rate, step, fluxes, smooths, sums)
-        for c in range(5):
-            out[c, i] = values[c]
-
-
-def even_kernel(base, step, x_rim, y_rim, out, peak, fluxes, smooths, sums):
-    x_below, y_below = odd("y"), odd("core")
-    rim_terms(x_below, y_below, x_rim, y_rim, fluxes, smooths, sums)
+    lax.fori_loop(0, 4, layer, 0)
+
+
+def finish(below, base, rate, step, fluxes, smooths, new, out, sems):
+    factor = jnp.tile(step[...], (2, 2))
     most = None
-    for t in range(8):
-        i, values = rim_layer(t, x_below, y_below, base, None, step, fluxes, smooths, sums)
-        for c in range(5):
-            out[c, i] = values[c]
+    copies = []
+    for t in range(4):
+        i = jnp.where(below == 1, t, 7 - t)
+        values = []
+        for c in range(5):
+            total = None if rate is None else rate[c, i]
+            for d in range(4 - t):
+                term = FIRST[d + t] * fluxes[c, d]
+                if c:
+                    term = term + SECOND[d + t] * smooths[c - 1, d]
+                total = term if total is None else total + term
+            value = base[c, i] + factor * total
+            new[c, t] = value
+            values.append(value)
+        copy = pltpu.make_async_copy(new.at[:, t], out.at[:, i], sems.at[t])
+        copy.start()
+        copies.append(copy)
         inverse, velocity, kinetic, pressure = primitive(values)
         speed = jnp.sqrt(2.0 * kinetic) + jnp.sqrt(GAMMA * pressure * inverse)
         most = speed if most is None else jnp.maximum(most, speed)
     most = jnp.maximum(most[:, :128], most[:, 128:])
-    spread(most, peak)
+    return copies, jnp.maximum(most[:8], most[8:])
+
+
+def one_side(rim, below, sums):
+    for side, rows, others in ((1, pl.ds(0, 8), pl.ds(8, 8)), (0, pl.ds(8, 8), pl.ds(0, 8))):
+
+        @pl.when(below == side)
+        def _(side=side, rows=rows, others=others):
+            y_side(rim, sums.at[:, :, rows], side == 1)
+            sums[:, :, others] = jnp.zeros((5, 8, 8, 256), jnp.float32)
+
+
+def y_kernel(rate, rim, out, sums):
+    one_side(rim, 1 - odd("core"), sums)
+    out[...] = rate[...] + sums[...]
+
+
+def odd_kernel(base, rate, step, x_rim, y_even, out, rest, most, fluxes, smooths, sums, new, sems):
+    below = 1 - odd("y")
+    one_side(y_even, odd("core"), sums)
+    factor = jnp.tile(step[...], (2, 2))
+
+    def layer(t, carry):
+        i = jnp.where(below == 1, 7 - t, t)
+        for c in range(5):
+            rest[c, i] = base[c, i] + factor * (rate[c, i] + sums[c, i])
+        return carry
+
+    def edge(t, carry):
+        i = jnp.where(below == 1, t, 7 - t)
+        for c in range(5):
+            sums[c, i] = sums[c, i] + rate[c, i]
+        return carry
+
+    x_side(x_rim, below, fluxes, smooths)
+    lax.fori_loop(0, 4, edge, 0)
+    copies, most[...] = finish(below, base, sums, step, fluxes, smooths, new, out, sems)
+    lax.fori_loop(0, 4, layer, 0)
+    for copy in copies:
+        copy.wait()
+
+
+def even_kernel(rest, step, most, x_rim, half, out, peak, fluxes, smooths, new, sems):
+    below = odd("y")
+    x_side(x_rim, below, fluxes, smooths)
+    copies, mine = finish(below, rest, None, step, fluxes, smooths, new, out, sems)
+    spread(jnp.maximum(mine, most[...]), peak)
+    for copy in copies:
+        copy.wait()
 
 
 def spread(values, out):
@@ -258,15 +280,16 @@
     return VMEM(sizes, jnp.float32)
 
 
-def call(kernel, outs, in_specs, scratch, cost, *arrays, out_space=VMEM):
+def call(kernel, outs, in_specs, scratch, cost, *arrays, out_specs=None, aliases=None):
     estimate = pl.CostEstimate(flops=cost * 300, bytes_accessed=cost, transcendentals=0) if cost else None
     return pl.pallas_call(
         kernel,
         out_shape=outs,
         in_specs=[pl.BlockSpec(memory_space=m) for m in in_specs],
-        out_specs=tuple(pl.BlockSpec(memory_space=out_space) for _ in outs),
+        out_specs=tuple(pl.BlockSpec(memory_space=m) for m in out_specs or (VMEM,) * len(outs)),
         scratch_shapes=scratch,
         cost_estimate=estimate,
+        input_output_aliases=aliases or {},
         compiler_params=pltpu.CompilerParams(vmem_limit_bytes=8 << 20),
     )(*arrays)
 
@@ -306,26 +329,42 @@
         far(section),
         rate,
     )
-    rims = [in_vmem(5, 4, 16, 256), in_vmem(4, 4, 16, 256), in_vmem(5, 8, 8, 256)]
-    (base,) = call(
-        odd_kernel, (state,), [VMEM] * 5, rims, ODD_COST, base, rate, step, x_odd, y_odd
+    rims = [in_vmem(5, 4, 16, 256), in_vmem(4, 4, 16, 256)]
+    outgoing = [in_vmem(5, 4, 16, 256), pltpu.SemaphoreType.DMA((4,))]
+    far_state = pltpu.HBM((5, 8, 16, 256), jnp.float32)
+    (rate,) = call(y_kernel, (state,), [VMEM] * 2, [state], Y_COST, rate, y_odd)
+    half, rest, most = call(
+        odd_kernel,
+        (far_state, state, in_vmem(8, 128)),
+        [VMEM] * 5,
+        rims + [state] + outgoing,
+        ODD_COST,
+        base,
+        rate,
+        step,
+        x_odd,
+        y_even,
+        out_specs=(pltpu.HBM, VMEM, VMEM),
     )
     new, peak = call(
         even_kernel,
-        (state, in_vmem(lax.axis_size(NEAR), 128)),
-        [VMEM] * 4,
-        rims,
+        (far_state, in_vmem(lax.axis_size(NEAR), 128)),
+        [VMEM] * 4 + [pltpu.HBM],
+        rims + outgoing,
         EVEN_COST,
-        base,
+        rest,
         step,
+        most,
         x_even,
-        y_even,
+        half,
+        out_specs=(pltpu.HBM, VMEM),
+        aliases={4: 0},
     )
     peaks = lax.all_to_all(peak, NEAR, 0, 0, tiled=True)
     (peak,) = call(pass_kernel, (in_vmem(lax.axis_size(FAR), 128),), [VMEM], [], 0, peaks)
     peaks = lax.all_to_all(peak, FAR, 0, 0, tiled=True)
     (most,) = call(
-        most_kernel, (SMEM((1,), jnp.float32),), [VMEM], [], 0, peaks, out_space=SMEM
+        most_kernel, (SMEM((1,), jnp.float32),), [VMEM], [], 0, peaks, out_specs=(SMEM,)
     )
     return new, most.reshape(())
 

time: 58.9 us -> 60.2 us (1.022)
  blocking collectives: 13.3 us -> 27.7 us
  waiting for transfers between devices: 7.83 us -> 0.01 us
  starting transfers between devices: 27.8 us -> 22.5 us
  local copies, waits for them, and re-layouts: 0.84 us -> 0 us
  Pallas kernels: 6.87 us -> 7.62 us
    all_to_all x0 -> x1, blocking collectives: none -> 13.4 us  [local(): peaks = lax.all_to_all(peak, FAR, 0, 0, tiled=True)]
    all_to_all x1 -> x0, waiting for transfers between devices: 7.82 us -> none  [local(): peaks = lax.all_to_all(peak, FAR, 0, 0, tiled=True)]
    all_to_all x1 -> x0, starting transfers between devices: 5.53 us -> none  [local(): peaks = lax.all_to_all(peak, FAR, 0, 0, tiled=True)]
    all_to_all x1, blocking collectives: 13.3 us -> 14.3 us  [local(): peaks = lax.all_to_all(peak, NEAR, 0, 0, tiled=True)]
    unnamed x1 -> x0, local copies, waits for them, and re-layouts: 0.84 us -> none
    pallas_call x6 -> x7, Pallas kernels: 6.87 us -> 7.62 us  [call(): pl.pallas_call(kernel, out_shape=outs, in_specs=[pl.BlockSpec(memory_spac...]
  transfers between devices with their start and end apart: 5 -> 4, of which waited for: 1 -> 0; matrix products, arithmetic and copies ran while one was open for 1% -> 0% of each run, Pallas kernels for 1% -> 3%
where the time goes in v7:
time: 60.2 us; the launch traced here: 59.8 us
  blocking collectives  27.7 us (46%)
  starting transfers between devices  22.5 us (37%)
  Pallas kernels  7.62 us (13%)
  between operations  1.9 us (3%)
    ppermute x4, starting transfers between devices, swap(): return lax.ppermute(x, axis, pairs + [(b, a) for a, b in pairs])  22.5 us
    all_to_all x1, blocking collectives, local(): peaks = lax.all_to_all(peak, NEAR, 0, 0, tiled=True)  14.3 us
    all_to_all x1, blocking collectives, local(): peaks = lax.all_to_all(peak, FAR, 0, 0, tiled=True)  13.4 us
    pallas_call x7, Pallas kernels, call(): pl.pallas_call(kernel, out_shape=outs, in_specs=[pl.BlockSpec(memory_spac...  7.62 us
  transfers between devices with their start and end apart: 4, of which 0 were waited for; matrix products, arithmetic and copies ran while one was open for 0% of the time, Pallas kernels for 3%

profile of v7, /device:TPU:1, one launch (start us, length us, event | category | flops | bytes accessed | tf_op | source)
XLA Modules:
  0.0 59.8 jit_solution(3696621712739542557)
XLA Ops:
  0.6 4.8 %shard_map.50 = (f32[5,4,16,256]{3,2,1,0:T(8,128)S(1)}, f32[5,4,8,256]{3,2,1,0:T(8,128)S(1)}, f32[5,4,16,256]{3,2,1,0:T(8,128)S(1)}, f32[5,4,8,256]{3,2,1,0:T(8,...) custom-call(f32[5,8,16,256]{3,2,1,0:T(8,128)} %far_start.1, f32[5,8,16,256]{3,2,1,0:T(8,128)} %section_far.3), custom_call_target="tpu_custom_call" | custom-call | tf_op jit(solution)/shard_map/pallas_call | solution.py:285
  5.4 4.5 %collective-permute-start = (f32[5,4,8,256]{3,2,1,0:T(8,128)S(1)}, f32[5,4,8,256]{3,2,1,0:T(8,128)S(1)}, u32[]{:S(2)}, u32[]{:S(2)}) collective-permute-start(f32[5,4,8,256]{3,2,1,0:T(8,128)S(1)} %get-tuple-element.20), channel_id=1, source_target_pairs={{1,2},{3,4},{5,6},{7,8},{9,10},{11,12},{13,14},{15,0},{2,1},{4,3},... | collective-permute-start | bytes 491528 | tf_op jit(solution)/shard_map/ppermute | solution.py:304
  9.9 7.1 %collective-permute-start.1 = (f32[5,4,16,256]{3,2,1,0:T(8,128)S(1)}, f32[5,4,16,256]{3,2,1,0:T(8,128)S(1)}, u32[]{:S(2)}, u32[]{:S(2)}) collective-permute-start(f32[5,4,16,256]{3,2,1,0:T(8,128)S(1)} %get-tuple-element.22), channel_id=1, source_target_pairs={{16,32},{48,64},{80,96},{112,128},{144,160},{176,192},{208,224},{2... | collective-permute-start | bytes 983048 | tf_op jit(solution)/shard_map/ppermute | solution.py:304
  17.0 1.9 %collective-permute-start.3 = (f32[5,4,16,256]{3,2,1,0:T(8,128)S(1)}, f32[5,4,16,256]{3,2,1,0:T(8,128)S(1)}, u32[]{:S(2)}, u32[]{:S(2)}) collective-permute-start(f32[5,4,16,256]{3,2,1,0:T(8,128)S(1)} %get-tuple-element.26), channel_id=1, source_target_pairs={{0,16},{32,48},{64,80},{96,112},{128,144},{160,176},{192,208},{224... | collective-permute-start | bytes 983048 | tf_op jit(solution)/shard_map/ppermute | solution.py:304
  18.9 9.0 %collective-permute-start.2 = (f32[5,4,8,256]{3,2,1,0:T(8,128)S(1)}, f32[5,4,8,256]{3,2,1,0:T(8,128)S(1)}, u32[]{:S(2)}, u32[]{:S(2)}) collective-permute-start(f32[5,4,8,256]{3,2,1,0:T(8,128)S(1)} %get-tuple-element.23), channel_id=1, source_target_pairs={{0,1},{2,3},{4,5},{6,7},{8,9},{10,11},{12,13},{14,15},{1,0},{3,2},... | collective-permute-start | bytes 491528 | tf_op jit(solution)/shard_map/ppermute | solution.py:304
  28.6 0.2 shard_map.51
  28.8 0.0 collective-permute-done.rim
  28.8 0.3 shard_map.52.rate
  29.1 0.0 collective-permute-done.2.y_even
  29.1 0.0 collective-permute-done.1.x_rim
  29.1 1.3 %shard_map.53 = (f32[5,8,16,256]{3,2,1,0:T(8,128)}, f32[5,8,16,256]{3,2,1,0:T(8,128)S(1)}, f32[8,128]{1,0:T(8,128)S(1)}) custom-call(f32[5,8,16,256]{3,2,1,0:T(8,128)S(1)} %get-tuple-element.18.base, f32[5,8,16,256]{3,2,1,0:T(8,128)S(1)} %shard_map.52.rate, f32[8,128]{1,0:T(8,128)S(1)} %get-tuple-element.21.step, ...), custom_call_target="tpu_custom_call" | custom-call | flops 78643200 | bytes 262144 | tf_op jit(solution)/shard_map/pallas_call | solution.py:285
  30.4 0.0 collective-permute-done.3.x_rim
  30.4 1.0 %shard_map.54 = (f32[5,8,16,256]{3,2,1,0:T(8,128)}, f32[16,128]{1,0:T(8,128)S(1)}) custom-call(f32[5,8,16,256]{3,2,1,0:T(8,128)S(1)} %get-tuple-element.24.rest, f32[8,128]{1,0:T(8,128)S(1)} %get-tuple-element.21.step, f32[8,128]{1,0:T(8,128)S(1)} %get-tuple-element.25.most, ...), custom_call_target="tpu_custom_call", output_to_operand_aliasing={{0}: (4, {})} | custom-call | flops 314572800 | bytes 1048576 | tf_op jit(solution)/shard_map/pallas_call | solution.py:285
  31.4 14.3 %all_to_all.22 = f32[16,1,128]{2,1,0:T(1,128)S(1)} all-to-all(f32[16,1,128]{2,1,0:T(1,128)S(1)} %bitcast.14), channel_id=1, replica_groups=mesh['z_lo'=4,'y'=8,'z_hi'=2,'x'=4,'core'=2] {'y','core'}, dimensions={0} | all-to-all | bytes 16384 | tf_op jit(solution)/shard_map/all_to_all | solution.py:363
  45.7 13.4 %all_to_all.23 = f32[32,1,128]{2,1,0:T(1,128)S(1)} all-to-all(f32[32,1,128]{2,1,0:T(1,128)S(1)} %bitcast.11), channel_id=1, replica_groups=mesh['z_lo'=4,'y'=8,'z_hi'=2,'x'=4,'core'=2] {'z_lo','z_hi','x'}, dimensions={0} | all-to-all | bytes 32768 | tf_op jit(solution)/shard_map/all_to_all | solution.py:365
  59.1 0.1 shard_map.56
  (1 shorter events, 0.0 us)
Async XLA Ops:
  5.4 23.4 %collective-permute-start = (f32[5,4,8,256]{3,2,1,0:T(8,128)S(1)}, f32[5,4,8,256]{3,2,1,0:T(8,128)S(1)}, u32[]{:S(2)}, u32[]{:S(2)}) collective-permute-start(f32[5,4,8,256]{3,2,1,0:T(8,128)S(1)} %get-tuple-element.20), channel_id=1, source_target_pairs={{1,2},{3,4},{5,6},{7,8},{9,10},{11,12},{13,14},{15,0},{2,1},{4,3},... | collective-permute-start | bytes 491528 | tf_op jit(solution)/shard_map/ppermute | solution.py:304
  9.9 19.2 %collective-permute-start.1 = (f32[5,4,16,256]{3,2,1,0:T(8,128)S(1)}, f32[5,4,16,256]{3,2,1,0:T(8,128)S(1)}, u32[]{:S(2)}, u32[]{:S(2)}) collective-permute-start(f32[5,4,16,256]{3,2,1,0:T(8,128)S(1)} %get-tuple-element.22), channel_id=1, source_target_pairs={{16,32},{48,64},{80,96},{112,128},{144,160},{176,192},{208,224},{2... | collective-permute-start | bytes 983048 | tf_op jit(solution)/shard_map/ppermute | solution.py:304
  17.0 13.4 %collective-permute-start.3 = (f32[5,4,16,256]{3,2,1,0:T(8,128)S(1)}, f32[5,4,16,256]{3,2,1,0:T(8,128)S(1)}, u32[]{:S(2)}, u32[]{:S(2)}) collective-permute-start(f32[5,4,16,256]{3,2,1,0:T(8,128)S(1)} %get-tuple-element.26), channel_id=1, source_target_pairs={{0,16},{32,48},{64,80},{96,112},{128,144},{160,176},{192,208},{224... | collective-permute-start | bytes 983048 | tf_op jit(solution)/shard_map/ppermute | solution.py:304
  18.9 10.2 %collective-permute-start.2 = (f32[5,4,8,256]{3,2,1,0:T(8,128)S(1)}, f32[5,4,8,256]{3,2,1,0:T(8,128)S(1)}, u32[]{:S(2)}, u32[]{:S(2)}) collective-permute-start(f32[5,4,8,256]{3,2,1,0:T(8,128)S(1)} %get-tuple-element.23), channel_id=1, source_target_pairs={{0,1},{2,3},{4,5},{6,7},{8,9},{10,11},{12,13},{14,15},{1,0},{3,2},... | collective-permute-start | bytes 491528 | tf_op jit(solution)/shard_map/ppermute | solution.py:304

commit v8 on v7

--- a/solution.py
+++ b/solution.py
@@ -19,8 +19,8 @@
 NEAR, FAR = ("y", "core"), ("z_lo", "z_hi", "x")
 VMEM = pltpu.VMEM
 SMEM = pltpu.SMEM
-INNER_COST, ODD_COST, EVEN_COST = 1 << 20, 1 << 18, 1 << 20
-Y_COST = 7 << 20
+INNER_COST, ODD_COST, EVEN_COST = 1 << 20, 3 << 20, 1 << 20
+Y_COST = 4 << 20
 
 
 def primitive(q):

time: 60.2 us -> 59.2 us (0.983)
    all_to_all x1, blocking collectives: 14.3 us -> 13.3 us  [local(): peaks = lax.all_to_all(peak, NEAR, 0, 0, tiled=True)]
where the time goes in v8:
time: 59.2 us; the launch traced here: 58.9 us
  blocking collectives  27.1 us (46%)
  starting transfers between devices  22.2 us (38%)
  Pallas kernels  7.62 us (13%)
  between operations  1.9 us (3%)
    ppermute x4, starting transfers between devices, swap(): return lax.ppermute(x, axis, pairs + [(b, a) for a, b in pairs])  22.2 us
    all_to_all x1, blocking collectives, local(): peaks = lax.all_to_all(peak, FAR, 0, 0, tiled=True)  13.8 us
    all_to_all x1, blocking collectives, local(): peaks = lax.all_to_all(peak, NEAR, 0, 0, tiled=True)  13.3 us
    pallas_call x7, Pallas kernels, call(): pl.pallas_call(kernel, out_shape=outs, in_specs=[pl.BlockSpec(memory_spac...  7.62 us
  transfers between devices with their start and end apart: 4, of which 0 were waited for; matrix products, arithmetic and copies ran while one was open for 0% of the time, Pallas kernels for 3%

profile of v8, /device:TPU:1, one launch (start us, length us, event | category | flops | bytes accessed | tf_op | source)
XLA Modules:
  0.0 58.9 jit_solution(17426482658823248277)
XLA Ops:
  0.6 4.8 %shard_map.50 = (f32[5,4,16,256]{3,2,1,0:T(8,128)S(1)}, f32[5,4,8,256]{3,2,1,0:T(8,128)S(1)}, f32[5,4,16,256]{3,2,1,0:T(8,128)S(1)}, f32[5,4,8,256]{3,2,1,0:T(8,...) custom-call(f32[5,8,16,256]{3,2,1,0:T(8,128)} %far_start.1, f32[5,8,16,256]{3,2,1,0:T(8,128)} %section_far.3), custom_call_target="tpu_custom_call" | custom-call | tf_op jit(solution)/shard_map/pallas_call | solution.py:285
  5.4 7.9 %collective-permute-start.1 = (f32[5,4,16,256]{3,2,1,0:T(8,128)S(1)}, f32[5,4,16,256]{3,2,1,0:T(8,128)S(1)}, u32[]{:S(2)}, u32[]{:S(2)}) collective-permute-start(f32[5,4,16,256]{3,2,1,0:T(8,128)S(1)} %get-tuple-element.22), channel_id=1, source_target_pairs={{16,32},{48,64},{80,96},{112,128},{144,160},{176,192},{208,224},{2... | collective-permute-start | bytes 983048 | tf_op jit(solution)/shard_map/ppermute | solution.py:304
  13.3 4.0 %collective-permute-start = (f32[5,4,8,256]{3,2,1,0:T(8,128)S(1)}, f32[5,4,8,256]{3,2,1,0:T(8,128)S(1)}, u32[]{:S(2)}, u32[]{:S(2)}) collective-permute-start(f32[5,4,8,256]{3,2,1,0:T(8,128)S(1)} %get-tuple-element.20), channel_id=1, source_target_pairs={{1,2},{3,4},{5,6},{7,8},{9,10},{11,12},{13,14},{15,0},{2,1},{4,3},... | collective-permute-start | bytes 491528 | tf_op jit(solution)/shard_map/ppermute | solution.py:304
  17.3 1.9 %collective-permute-start.3 = (f32[5,4,16,256]{3,2,1,0:T(8,128)S(1)}, f32[5,4,16,256]{3,2,1,0:T(8,128)S(1)}, u32[]{:S(2)}, u32[]{:S(2)}) collective-permute-start(f32[5,4,16,256]{3,2,1,0:T(8,128)S(1)} %get-tuple-element.26), channel_id=1, source_target_pairs={{0,16},{32,48},{64,80},{96,112},{128,144},{160,176},{192,208},{224... | collective-permute-start | bytes 983048 | tf_op jit(solution)/shard_map/ppermute | solution.py:304
  19.2 8.5 %collective-permute-start.2 = (f32[5,4,8,256]{3,2,1,0:T(8,128)S(1)}, f32[5,4,8,256]{3,2,1,0:T(8,128)S(1)}, u32[]{:S(2)}, u32[]{:S(2)}) collective-permute-start(f32[5,4,8,256]{3,2,1,0:T(8,128)S(1)} %get-tuple-element.23), channel_id=1, source_target_pairs={{0,1},{2,3},{4,5},{6,7},{8,9},{10,11},{12,13},{14,15},{1,0},{3,2},... | collective-permute-start | bytes 491528 | tf_op jit(solution)/shard_map/ppermute | solution.py:304
  28.3 0.2 shard_map.51
  28.5 0.0 collective-permute-done.rim
  28.5 0.3 shard_map.52.rate
  28.8 0.0 collective-permute-done.2.y_even
  28.9 0.0 collective-permute-done.1.x_rim
  28.9 1.3 %shard_map.53 = (f32[5,8,16,256]{3,2,1,0:T(8,128)}, f32[5,8,16,256]{3,2,1,0:T(8,128)S(1)}, f32[8,128]{1,0:T(8,128)S(1)}) custom-call(f32[5,8,16,256]{3,2,1,0:T(8,128)S(1)} %get-tuple-element.18.base, f32[5,8,16,256]{3,2,1,0:T(8,128)S(1)} %shard_map.52.rate, f32[8,128]{1,0:T(8,128)S(1)} %get-tuple-element.21.step, ...), custom_call_target="tpu_custom_call" | custom-call | flops 943718400 | bytes 3145728 | tf_op jit(solution)/shard_map/pallas_call | solution.py:285
  30.1 0.0 collective-permute-done.3.x_rim
  30.2 1.0 %shard_map.54 = (f32[5,8,16,256]{3,2,1,0:T(8,128)}, f32[16,128]{1,0:T(8,128)S(1)}) custom-call(f32[5,8,16,256]{3,2,1,0:T(8,128)S(1)} %get-tuple-element.24.rest, f32[8,128]{1,0:T(8,128)S(1)} %get-tuple-element.21.step, f32[8,128]{1,0:T(8,128)S(1)} %get-tuple-element.25.most, ...), custom_call_target="tpu_custom_call", output_to_operand_aliasing={{0}: (4, {})} | custom-call | flops 314572800 | bytes 1048576 | tf_op jit(solution)/shard_map/pallas_call | solution.py:285
  31.1 13.3 %all_to_all.22 = f32[16,1,128]{2,1,0:T(1,128)S(1)} all-to-all(f32[16,1,128]{2,1,0:T(1,128)S(1)} %bitcast.14), channel_id=1, replica_groups=mesh['z_lo'=4,'y'=8,'z_hi'=2,'x'=4,'core'=2] {'y','core'}, dimensions={0} | all-to-all | bytes 16384 | tf_op jit(solution)/shard_map/all_to_all | solution.py:363
  44.4 13.8 %all_to_all.23 = f32[32,1,128]{2,1,0:T(1,128)S(1)} all-to-all(f32[32,1,128]{2,1,0:T(1,128)S(1)} %bitcast.11), channel_id=1, replica_groups=mesh['z_lo'=4,'y'=8,'z_hi'=2,'x'=4,'core'=2] {'z_lo','z_hi','x'}, dimensions={0} | all-to-all | bytes 32768 | tf_op jit(solution)/shard_map/all_to_all | solution.py:365
  58.2 0.1 shard_map.56
  (1 shorter events, 0.0 us)
Async XLA Ops:
  5.4 23.5 %collective-permute-start.1 = (f32[5,4,16,256]{3,2,1,0:T(8,128)S(1)}, f32[5,4,16,256]{3,2,1,0:T(8,128)S(1)}, u32[]{:S(2)}, u32[]{:S(2)}) collective-permute-start(f32[5,4,16,256]{3,2,1,0:T(8,128)S(1)} %get-tuple-element.22), channel_id=1, source_target_pairs={{16,32},{48,64},{80,96},{112,128},{144,160},{176,192},{208,224},{2... | collective-permute-start | bytes 983048 | tf_op jit(solution)/shard_map/ppermute | solution.py:304
  13.3 15.2 %collective-permute-start = (f32[5,4,8,256]{3,2,1,0:T(8,128)S(1)}, f32[5,4,8,256]{3,2,1,0:T(8,128)S(1)}, u32[]{:S(2)}, u32[]{:S(2)}) collective-permute-start(f32[5,4,8,256]{3,2,1,0:T(8,128)S(1)} %get-tuple-element.20), channel_id=1, source_target_pairs={{1,2},{3,4},{5,6},{7,8},{9,10},{11,12},{13,14},{15,0},{2,1},{4,3},... | collective-permute-start | bytes 491528 | tf_op jit(solution)/shard_map/ppermute | solution.py:304
  17.3 12.9 %collective-permute-start.3 = (f32[5,4,16,256]{3,2,1,0:T(8,128)S(1)}, f32[5,4,16,256]{3,2,1,0:T(8,128)S(1)}, u32[]{:S(2)}, u32[]{:S(2)}) collective-permute-start(f32[5,4,16,256]{3,2,1,0:T(8,128)S(1)} %get-tuple-element.26), channel_id=1, source_target_pairs={{0,16},{32,48},{64,80},{96,112},{128,144},{160,176},{192,208},{224... | collective-permute-start | bytes 983048 | tf_op jit(solution)/shard_map/ppermute | solution.py:304
  19.2 9.7 %collective-permute-start.2 = (f32[5,4,8,256]{3,2,1,0:T(8,128)S(1)}, f32[5,4,8,256]{3,2,1,0:T(8,128)S(1)}, u32[]{:S(2)}, u32[]{:S(2)}) collective-permute-start(f32[5,4,8,256]{3,2,1,0:T(8,128)S(1)} %get-tuple-element.23), channel_id=1, source_target_pairs={{0,1},{2,3},{4,5},{6,7},{8,9},{10,11},{12,13},{14,15},{1,0},{3,2},... | collective-permute-start | bytes 491528 | tf_op jit(solution)/shard_map/ppermute | solution.py:304

commit v9 on v8

--- a/solution.py
+++ b/solution.py
@@ -16,11 +16,9 @@
 AXES = ("z_lo", "y", "z_hi", "x", "core")
 SIZES = (4, 8, 2, 4, 2)
 GX, GY = AXES[:2], AXES[2:]
-NEAR, FAR = ("y", "core"), ("z_lo", "z_hi", "x")
 VMEM = pltpu.VMEM
 SMEM = pltpu.SMEM
-INNER_COST, ODD_COST, EVEN_COST = 1 << 20, 3 << 20, 1 << 20
-Y_COST = 4 << 20
+INNER_COST, X_COST, Y_COST, LAST_COST = 1 << 20, 1 << 20, 7 << 20, 1 << 20
 
 
 def primitive(q):
@@ -189,20 +187,53 @@
     lax.fori_loop(0, 4, layer, 0)
 
 
-def finish(below, base, rate, step, fluxes, smooths, new, out, sems):
+def x_terms(c, t, fluxes, smooths):
+    total = None
+    for d in range(4 - t):
+        term = FIRST[d + t] * fluxes[c, d]
+        if c:
+            term = term + SECOND[d + t] * smooths[c - 1, d]
+        total = term if total is None else total + term
+    return total
+
+
+def one_side(rim, below, sums):
+    for side, rows, others in ((1, pl.ds(0, 8), pl.ds(8, 8)), (0, pl.ds(8, 8), pl.ds(0, 8))):
+
+        @pl.when(below == side)
+        def _(side=side, rows=rows, others=others):
+            y_side(rim, sums.at[:, :, rows], side == 1)
+            sums[:, :, others] = jnp.zeros((5, 8, 8, 256), jnp.float32)
+
+
+def y_kernel(rate, rim, out, sums):
+    one_side(rim, 1 - odd("core"), sums)
+    out[...] = rate[...] + sums[...]
+
+
+def x_kernel(rate, rim, out, fluxes, smooths):
+    below = 1 - odd("y")
+    x_side(rim, below, fluxes, smooths)
+    for t in range(8):
+        i = jnp.where(below == 1, t, 7 - t)
+        for c in range(5):
+            out[c, i] = rate[c, i] + x_terms(c, t, fluxes, smooths) if t < 4 else rate[c, i]
+
+
+def last_kernel(base, rate, step, x_rim, y_rim, out, peak, fluxes, smooths, sums, new, sems):
+    below = odd("y")
+    one_side(y_rim, odd("core"), sums)
+    x_side(x_rim, below, fluxes, smooths)
     factor = jnp.tile(step[...], (2, 2))
     most = None
     copies = []
-    for t in range(4):
+    for t in range(7, -1, -1):
         i = jnp.where(below == 1, t, 7 - t)
         values = []
         for c in range(5):
-            total = None if rate is None else rate[c, i]
-            for d in range(4 - t):
-                term = FIRST[d + t] * fluxes[c, d]
-                if c:
-                    term = term + SECOND[d + t] * smooths[c - 1, d]
-                total = term if total is None else total + term
+            total = rate[c, i] + sums[c, i]
+            if t < 4:
+                total = total + x_terms(c, t, fluxes, smooths)
             value = base[c, i] + factor * total
             new[c, t] = value
             values.append(value)
@@ -212,64 +243,13 @@
         inverse, velocity, kinetic, pressure = primitive(values)
         speed = jnp.sqrt(2.0 * kinetic) + jnp.sqrt(GAMMA * pressure * inverse)
         most = speed if most is None else jnp.maximum(most, speed)
-    most = jnp.maximum(most[:, :128], most[:, 128:])
-    return copies, jnp.maximum(most[:8], most[8:])
-
-
-def one_side(rim, below, sums):
-    for side, rows, others in ((1, pl.ds(0, 8), pl.ds(8, 8)), (0, pl.ds(8, 8), pl.ds(0, 8))):
-
-        @pl.when(below == side)
-        def _(side=side, rows=rows, others=others):
-            y_side(rim, sums.at[:, :, rows], side == 1)
-            sums[:, :, others] = jnp.zeros((5, 8, 8, 256), jnp.float32)
-
-
-def y_kernel(rate, rim, out, sums):
-    one_side(rim, 1 - odd("core"), sums)
-    out[...] = rate[...] + sums[...]
-
-
-def odd_kernel(base, rate, step, x_rim, y_even, out, rest, most, fluxes, smooths, sums, new, sems):
-    below = 1 - odd("y")
-    one_side(y_even, odd("core"), sums)
-    factor = jnp.tile(step[...], (2, 2))
-
-    def layer(t, carry):
-        i = jnp.where(below == 1, 7 - t, t)
-        for c in range(5):
-            rest[c, i] = base[c, i] + factor * (rate[c, i] + sums[c, i])
-        return carry
-
-    def edge(t, carry):
-        i = jnp.where(below == 1, t, 7 - t)
-        for c in range(5):
-            sums[c, i] = sums[c, i] + rate[c, i]
-        return carry
-
-    x_side(x_rim, below, fluxes, smooths)
-    lax.fori_loop(0, 4, edge, 0)
-    copies, most[...] = finish(below, base, sums, step, fluxes, smooths, new, out, sems)
-    lax.fori_loop(0, 4, layer, 0)
+    spread(jnp.maximum(most[:, :128], most[:, 128:]), peak)
     for copy in copies:
         copy.wait()
 
 
-def even_kernel(rest, step, most, x_rim, half, out, peak, fluxes, smooths, new, sems):
-    below = odd("y")
-    x_side(x_rim, below, fluxes, smooths)
-    copies, mine = finish(below, rest, None, step, fluxes, smooths, new, out, sems)
-    spread(jnp.maximum(mine, most[...]), peak)
-    for copy in copies:
-        copy.wait()
-
-
 def spread(values, out):
     out[...] = jnp.broadcast_to(jnp.max(values, axis=0, keepdims=True), out.shape)
-
-
-def pass_kernel(peaks, out):
-    spread(peaks[...], out)
 
 
 def most_kernel(peaks, out):
@@ -330,39 +310,22 @@
         rate,
     )
     rims = [in_vmem(5, 4, 16, 256), in_vmem(4, 4, 16, 256)]
-    outgoing = [in_vmem(5, 4, 16, 256), pltpu.SemaphoreType.DMA((4,))]
-    far_state = pltpu.HBM((5, 8, 16, 256), jnp.float32)
+    (rate,) = call(x_kernel, (state,), [VMEM] * 2, rims, X_COST, rate, x_odd)
     (rate,) = call(y_kernel, (state,), [VMEM] * 2, [state], Y_COST, rate, y_odd)
-    half, rest, most = call(
-        odd_kernel,
-        (far_state, state, in_vmem(8, 128)),
+    new, peak = call(
+        last_kernel,
+        (pltpu.HBM((5, 8, 16, 256), jnp.float32), in_vmem(lax.axis_size(AXES), 128)),
         [VMEM] * 5,
-        rims + [state] + outgoing,
-        ODD_COST,
+        rims + [state, state, pltpu.SemaphoreType.DMA((8,))],
+        LAST_COST,
         base,
         rate,
         step,
-        x_odd,
+        x_even,
         y_even,
-        out_specs=(pltpu.HBM, VMEM, VMEM),
-    )
-    new, peak = call(
-        even_kernel,
-        (far_state, in_vmem(lax.axis_size(NEAR), 128)),
-        [VMEM] * 4 + [pltpu.HBM],
-        rims + outgoing,
-        EVEN_COST,
-        rest,
-        step,
-        most,
-        x_even,
-        half,
         out_specs=(pltpu.HBM, VMEM),
-        aliases={4: 0},
-    )
-    peaks = lax.all_to_all(peak, NEAR, 0, 0, tiled=True)
-    (peak,) = call(pass_kernel, (in_vmem(lax.axis_size(FAR), 128),), [VMEM], [], 0, peaks)
-    peaks = lax.all_to_all(peak, FAR, 0, 0, tiled=True)
+    )
+    peaks = lax.all_to_all(peak, AXES, 0, 0, tiled=True)
     (most,) = call(
         most_kernel, (SMEM((1,), jnp.float32),), [VMEM], [], 0, peaks, out_specs=(SMEM,)
     )

time: 59.2 us -> 60.4 us (1.020)
  blocking collectives: 27.1 us -> 28.9 us
    all_to_all x2 -> x1, blocking collectives: 27.1 us -> 28.9 us  [local(): peaks = lax.all_to_all(peak, AXES, 0, 0, tiled=True)]
    pallas_call x7 -> x6, Pallas kernels: 7.62 us -> 7.06 us  [call(): pl.pallas_call(kernel, out_shape=outs, in_specs=[pl.BlockSpec(memory_spac...]
  transfers between devices with their start and end apart: 4 -> 4, of which waited for: 0 -> 0; matrix products, arithmetic and copies ran while one was open for 0% -> 0% of each run, Pallas kernels for 3% -> 1%
where the time goes in v9:
time: 60.4 us; the launch traced here: 60.1 us
  blocking collectives  28.9 us (48%)
  starting transfers between devices  22.2 us (37%)
  Pallas kernels  7.06 us (12%)
  between operations  1.9 us (3%)
    all_to_all x1, blocking collectives, local(): peaks = lax.all_to_all(peak, AXES, 0, 0, tiled=True)  28.9 us
    ppermute x4, starting transfers between devices, swap(): return lax.ppermute(x, axis, pairs + [(b, a) for a, b in pairs])  22.2 us
    pallas_call x6, Pallas kernels, call(): pl.pallas_call(kernel, out_shape=outs, in_specs=[pl.BlockSpec(memory_spac...  7.06 us
  transfers between devices with their start and end apart: 4, of which 0 were waited for; matrix products, arithmetic and copies ran while one was open for 0% of the time, Pallas kernels for 1%

profile of v9, /device:TPU:1, one launch (start us, length us, event | category | flops | bytes accessed | tf_op | source)
XLA Modules:
  0.0 60.1 jit_solution(13836488218519916088)
XLA Ops:
  0.6 4.8 %shard_map.50 = (f32[5,4,16,256]{3,2,1,0:T(8,128)S(1)}, f32[5,4,8,256]{3,2,1,0:T(8,128)S(1)}, f32[5,4,16,256]{3,2,1,0:T(8,128)S(1)}, f32[5,4,8,256]{3,2,1,0:T(8,...) custom-call(f32[5,8,16,256]{3,2,1,0:T(8,128)} %far_start.1, f32[5,8,16,256]{3,2,1,0:T(8,128)} %section_far.3), custom_call_target="tpu_custom_call" | custom-call | tf_op jit(solution)/shard_map/pallas_call | solution.py:265
  5.4 7.9 %collective-permute-start = (f32[5,4,16,256]{3,2,1,0:T(8,128)S(1)}, f32[5,4,16,256]{3,2,1,0:T(8,128)S(1)}, u32[]{:S(2)}, u32[]{:S(2)}) collective-permute-start(f32[5,4,16,256]{3,2,1,0:T(8,128)S(1)} %get-tuple-element.17), channel_id=1, source_target_pairs={{16,32},{48,64},{80,96},{112,128},{144,160},{176,192},{208,224},{2... | collective-permute-start | bytes 983048 | tf_op jit(solution)/shard_map/ppermute | solution.py:284
  13.3 4.0 %collective-permute-start.1 = (f32[5,4,8,256]{3,2,1,0:T(8,128)S(1)}, f32[5,4,8,256]{3,2,1,0:T(8,128)S(1)}, u32[]{:S(2)}, u32[]{:S(2)}) collective-permute-start(f32[5,4,8,256]{3,2,1,0:T(8,128)S(1)} %get-tuple-element.18), channel_id=1, source_target_pairs={{1,2},{3,4},{5,6},{7,8},{9,10},{11,12},{13,14},{15,0},{2,1},{4,3},... | collective-permute-start | bytes 491528 | tf_op jit(solution)/shard_map/ppermute | solution.py:284
  17.3 1.9 %collective-permute-start.2 = (f32[5,4,16,256]{3,2,1,0:T(8,128)S(1)}, f32[5,4,16,256]{3,2,1,0:T(8,128)S(1)}, u32[]{:S(2)}, u32[]{:S(2)}) collective-permute-start(f32[5,4,16,256]{3,2,1,0:T(8,128)S(1)} %get-tuple-element.20), channel_id=1, source_target_pairs={{0,16},{32,48},{64,80},{96,112},{128,144},{160,176},{192,208},{224... | collective-permute-start | bytes 983048 | tf_op jit(solution)/shard_map/ppermute | solution.py:284
  19.2 8.5 %collective-permute-start.3 = (f32[5,4,8,256]{3,2,1,0:T(8,128)S(1)}, f32[5,4,8,256]{3,2,1,0:T(8,128)S(1)}, u32[]{:S(2)}, u32[]{:S(2)}) collective-permute-start(f32[5,4,8,256]{3,2,1,0:T(8,128)S(1)} %get-tuple-element.21), channel_id=1, source_target_pairs={{0,1},{2,3},{4,5},{6,7},{8,9},{10,11},{12,13},{14,15},{1,0},{3,2},... | collective-permute-start | bytes 491528 | tf_op jit(solution)/shard_map/ppermute | solution.py:284
  28.3 0.2 shard_map.51
  28.5 0.0 collective-permute-done.rim
  28.5 0.3 shard_map.52.rate
  28.8 0.0 collective-permute-done.1.rim
  28.8 0.3 shard_map.53.rate
  29.1 0.0 collective-permute-done.3.y_rim
  29.1 0.0 collective-permute-done.2.x_rim
  29.1 1.4 %shard_map.54 = (f32[5,8,16,256]{3,2,1,0:T(8,128)}, f32[512,128]{1,0:T(8,128)S(1)}) custom-call(f32[5,8,16,256]{3,2,1,0:T(8,128)S(1)} %get-tuple-element.15.base, f32[5,8,16,256]{3,2,1,0:T(8,128)S(1)} %shard_map.53.rate, f32[8,128]{1,0:T(8,128)S(1)} %get-tuple-element.19.step, f32[5,4,16,256]{3,2,1,0:T(8,128)S(1)} %collective-permute-done.2.x_rim, ...), custom_call_target="tpu_custom_call" | custom-call | flops 314572800 | bytes 1048576 | tf_op jit(solution)/shard_map/pallas_call | solution.py:265
  30.6 28.9 %all_to_all.11 = f32[512,1,128]{2,1,0:T(1,128)S(1)} all-to-all(f32[512,1,128]{2,1,0:T(1,128)S(1)} %bitcast.8), channel_id=1, replica_groups=mesh['z_lo'=4,'y'=8,'z_hi'=2,'x'=4,'core'=2] {'z_lo','y','z_hi','x','core'}, dimensions={0} | all-to-all | bytes 524288 | tf_op jit(solution)/shard_map/all_to_all | solution.py:328
  59.4 0.1 shard_map.55
Async XLA Ops:
  5.4 23.1 %collective-permute-start = (f32[5,4,16,256]{3,2,1,0:T(8,128)S(1)}, f32[5,4,16,256]{3,2,1,0:T(8,128)S(1)}, u32[]{:S(2)}, u32[]{:S(2)}) collective-permute-start(f32[5,4,16,256]{3,2,1,0:T(8,128)S(1)} %get-tuple-element.17), channel_id=1, source_target_pairs={{16,32},{48,64},{80,96},{112,128},{144,160},{176,192},{208,224},{2... | collective-permute-start | bytes 983048 | tf_op jit(solution)/shard_map/ppermute | solution.py:284
  13.3 15.5 %collective-permute-start.1 = (f32[5,4,8,256]{3,2,1,0:T(8,128)S(1)}, f32[5,4,8,256]{3,2,1,0:T(8,128)S(1)}, u32[]{:S(2)}, u32[]{:S(2)}) collective-permute-start(f32[5,4,8,256]{3,2,1,0:T(8,128)S(1)} %get-tuple-element.18), channel_id=1, source_target_pairs={{1,2},{3,4},{5,6},{7,8},{9,10},{11,12},{13,14},{15,0},{2,1},{4,3},... | collective-permute-start | bytes 491528 | tf_op jit(solution)/shard_map/ppermute | solution.py:284
  17.3 11.9 %collective-permute-start.2 = (f32[5,4,16,256]{3,2,1,0:T(8,128)S(1)}, f32[5,4,16,256]{3,2,1,0:T(8,128)S(1)}, u32[]{:S(2)}, u32[]{:S(2)}) collective-permute-start(f32[5,4,16,256]{3,2,1,0:T(8,128)S(1)} %get-tuple-element.20), channel_id=1, source_target_pairs={{0,16},{32,48},{64,80},{96,112},{128,144},{160,176},{192,208},{224... | collective-permute-start | bytes 983048 | tf_op jit(solution)/shard_map/ppermute | solution.py:284
  19.2 9.9 %collective-permute-start.3 = (f32[5,4,8,256]{3,2,1,0:T(8,128)S(1)}, f32[5,4,8,256]{3,2,1,0:T(8,128)S(1)}, u32[]{:S(2)}, u32[]{:S(2)}) collective-permute-start(f32[5,4,8,256]{3,2,1,0:T(8,128)S(1)} %get-tuple-element.21), channel_id=1, source_target_pairs={{0,1},{2,3},{4,5},{6,7},{8,9},{10,11},{12,13},{14,15},{1,0},{3,2},... | collective-permute-start | bytes 491528 | tf_op jit(solution)/shard_map/ppermute | solution.py:284

commit v10 on v5

--- a/solution.py
+++ b/solution.py
@@ -19,7 +19,7 @@
 NEAR, FAR = ("y", "core"), ("z_lo", "z_hi", "x")
 VMEM = pltpu.VMEM
 SMEM = pltpu.SMEM
-INNER_COST, ODD_COST, EVEN_COST = 1 << 20, 8 << 20, 1 << 20
+PACK_COST, INNER_COST, ODD_COST, EVEN_COST = 1 << 20, 1 << 20, 8 << 20, 1 << 20
 
 
 def primitive(q):
@@ -54,22 +54,23 @@
     return lax.rem(lax.axis_index(axis), 2)
 
 
-def pack_kernel(far_start, x_odd, y_odd, x_even, y_even, start, sems):
+def first_kernel(far_start, x_odd, sems):
     copies = [
-        pltpu.make_async_copy(far_start.at[c, rows], start.at[c, rows], sems.at[c, k])
+        pltpu.make_async_copy(far_start.at[c, pl.ds(4 * odd("y"), 4)], x_odd.at[c], sems.at[c])
         for c in range(5)
-        for k, rows in enumerate((pl.ds(0, 4), pl.ds(4, 4)))
     ]
     for copy in copies:
         copy.start()
+    for copy in copies:
+        copy.wait()
+
+
+def pack_kernel(start, y_odd, x_even, y_even):
     side = odd("y")
     first = lax.broadcasted_iota(jnp.int32, (8, 256), 0) < 4
     upper = odd("core") == 0
     for c in range(5):
-        copies[2 * c].wait()
-        copies[2 * c + 1].wait()
         x_even[c] = start[c, pl.ds(4 - 4 * side, 4)]
-        x_odd[c] = start[c, pl.ds(4 * side, 4)]
         for j in range(4):
             a, b = start[c, 2 * j, 0:8], start[c, 2 * j + 1, 0:8]
             low = jnp.where(first, a, pltpu.roll(b, 4, 0))
@@ -248,7 +249,7 @@
         out_specs=tuple(pl.BlockSpec(memory_space=out_space) for _ in outs),
         scratch_shapes=scratch,
         cost_estimate=estimate,
-        compiler_params=pltpu.CompilerParams(vmem_limit_bytes=24 << 20),
+        compiler_params=pltpu.CompilerParams(vmem_limit_bytes=8 << 20),
     )(*arrays)
 
 
@@ -263,14 +264,11 @@
 
 
 def local(start, section, previous_speed):
-    x_odd, y_odd, x_even, y_even = call(
-        pack_kernel,
-        (in_vmem(5, 4, 16, 256), in_vmem(5, 4, 8, 256)) * 2,
-        [pltpu.HBM],
-        [in_vmem(5, 8, 16, 256), pltpu.SemaphoreType.DMA((5, 2))],
-        0,
-        far(start),
-    )
+    x_rim, y_rim = in_vmem(5, 4, 16, 256), in_vmem(5, 4, 8, 256)
+    (x_odd,) = call(
+        first_kernel, (x_rim,), [pltpu.HBM], [pltpu.SemaphoreType.DMA((5,))], 0, far(start)
+    )
+    y_odd, x_even, y_even = call(pack_kernel, (y_rim, x_rim, y_rim), [VMEM], [], PACK_COST, start)
     x_odd, y_odd = swap(x_odd, GX, 1), swap(y_odd, GY, 1)
     y_even, x_even = swap(y_even, GY, 0), swap(x_even, GX, 0)
     state = in_vmem(5, 8, 16, 256)

time: 58.8 us -> 58.7 us (level)
    pallas_call x6 -> x7, Pallas kernels: 6.91 us -> 6.77 us  [call(): pl.pallas_call(kernel, out_shape=outs, in_specs=[pl.BlockSpec(memory_spac...]
where the time goes in v10:
time: 58.7 us; the launch traced here: 58.3 us
  starting transfers between devices  30.8 us (52%)
  blocking collectives  10.2 us (17%)
  waiting for transfers between devices  7.83 us (13%)
  Pallas kernels  6.77 us (12%)
  between operations  1.92 us (3%)
  local copies, waits for them, and re-layouts  0.84 us (1%)
    ppermute x4, starting transfers between devices, swap(): return lax.ppermute(x, axis, pairs + [(b, a) for a, b in pairs])  25.7 us
    all_to_all x1, blocking collectives, local(): peaks = lax.all_to_all(peak, NEAR, 0, 0, tiled=True)  10.2 us
    all_to_all x1, waiting for transfers between devices, local(): peaks = lax.all_to_all(peak, FAR, 0, 0, tiled=True)  7.82 us
    pallas_call x7, Pallas kernels, call(): pl.pallas_call(kernel, out_shape=outs, in_specs=[pl.BlockSpec(memory_spac...  6.77 us
    all_to_all x1, starting transfers between devices, local(): peaks = lax.all_to_all(peak, FAR, 0, 0, tiled=True)  5.05 us
  transfers between devices with their start and end apart: 5, of which 1 were waited for; matrix products, arithmetic and copies ran while one was open for 1% of the time, Pallas kernels for 7%

profile of v10, /device:TPU:1, one launch (start us, length us, event | category | flops | bytes accessed | tf_op | source)
XLA Modules:
  0.0 58.3 jit_solution(4396670685345160245)
XLA Ops:
  0.6 0.0 copy-start
  0.6 1.1 %shard_map.51 = f32[5,4,16,256]{3,2,1,0:T(8,128)S(1)} custom-call(f32[5,8,16,256]{3,2,1,0:T(8,128)} %start.3), custom_call_target="tpu_custom_call" | custom-call | tf_op jit(solution)/shard_map/pallas_call | solution.py:245
  1.7 11.4 %collective-permute-start = (f32[5,4,16,256]{3,2,1,0:T(8,128)S(1)}, f32[5,4,16,256]{3,2,1,0:T(8,128)S(1)}, u32[]{:S(2)}, u32[]{:S(2)}) collective-permute-start(f32[5,4,16,256]{3,2,1,0:T(8,128)S(1)} %shard_map.51), channel_id=1, source_target_pairs={{16,32},{48,64},{80,96},{112,128},{144,160},{176,192},{208,224},{2... | collective-permute-start | bytes 983048 | tf_op jit(solution)/shard_map/ppermute | solution.py:263
  13.1 0.0 copy-done
  13.1 0.1 shard_map.52
  13.2 4.0 %collective-permute-start.1 = (f32[5,4,8,256]{3,2,1,0:T(8,128)S(1)}, f32[5,4,8,256]{3,2,1,0:T(8,128)S(1)}, u32[]{:S(2)}, u32[]{:S(2)}) collective-permute-start(f32[5,4,8,256]{3,2,1,0:T(8,128)S(1)} %get-tuple-element.11), channel_id=1, source_target_pairs={{1,2},{3,4},{5,6},{7,8},{9,10},{11,12},{13,14},{15,0},{2,1},{4,3},... | collective-permute-start | bytes 491528 | tf_op jit(solution)/shard_map/ppermute | solution.py:263
  17.1 1.9 %collective-permute-start.2 = (f32[5,4,16,256]{3,2,1,0:T(8,128)S(1)}, f32[5,4,16,256]{3,2,1,0:T(8,128)S(1)}, u32[]{:S(2)}, u32[]{:S(2)}) collective-permute-start(f32[5,4,16,256]{3,2,1,0:T(8,128)S(1)} %get-tuple-element.12), channel_id=1, source_target_pairs={{0,16},{32,48},{64,80},{96,112},{128,144},{160,176},{192,208},{224... | collective-permute-start | bytes 983048 | tf_op jit(solution)/shard_map/ppermute | solution.py:263
  19.1 8.5 %collective-permute-start.3 = (f32[5,4,8,256]{3,2,1,0:T(8,128)S(1)}, f32[5,4,8,256]{3,2,1,0:T(8,128)S(1)}, u32[]{:S(2)}, u32[]{:S(2)}) collective-permute-start(f32[5,4,8,256]{3,2,1,0:T(8,128)S(1)} %get-tuple-element.13), channel_id=1, source_target_pairs={{0,1},{2,3},{4,5},{6,7},{8,9},{10,11},{12,13},{14,15},{1,0},{3,2},... | collective-permute-start | bytes 491528 | tf_op jit(solution)/shard_map/ppermute | solution.py:263
  28.2 3.7 %shard_map.50 = (f32[5,8,16,256]{3,2,1,0:T(8,128)S(1)}, f32[8,128]{1,0:T(8,128)S(1)}) custom-call(f32[1,1]{1,0:T(1,128)} %bitcast.10.speed, f32[5,8,16,256]{3,2,1,0:T(8,128)S(1)} %copy-done, f32[5,8,16,256]{3,2,1,0:T(8,128)} %section_far.1), custom_call_target="tpu_custom_call" | custom-call | flops 314572800 | bytes 1048576 | tf_op jit(solution)/shard_map/pallas_call | solution.py:245
  31.9 0.0 collective-permute-done.1.y_rim
  32.0 0.0 collective-permute-done.x_rim
  32.0 0.5 shard_map.53.inner
  32.5 0.0 collective-permute-done.3.y_rim
  32.5 0.0 collective-permute-done.2.x_rim
  32.5 0.7 %shard_map.54 = (f32[5,8,16,256]{3,2,1,0:T(8,128)S(1)}, f32[16,128]{1,0:T(8,128)S(1)}) custom-call(f32[5,8,16,256]{3,2,1,0:T(8,128)S(1)} %shard_map.53.inner, f32[8,128]{1,0:T(8,128)S(1)} %get-tuple-element.10.step, f32[5,4,16,256]{3,2,1,0:T(8,128)S(1)} %collective-permute-done.2.x_rim, f32[5,4,8,256]{3,2,1,0:T(8,128)S(1)} %collective-permute-done.3.y_rim), custom_call_target="tpu_custom_call" | custom-call | flops 314572800 | bytes 1048576 | tf_op jit(solution)/shard_map/pallas_call | solution.py:245
  33.2 10.2 %all_to_all.22 = f32[16,1,128]{2,1,0:T(1,128)S(1)} all-to-all(f32[16,1,128]{2,1,0:T(1,128)S(1)} %bitcast.13), channel_id=1, replica_groups=mesh['z_lo'=4,'y'=8,'z_hi'=2,'x'=4,'core'=2] {'y','core'}, dimensions={0} | all-to-all | bytes 16384 | tf_op jit(solution)/shard_map/all_to_all | solution.py:303
  43.4 0.6 %shard_map.55 = f32[32,128]{1,0:T(8,128)} custom-call(f32[16,128]{1,0:T(8,128)S(1)} %bitcast.12), custom_call_target="tpu_custom_call" | custom-call | tf_op jit(solution)/shard_map/pallas_call | solution.py:245
  44.0 5.1 %all-to-all-start.1 = ((f32[32,1,128]{2,1,0:T(1,128)}), f32[32,1,128]{2,1,0:T(1,128)S(1)}, u32[]{:S(2)}, u32[]{:S(2)}) async-start(f32[32,1,128]{2,1,0:T(1,128)} %bitcast.5), calls=%async_computation.1 | async-start | bytes 32768 | tf_op jit(solution)/shard_map/all_to_all | solution.py:305
  49.1 0.8 %copy.7 = f32[5,8,16,256]{3,2,1,0:T(8,128)} copy(f32[5,8,16,256]{3,2,1,0:T(8,128)S(1)} %get-tuple-element.16) | data formatting | bytes 1310720
  49.9 7.8 %all-to-all-done.1 = f32[32,1,128]{2,1,0:T(1,128)S(1)} async-done(((f32[32,1,128]{2,1,0:T(1,128)}), f32[32,1,128]{2,1,0:T(1,128)S(1)}, u32[]{:S(2)}, u32[]{:S(2)}) %all-to-all-start.1) | async-done | bytes 16416 | tf_op jit(solution)/shard_map/all_to_all | solution.py:305
  57.7 0.1 shard_map.56
Async XLA Ops:
  0.6 12.5 %copy-start = (f32[5,8,16,256]{3,2,1,0:T(8,128)S(1)}, f32[5,8,16,256]{3,2,1,0:T(8,128)}, u32[]{:S(2)}) copy-start(f32[5,8,16,256]{3,2,1,0:T(8,128)} %start.3) | copy-start | bytes 1966084
  1.7 30.2 %collective-permute-start = (f32[5,4,16,256]{3,2,1,0:T(8,128)S(1)}, f32[5,4,16,256]{3,2,1,0:T(8,128)S(1)}, u32[]{:S(2)}, u32[]{:S(2)}) collective-permute-start(f32[5,4,16,256]{3,2,1,0:T(8,128)S(1)} %shard_map.51), channel_id=1, source_target_pairs={{16,32},{48,64},{80,96},{112,128},{144,160},{176,192},{208,224},{2... | collective-permute-start | bytes 983048 | tf_op jit(solution)/shard_map/ppermute | solution.py:263
  13.2 18.8 %collective-permute-start.1 = (f32[5,4,8,256]{3,2,1,0:T(8,128)S(1)}, f32[5,4,8,256]{3,2,1,0:T(8,128)S(1)}, u32[]{:S(2)}, u32[]{:S(2)}) collective-permute-start(f32[5,4,8,256]{3,2,1,0:T(8,128)S(1)} %get-tuple-element.11), channel_id=1, source_target_pairs={{1,2},{3,4},{5,6},{7,8},{9,10},{11,12},{13,14},{15,0},{2,1},{4,3},... | collective-permute-start | bytes 491528 | tf_op jit(solution)/shard_map/ppermute | solution.py:263
  17.1 15.4 %collective-permute-start.2 = (f32[5,4,16,256]{3,2,1,0:T(8,128)S(1)}, f32[5,4,16,256]{3,2,1,0:T(8,128)S(1)}, u32[]{:S(2)}, u32[]{:S(2)}) collective-permute-start(f32[5,4,16,256]{3,2,1,0:T(8,128)S(1)} %get-tuple-element.12), channel_id=1, source_target_pairs={{0,16},{32,48},{64,80},{96,112},{128,144},{160,176},{192,208},{224... | collective-permute-start | bytes 983048 | tf_op jit(solution)/shard_map/ppermute | solution.py:263
  19.1 13.4 %collective-permute-start.3 = (f32[5,4,8,256]{3,2,1,0:T(8,128)S(1)}, f32[5,4,8,256]{3,2,1,0:T(8,128)S(1)}, u32[]{:S(2)}, u32[]{:S(2)}) collective-permute-start(f32[5,4,8,256]{3,2,1,0:T(8,128)S(1)} %get-tuple-element.13), channel_id=1, source_target_pairs={{0,1},{2,3},{4,5},{6,7},{8,9},{10,11},{12,13},{14,15},{1,0},{3,2},... | collective-permute-start | bytes 491528 | tf_op jit(solution)/shard_map/ppermute | solution.py:263
  44.0 13.7 %all-to-all-start.1 = ((f32[32,1,128]{2,1,0:T(1,128)}), f32[32,1,128]{2,1,0:T(1,128)S(1)}, u32[]{:S(2)}, u32[]{:S(2)}) async-start(f32[32,1,128]{2,1,0:T(1,128)} %bitcast.5), calls=%async_computation.1 | async-start | bytes 32768 | tf_op jit(solution)/shard_map/all_to_all | solution.py:305

commit v11 on v10

--- a/solution.py
+++ b/solution.py
@@ -19,7 +19,7 @@
 NEAR, FAR = ("y", "core"), ("z_lo", "z_hi", "x")
 VMEM = pltpu.VMEM
 SMEM = pltpu.SMEM
-PACK_COST, INNER_COST, ODD_COST, EVEN_COST = 1 << 20, 1 << 20, 8 << 20, 1 << 20
+PACK_COST, INNER_COST, ODD_COST, EVEN_COST = 1 << 20, 1 << 20, 7 << 20, 1 << 19
 
 
 def primitive(q):
@@ -81,15 +81,20 @@
 
 
 def inner_kernel(speed, start, section_far, out, step, section, fluxes, smooths, sems):
-    copies = [
-        pltpu.make_async_copy(section_far.at[:, i], section.at[:, i], sems.at[i]) for i in range(8)
-    ]
-    for copy in copies:
-        copy.start()
+    def load(i):
+        return pltpu.make_async_copy(section_far.at[:, i], section.at[:, i], sems.at[i])
+
+    load(0).start()
+    load(1).start()
     rows = lax.broadcasted_iota(jnp.int32, (16, 256), 0)
 
     def layer(i, carry):
-        pltpu.make_async_copy(section_far.at[:, i], section.at[:, i], sems.at[i]).wait()
+        load(i).wait()
+
+        @pl.when(i < 6)
+        def _():
+            load(i + 2).start()
+
         q = [section[c, i] for c in range(5)]
         inverse, velocity, kinetic, pressure = primitive(q)
         g = smooth(inverse, velocity, kinetic, pressure)
@@ -152,7 +157,7 @@
     lax.fori_loop(0, 4, pair, 0)
 
 
-def rim_terms(x_below, y_below, x_rim, y_rim, fluxes, smooths, sums):
+def y_terms(y_below, y_rim, sums):
     @pl.when(y_below == 1)
     def _():
         y_side(y_rim, sums, True)
@@ -161,6 +166,8 @@
     def _():
         y_side(y_rim, sums, False)
 
+
+def x_terms(x_below, x_rim, fluxes, smooths):
     sign = jnp.where(x_below == 1, 1.0, -1.0)
 
     def x_layer(d, carry):
@@ -181,15 +188,18 @@
 def rim_layer(t, x_below, y_below, inner, step, fluxes, smooths, sums):
     i = jnp.where(x_below == 1, t, 7 - t)
     factor = jnp.tile(step[...], (1, 2))
-    low = jnp.where(y_below == 1, factor, 0.0)
-    edge = jnp.concatenate([low, factor - low], axis=0)
+    if sums is not None:
+        low = jnp.where(y_below == 1, factor, 0.0)
+        edge = jnp.concatenate([low, factor - low], axis=0)
     factor = jnp.concatenate([factor, factor], axis=0)
     values = []
     for c in range(5):
-        part = sums[c, i]
-        value = inner[c, i] + edge * jnp.concatenate([part, part], axis=0)
+        value = inner[c, i]
+        if sums is not None:
+            part = sums[c, i]
+            value = value + edge * jnp.concatenate([part, part], axis=0)
         total = None
-        for d in range(4 - t):
+        for d in range(4 - t) if fluxes is not None else ():
             term = FIRST[d + t] * fluxes[c, d]
             if c:
                 term = term + SECOND[d + t] * smooths[c - 1, d]
@@ -202,19 +212,29 @@
 
 def odd_kernel(inner, step, x_rim, y_rim, out, fluxes, smooths, sums):
     x_below, y_below = 1 - odd("y"), 1 - odd("core")
-    rim_terms(x_below, y_below, x_rim, y_rim, fluxes, smooths, sums)
+    y_terms(y_below, y_rim, sums)
+    x_terms(x_below, x_rim, fluxes, smooths)
     for t in range(8):
         i, values = rim_layer(t, x_below, y_below, inner, step, fluxes, smooths, sums)
         for c in range(5):
             out[c, i] = values[c]
 
 
-def even_kernel(inner, step, x_rim, y_rim, out, peak, fluxes, smooths, sums):
-    x_below, y_below = odd("y"), odd("core")
-    rim_terms(x_below, y_below, x_rim, y_rim, fluxes, smooths, sums)
+def y_kernel(inner, step, y_rim, out, sums):
+    y_below = odd("core")
+    y_terms(y_below, y_rim, sums)
+    for t in range(8):
+        i, values = rim_layer(t, 1, y_below, inner, step, None, None, sums)
+        for c in range(5):
+            out[c, i] = values[c]
+
+
+def even_kernel(inner, step, x_rim, out, peak, fluxes, smooths):
+    x_below = odd("y")
+    x_terms(x_below, x_rim, fluxes, smooths)
     most = None
     for t in range(8):
-        i, values = rim_layer(t, x_below, y_below, inner, step, fluxes, smooths, sums)
+        i, values = rim_layer(t, x_below, None, inner, step, fluxes, smooths, None)
         for c in range(5):
             out[c, i] = values[c]
         inverse, velocity, kinetic, pressure = primitive(values)
@@ -287,18 +307,20 @@
         start,
         far(section),
     )
-    rims = [in_vmem(5, 4, 16, 256), in_vmem(4, 4, 16, 256), in_vmem(5, 8, 8, 256)]
-    (inner,) = call(odd_kernel, (state,), [VMEM] * 4, rims, ODD_COST, inner, step, x_odd, y_odd)
+    rims, sums = [x_rim, in_vmem(4, 4, 16, 256)], in_vmem(5, 8, 8, 256)
+    (inner,) = call(
+        odd_kernel, (state,), [VMEM] * 4, rims + [sums], ODD_COST, inner, step, x_odd, y_odd
+    )
+    (inner,) = call(y_kernel, (state,), [VMEM] * 3, [sums], EVEN_COST, inner, step, y_even)
     new, peak = call(
         even_kernel,
         (state, in_vmem(lax.axis_size(NEAR), 128)),
-        [VMEM] * 4,
+        [VMEM] * 3,
         rims,
         EVEN_COST,
         inner,
         step,
         x_even,
-        y_even,
     )
     peaks = lax.all_to_all(peak, NEAR, 0, 0, tiled=True)
     (peak,) = call(pass_kernel, (in_vmem(lax.axis_size(FAR), 128),), [VMEM], [], 0, peaks)

time: 58.7 us -> 59 us (level)
  Pallas kernels: 6.77 us -> 7.83 us
  starting transfers between devices: 30.8 us -> 29.8 us
    pallas_call x7 -> x8, Pallas kernels: 6.77 us -> 7.83 us  [call(): pl.pallas_call(kernel, out_shape=outs, in_specs=[pl.BlockSpec(memory_spac...]
    all_to_all x1, starting transfers between devices: 5.05 us -> 4.11 us  [local(): peaks = lax.all_to_all(peak, FAR, 0, 0, tiled=True)]
  transfers between devices with their start and end apart: 5 -> 5, of which waited for: 1 -> 1; matrix products, arithmetic and copies ran while one was open for 1% -> 1% of each run, Pallas kernels for 7% -> 10%
where the time goes in v11:
time: 59 us; the launch traced here: 58.5 us
  starting transfers between devices  29.8 us (51%)
  blocking collectives  10.2 us (17%)
  Pallas kernels  7.83 us (13%)
  waiting for transfers between devices  7.83 us (13%)
  between operations  1.92 us (3%)
  local copies, waits for them, and re-layouts  0.84 us (1%)
    ppermute x4, starting transfers between devices, swap(): return lax.ppermute(x, axis, pairs + [(b, a) for a, b in pairs])  25.7 us
    all_to_all x1, blocking collectives, local(): peaks = lax.all_to_all(peak, NEAR, 0, 0, tiled=True)  10.2 us
    pallas_call x8, Pallas kernels, call(): pl.pallas_call(kernel, out_shape=outs, in_specs=[pl.BlockSpec(memory_spac...  7.83 us
    all_to_all x1, waiting for transfers between devices, local(): peaks = lax.all_to_all(peak, FAR, 0, 0, tiled=True)  7.82 us
    all_to_all x1, starting transfers between devices, local(): peaks = lax.all_to_all(peak, FAR, 0, 0, tiled=True)  4.11 us
  transfers between devices with their start and end apart: 5, of which 1 were waited for; matrix products, arithmetic and copies ran while one was open for 1% of the time, Pallas kernels for 10%

profile of v11, /device:TPU:1, one launch (start us, length us, event | category | flops | bytes accessed | tf_op | source)
XLA Modules:
  0.0 58.5 jit_solution(14272057777981369909)
XLA Ops:
  0.6 0.0 copy-start
  0.6 1.1 %shard_map.51 = f32[5,4,16,256]{3,2,1,0:T(8,128)S(1)} custom-call(f32[5,8,16,256]{3,2,1,0:T(8,128)} %start.3), custom_call_target="tpu_custom_call" | custom-call | tf_op jit(solution)/shard_map/pallas_call | solution.py:265
  1.7 11.4 %collective-permute-start = (f32[5,4,16,256]{3,2,1,0:T(8,128)S(1)}, f32[5,4,16,256]{3,2,1,0:T(8,128)S(1)}, u32[]{:S(2)}, u32[]{:S(2)}) collective-permute-start(f32[5,4,16,256]{3,2,1,0:T(8,128)S(1)} %shard_map.51), channel_id=1, source_target_pairs={{16,32},{48,64},{80,96},{112,128},{144,160},{176,192},{208,224},{2... | collective-permute-start | bytes 983048 | tf_op jit(solution)/shard_map/ppermute | solution.py:283
  13.1 0.0 copy-done
  13.1 0.1 shard_map.52
  13.2 4.0 %collective-permute-start.1 = (f32[5,4,8,256]{3,2,1,0:T(8,128)S(1)}, f32[5,4,8,256]{3,2,1,0:T(8,128)S(1)}, u32[]{:S(2)}, u32[]{:S(2)}) collective-permute-start(f32[5,4,8,256]{3,2,1,0:T(8,128)S(1)} %get-tuple-element.11), channel_id=1, source_target_pairs={{1,2},{3,4},{5,6},{7,8},{9,10},{11,12},{13,14},{15,0},{2,1},{4,3},... | collective-permute-start | bytes 491528 | tf_op jit(solution)/shard_map/ppermute | solution.py:283
  17.1 1.9 %collective-permute-start.3 = (f32[5,4,16,256]{3,2,1,0:T(8,128)S(1)}, f32[5,4,16,256]{3,2,1,0:T(8,128)S(1)}, u32[]{:S(2)}, u32[]{:S(2)}) collective-permute-start(f32[5,4,16,256]{3,2,1,0:T(8,128)S(1)} %get-tuple-element.13), channel_id=1, source_target_pairs={{0,16},{32,48},{64,80},{96,112},{128,144},{160,176},{192,208},{224... | collective-permute-start | bytes 983048 | tf_op jit(solution)/shard_map/ppermute | solution.py:283
  19.1 8.5 %collective-permute-start.2 = (f32[5,4,8,256]{3,2,1,0:T(8,128)S(1)}, f32[5,4,8,256]{3,2,1,0:T(8,128)S(1)}, u32[]{:S(2)}, u32[]{:S(2)}) collective-permute-start(f32[5,4,8,256]{3,2,1,0:T(8,128)S(1)} %get-tuple-element.12), channel_id=1, source_target_pairs={{0,1},{2,3},{4,5},{6,7},{8,9},{10,11},{12,13},{14,15},{1,0},{3,2},... | collective-permute-start | bytes 491528 | tf_op jit(solution)/shard_map/ppermute | solution.py:283
  28.2 4.8 %shard_map.50 = (f32[5,8,16,256]{3,2,1,0:T(8,128)S(1)}, f32[8,128]{1,0:T(8,128)S(1)}) custom-call(f32[1,1]{1,0:T(1,128)} %bitcast.10.speed, f32[5,8,16,256]{3,2,1,0:T(8,128)S(1)} %copy-done, f32[5,8,16,256]{3,2,1,0:T(8,128)} %section_far.1), custom_call_target="tpu_custom_call" | custom-call | flops 314572800 | bytes 1048576 | tf_op jit(solution)/shard_map/pallas_call | solution.py:265
  33.0 0.0 collective-permute-done.1.y_rim
  33.0 0.0 collective-permute-done.x_rim
  33.0 0.5 shard_map.53.inner
  33.5 0.0 collective-permute-done.2.y_rim
  33.5 0.3 shard_map.54.inner
  33.8 0.0 collective-permute-done.3.x_rim
  33.8 0.4 shard_map.55
  34.2 10.2 %all_to_all.22 = f32[16,1,128]{2,1,0:T(1,128)S(1)} all-to-all(f32[16,1,128]{2,1,0:T(1,128)S(1)} %bitcast.13), channel_id=1, replica_groups=mesh['z_lo'=4,'y'=8,'z_hi'=2,'x'=4,'core'=2] {'y','core'}, dimensions={0} | all-to-all | bytes 16384 | tf_op jit(solution)/shard_map/all_to_all | solution.py:325
  44.5 0.6 %shard_map.56 = f32[32,128]{1,0:T(8,128)} custom-call(f32[16,128]{1,0:T(8,128)S(1)} %bitcast.12), custom_call_target="tpu_custom_call" | custom-call | tf_op jit(solution)/shard_map/pallas_call | solution.py:265
  45.1 4.1 %all-to-all-start.1 = ((f32[32,1,128]{2,1,0:T(1,128)}), f32[32,1,128]{2,1,0:T(1,128)S(1)}, u32[]{:S(2)}, u32[]{:S(2)}) async-start(f32[32,1,128]{2,1,0:T(1,128)} %bitcast.5), calls=%async_computation.1 | async-start | bytes 32768 | tf_op jit(solution)/shard_map/all_to_all | solution.py:327
  49.2 0.8 %copy.7 = f32[5,8,16,256]{3,2,1,0:T(8,128)} copy(f32[5,8,16,256]{3,2,1,0:T(8,128)S(1)} %get-tuple-element.16) | data formatting | bytes 1310720
  50.0 7.8 %all-to-all-done.1 = f32[32,1,128]{2,1,0:T(1,128)S(1)} async-done(((f32[32,1,128]{2,1,0:T(1,128)}), f32[32,1,128]{2,1,0:T(1,128)S(1)}, u32[]{:S(2)}, u32[]{:S(2)}) %all-to-all-start.1) | async-done | bytes 16416 | tf_op jit(solution)/shard_map/all_to_all | solution.py:327
  57.8 0.1 shard_map.57
Async XLA Ops:
  0.6 12.5 %copy-start = (f32[5,8,16,256]{3,2,1,0:T(8,128)S(1)}, f32[5,8,16,256]{3,2,1,0:T(8,128)}, u32[]{:S(2)}) copy-start(f32[5,8,16,256]{3,2,1,0:T(8,128)} %start.3) | copy-start | bytes 1966084
  1.7 31.2 %collective-permute-start = (f32[5,4,16,256]{3,2,1,0:T(8,128)S(1)}, f32[5,4,16,256]{3,2,1,0:T(8,128)S(1)}, u32[]{:S(2)}, u32[]{:S(2)}) collective-permute-start(f32[5,4,16,256]{3,2,1,0:T(8,128)S(1)} %shard_map.51), channel_id=1, source_target_pairs={{16,32},{48,64},{80,96},{112,128},{144,160},{176,192},{208,224},{2... | collective-permute-start | bytes 983048 | tf_op jit(solution)/shard_map/ppermute | solution.py:283
  13.2 19.8 %collective-permute-start.1 = (f32[5,4,8,256]{3,2,1,0:T(8,128)S(1)}, f32[5,4,8,256]{3,2,1,0:T(8,128)S(1)}, u32[]{:S(2)}, u32[]{:S(2)}) collective-permute-start(f32[5,4,8,256]{3,2,1,0:T(8,128)S(1)} %get-tuple-element.11), channel_id=1, source_target_pairs={{1,2},{3,4},{5,6},{7,8},{9,10},{11,12},{13,14},{15,0},{2,1},{4,3},... | collective-permute-start | bytes 491528 | tf_op jit(solution)/shard_map/ppermute | solution.py:283
  17.1 16.7 %collective-permute-start.3 = (f32[5,4,16,256]{3,2,1,0:T(8,128)S(1)}, f32[5,4,16,256]{3,2,1,0:T(8,128)S(1)}, u32[]{:S(2)}, u32[]{:S(2)}) collective-permute-start(f32[5,4,16,256]{3,2,1,0:T(8,128)S(1)} %get-tuple-element.13), channel_id=1, source_target_pairs={{0,16},{32,48},{64,80},{96,112},{128,144},{160,176},{192,208},{224... | collective-permute-start | bytes 983048 | tf_op jit(solution)/shard_map/ppermute | solution.py:283
  19.1 14.4 %collective-permute-start.2 = (f32[5,4,8,256]{3,2,1,0:T(8,128)S(1)}, f32[5,4,8,256]{3,2,1,0:T(8,128)S(1)}, u32[]{:S(2)}, u32[]{:S(2)}) collective-permute-start(f32[5,4,8,256]{3,2,1,0:T(8,128)S(1)} %get-tuple-element.12), channel_id=1, source_target_pairs={{0,1},{2,3},{4,5},{6,7},{8,9},{10,11},{12,13},{14,15},{1,0},{3,2},... | collective-permute-start | bytes 491528 | tf_op jit(solution)/shard_map/ppermute | solution.py:283
  45.1 12.8 %all-to-all-start.1 = ((f32[32,1,128]{2,1,0:T(1,128)}), f32[32,1,128]{2,1,0:T(1,128)S(1)}, u32[]{:S(2)}, u32[]{:S(2)}) async-start(f32[32,1,128]{2,1,0:T(1,128)} %bitcast.5), calls=%async_computation.1 | async-start | bytes 32768 | tf_op jit(solution)/shard_map/all_to_all | solution.py:327

commit v12 on v11

--- a/solution.py
+++ b/solution.py
@@ -81,19 +81,25 @@
 
 
 def inner_kernel(speed, start, section_far, out, step, section, fluxes, smooths, sems):
-    def load(i):
-        return pltpu.make_async_copy(section_far.at[:, i], section.at[:, i], sems.at[i])
-
-    load(0).start()
-    load(1).start()
+    def loads(half):
+        rows = pl.ds(4 * half, 4)
+        return [
+            pltpu.make_async_copy(section_far.at[c, rows], section.at[c, rows], sems.at[half, c])
+            for c in range(5)
+        ]
+
+    for half in range(2):
+        for copy in loads(half):
+            copy.start()
     rows = lax.broadcasted_iota(jnp.int32, (16, 256), 0)
 
     def layer(i, carry):
-        load(i).wait()
-
-        @pl.when(i < 6)
-        def _():
-            load(i + 2).start()
+        for half in range(2):
+
+            @pl.when(i == 4 * half)
+            def _(half=half):
+                for copy in loads(half):
+                    copy.wait()
 
         q = [section[c, i] for c in range(5)]
         inverse, velocity, kinetic, pressure = primitive(q)
@@ -300,7 +306,7 @@
             state,
             state,
             in_vmem(4, 8, 16, 256),
-            pltpu.SemaphoreType.DMA((8,)),
+            pltpu.SemaphoreType.DMA((2, 5)),
         ],
         INNER_COST,
         previous_speed.reshape(1, 1),

time: 59 us -> 58.5 us (level)
  Pallas kernels: 7.83 us -> 6.94 us
    pallas_call x8, Pallas kernels: 7.83 us -> 6.94 us  [call(): pl.pallas_call(kernel, out_shape=outs, in_specs=[pl.BlockSpec(memory_spac...]
  transfers between devices with their start and end apart: 5 -> 5, of which waited for: 1 -> 1; matrix products, arithmetic and copies ran while one was open for 1% -> 1% of each run, Pallas kernels for 10% -> 8%
where the time goes in v12:
time: 58.5 us; the launch traced here: 58.1 us
  starting transfers between devices  30.3 us (52%)
  blocking collectives  10.2 us (17%)
  waiting for transfers between devices  7.83 us (13%)
  Pallas kernels  6.94 us (12%)
  between operations  1.92 us (3%)
  local copies, waits for them, and re-layouts  0.84 us (1%)
    ppermute x4, starting transfers between devices, swap(): return lax.ppermute(x, axis, pairs + [(b, a) for a, b in pairs])  25.7 us
    all_to_all x1, blocking collectives, local(): peaks = lax.all_to_all(peak, NEAR, 0, 0, tiled=True)  10.2 us
    all_to_all x1, waiting for transfers between devices, local(): peaks = lax.all_to_all(peak, FAR, 0, 0, tiled=True)  7.82 us
    pallas_call x8, Pallas kernels, call(): pl.pallas_call(kernel, out_shape=outs, in_specs=[pl.BlockSpec(memory_spac...  6.94 us
    all_to_all x1, starting transfers between devices, local(): peaks = lax.all_to_all(peak, FAR, 0, 0, tiled=True)  4.61 us
  transfers between devices with their start and end apart: 5, of which 1 were waited for; matrix products, arithmetic and copies ran while one was open for 1% of the time, Pallas kernels for 8%

profile of v12, /device:TPU:1, one launch (start us, length us, event | category | flops | bytes accessed | tf_op | source)
XLA Modules:
  0.0 58.1 jit_solution(2446570700007150352)
XLA Ops:
  0.6 0.0 copy-start
  0.6 1.1 %shard_map.51 = f32[5,4,16,256]{3,2,1,0:T(8,128)S(1)} custom-call(f32[5,8,16,256]{3,2,1,0:T(8,128)} %start.3), custom_call_target="tpu_custom_call" | custom-call | tf_op jit(solution)/shard_map/pallas_call | solution.py:271
  1.7 11.4 %collective-permute-start = (f32[5,4,16,256]{3,2,1,0:T(8,128)S(1)}, f32[5,4,16,256]{3,2,1,0:T(8,128)S(1)}, u32[]{:S(2)}, u32[]{:S(2)}) collective-permute-start(f32[5,4,16,256]{3,2,1,0:T(8,128)S(1)} %shard_map.51), channel_id=1, source_target_pairs={{16,32},{48,64},{80,96},{112,128},{144,160},{176,192},{208,224},{2... | collective-permute-start | bytes 983048 | tf_op jit(solution)/shard_map/ppermute | solution.py:289
  13.1 0.0 copy-done
  13.1 0.1 shard_map.52
  13.2 4.0 %collective-permute-start.1 = (f32[5,4,8,256]{3,2,1,0:T(8,128)S(1)}, f32[5,4,8,256]{3,2,1,0:T(8,128)S(1)}, u32[]{:S(2)}, u32[]{:S(2)}) collective-permute-start(f32[5,4,8,256]{3,2,1,0:T(8,128)S(1)} %get-tuple-element.11), channel_id=1, source_target_pairs={{1,2},{3,4},{5,6},{7,8},{9,10},{11,12},{13,14},{15,0},{2,1},{4,3},... | collective-permute-start | bytes 491528 | tf_op jit(solution)/shard_map/ppermute | solution.py:289
  17.1 1.9 %collective-permute-start.3 = (f32[5,4,16,256]{3,2,1,0:T(8,128)S(1)}, f32[5,4,16,256]{3,2,1,0:T(8,128)S(1)}, u32[]{:S(2)}, u32[]{:S(2)}) collective-permute-start(f32[5,4,16,256]{3,2,1,0:T(8,128)S(1)} %get-tuple-element.13), channel_id=1, source_target_pairs={{0,16},{32,48},{64,80},{96,112},{128,144},{160,176},{192,208},{224... | collective-permute-start | bytes 983048 | tf_op jit(solution)/shard_map/ppermute | solution.py:289
  19.1 8.5 %collective-permute-start.2 = (f32[5,4,8,256]{3,2,1,0:T(8,128)S(1)}, f32[5,4,8,256]{3,2,1,0:T(8,128)S(1)}, u32[]{:S(2)}, u32[]{:S(2)}) collective-permute-start(f32[5,4,8,256]{3,2,1,0:T(8,128)S(1)} %get-tuple-element.12), channel_id=1, source_target_pairs={{0,1},{2,3},{4,5},{6,7},{8,9},{10,11},{12,13},{14,15},{1,0},{3,2},... | collective-permute-start | bytes 491528 | tf_op jit(solution)/shard_map/ppermute | solution.py:289
  28.2 3.9 %shard_map.50 = (f32[5,8,16,256]{3,2,1,0:T(8,128)S(1)}, f32[8,128]{1,0:T(8,128)S(1)}) custom-call(f32[1,1]{1,0:T(1,128)} %bitcast.10.speed, f32[5,8,16,256]{3,2,1,0:T(8,128)S(1)} %copy-done, f32[5,8,16,256]{3,2,1,0:T(8,128)} %section_far.1), custom_call_target="tpu_custom_call" | custom-call | flops 314572800 | bytes 1048576 | tf_op jit(solution)/shard_map/pallas_call | solution.py:271
  32.1 0.0 collective-permute-done.1.y_rim
  32.1 0.0 collective-permute-done.x_rim
  32.1 0.5 shard_map.53.inner
  32.6 0.0 collective-permute-done.2.y_rim
  32.6 0.3 shard_map.54.inner
  32.9 0.0 collective-permute-done.3.x_rim
  32.9 0.4 shard_map.55
  33.3 10.2 %all_to_all.22 = f32[16,1,128]{2,1,0:T(1,128)S(1)} all-to-all(f32[16,1,128]{2,1,0:T(1,128)S(1)} %bitcast.13), channel_id=1, replica_groups=mesh['z_lo'=4,'y'=8,'z_hi'=2,'x'=4,'core'=2] {'y','core'}, dimensions={0} | all-to-all | bytes 16384 | tf_op jit(solution)/shard_map/all_to_all | solution.py:331
  43.6 0.6 %shard_map.56 = f32[32,128]{1,0:T(8,128)} custom-call(f32[16,128]{1,0:T(8,128)S(1)} %bitcast.12), custom_call_target="tpu_custom_call" | custom-call | tf_op jit(solution)/shard_map/pallas_call | solution.py:271
  44.2 4.6 %all-to-all-start.1 = ((f32[32,1,128]{2,1,0:T(1,128)}), f32[32,1,128]{2,1,0:T(1,128)S(1)}, u32[]{:S(2)}, u32[]{:S(2)}) async-start(f32[32,1,128]{2,1,0:T(1,128)} %bitcast.5), calls=%async_computation.1 | async-start | bytes 32768 | tf_op jit(solution)/shard_map/all_to_all | solution.py:333
  48.8 0.8 %copy.7 = f32[5,8,16,256]{3,2,1,0:T(8,128)} copy(f32[5,8,16,256]{3,2,1,0:T(8,128)S(1)} %get-tuple-element.16) | data formatting | bytes 1310720
  49.6 7.8 %all-to-all-done.1 = f32[32,1,128]{2,1,0:T(1,128)S(1)} async-done(((f32[32,1,128]{2,1,0:T(1,128)}), f32[32,1,128]{2,1,0:T(1,128)S(1)}, u32[]{:S(2)}, u32[]{:S(2)}) %all-to-all-start.1) | async-done | bytes 16416 | tf_op jit(solution)/shard_map/all_to_all | solution.py:333
  57.4 0.1 shard_map.57
Async XLA Ops:
  0.6 12.5 %copy-start = (f32[5,8,16,256]{3,2,1,0:T(8,128)S(1)}, f32[5,8,16,256]{3,2,1,0:T(8,128)}, u32[]{:S(2)}) copy-start(f32[5,8,16,256]{3,2,1,0:T(8,128)} %start.3) | copy-start | bytes 1966084
  1.7 30.4 %collective-permute-start = (f32[5,4,16,256]{3,2,1,0:T(8,128)S(1)}, f32[5,4,16,256]{3,2,1,0:T(8,128)S(1)}, u32[]{:S(2)}, u32[]{:S(2)}) collective-permute-start(f32[5,4,16,256]{3,2,1,0:T(8,128)S(1)} %shard_map.51), channel_id=1, source_target_pairs={{16,32},{48,64},{80,96},{112,128},{144,160},{176,192},{208,224},{2... | collective-permute-start | bytes 983048 | tf_op jit(solution)/shard_map/ppermute | solution.py:289
  13.2 18.9 %collective-permute-start.1 = (f32[5,4,8,256]{3,2,1,0:T(8,128)S(1)}, f32[5,4,8,256]{3,2,1,0:T(8,128)S(1)}, u32[]{:S(2)}, u32[]{:S(2)}) collective-permute-start(f32[5,4,8,256]{3,2,1,0:T(8,128)S(1)} %get-tuple-element.11), channel_id=1, source_target_pairs={{1,2},{3,4},{5,6},{7,8},{9,10},{11,12},{13,14},{15,0},{2,1},{4,3},... | collective-permute-start | bytes 491528 | tf_op jit(solution)/shard_map/ppermute | solution.py:289
  17.1 15.8 %collective-permute-start.3 = (f32[5,4,16,256]{3,2,1,0:T(8,128)S(1)}, f32[5,4,16,256]{3,2,1,0:T(8,128)S(1)}, u32[]{:S(2)}, u32[]{:S(2)}) collective-permute-start(f32[5,4,16,256]{3,2,1,0:T(8,128)S(1)} %get-tuple-element.13), channel_id=1, source_target_pairs={{0,16},{32,48},{64,80},{96,112},{128,144},{160,176},{192,208},{224... | collective-permute-start | bytes 983048 | tf_op jit(solution)/shard_map/ppermute | solution.py:289
  19.1 13.5 %collective-permute-start.2 = (f32[5,4,8,256]{3,2,1,0:T(8,128)S(1)}, f32[5,4,8,256]{3,2,1,0:T(8,128)S(1)}, u32[]{:S(2)}, u32[]{:S(2)}) collective-permute-start(f32[5,4,8,256]{3,2,1,0:T(8,128)S(1)} %get-tuple-element.12), channel_id=1, source_target_pairs={{0,1},{2,3},{4,5},{6,7},{8,9},{10,11},{12,13},{14,15},{1,0},{3,2},... | collective-permute-start | bytes 491528 | tf_op jit(solution)/shard_map/ppermute | solution.py:289
  44.2 13.3 %all-to-all-start.1 = ((f32[32,1,128]{2,1,0:T(1,128)}), f32[32,1,128]{2,1,0:T(1,128)S(1)}, u32[]{:S(2)}, u32[]{:S(2)}) async-start(f32[32,1,128]{2,1,0:T(1,128)} %bitcast.5), calls=%async_computation.1 | async-start | bytes 32768 | tf_op jit(solution)/shard_map/all_to_all | solution.py:333

commit v13 on v12

--- a/solution.py
+++ b/solution.py
@@ -16,7 +16,7 @@
 AXES = ("z_lo", "y", "z_hi", "x", "core")
 SIZES = (4, 8, 2, 4, 2)
 GX, GY = AXES[:2], AXES[2:]
-NEAR, FAR = ("y", "core"), ("z_lo", "z_hi", "x")
+NEAR, FAR = ("y", "x", "core"), ("z_lo", "z_hi")
 VMEM = pltpu.VMEM
 SMEM = pltpu.SMEM
 PACK_COST, INNER_COST, ODD_COST, EVEN_COST = 1 << 20, 1 << 20, 7 << 20, 1 << 19

time: 58.5 us -> 58.3 us (level)
  blocking collectives: 10.2 us -> 13.6 us
  waiting for transfers between devices: 7.83 us -> 5.6 us
  starting transfers between devices: 30.3 us -> 29 us
    all_to_all x1, blocking collectives: 10.2 us -> 13.6 us  [local(): peaks = lax.all_to_all(peak, NEAR, 0, 0, tiled=True)]
    all_to_all x1, waiting for transfers between devices: 7.82 us -> 5.59 us  [local(): peaks = lax.all_to_all(peak, FAR, 0, 0, tiled=True)]
    all_to_all x1, starting transfers between devices: 4.61 us -> 3.31 us  [local(): peaks = lax.all_to_all(peak, FAR, 0, 0, tiled=True)]
where the time goes in v13:
time: 58.3 us; the launch traced here: 57.9 us
  starting transfers between devices  29 us (50%)
  blocking collectives  13.6 us (23%)
  Pallas kernels  6.93 us (12%)
  waiting for transfers between devices  5.6 us (10%)
  between operations  1.92 us (3%)
  local copies, waits for them, and re-layouts  0.84 us (1%)
    ppermute x4, starting transfers between devices, swap(): return lax.ppermute(x, axis, pairs + [(b, a) for a, b in pairs])  25.7 us
    all_to_all x1, blocking collectives, local(): peaks = lax.all_to_all(peak, NEAR, 0, 0, tiled=True)  13.6 us
    pallas_call x8, Pallas kernels, call(): pl.pallas_call(kernel, out_shape=outs, in_specs=[pl.BlockSpec(memory_spac...  6.93 us
    all_to_all x1, waiting for transfers between devices, local(): peaks = lax.all_to_all(peak, FAR, 0, 0, tiled=True)  5.59 us
    all_to_all x1, starting transfers between devices, local(): peaks = lax.all_to_all(peak, FAR, 0, 0, tiled=True)  3.31 us
  transfers between devices with their start and end apart: 5, of which 1 were waited for; matrix products, arithmetic and copies ran while one was open for 1% of the time, Pallas kernels for 8%

profile of v13, /device:TPU:1, one launch (start us, length us, event | category | flops | bytes accessed | tf_op | source)
XLA Modules:
  0.0 57.9 jit_solution(9987202471412489490)
XLA Ops:
  0.6 0.0 copy-start
  0.6 1.1 %shard_map.51 = f32[5,4,16,256]{3,2,1,0:T(8,128)S(1)} custom-call(f32[5,8,16,256]{3,2,1,0:T(8,128)} %start.3), custom_call_target="tpu_custom_call" | custom-call | tf_op jit(solution)/shard_map/pallas_call | solution.py:271
  1.7 11.4 %collective-permute-start = (f32[5,4,16,256]{3,2,1,0:T(8,128)S(1)}, f32[5,4,16,256]{3,2,1,0:T(8,128)S(1)}, u32[]{:S(2)}, u32[]{:S(2)}) collective-permute-start(f32[5,4,16,256]{3,2,1,0:T(8,128)S(1)} %shard_map.51), channel_id=1, source_target_pairs={{16,32},{48,64},{80,96},{112,128},{144,160},{176,192},{208,224},{2... | collective-permute-start | bytes 983048 | tf_op jit(solution)/shard_map/ppermute | solution.py:289
  13.1 0.0 copy-done
  13.1 0.1 shard_map.52
  13.2 4.0 %collective-permute-start.1 = (f32[5,4,8,256]{3,2,1,0:T(8,128)S(1)}, f32[5,4,8,256]{3,2,1,0:T(8,128)S(1)}, u32[]{:S(2)}, u32[]{:S(2)}) collective-permute-start(f32[5,4,8,256]{3,2,1,0:T(8,128)S(1)} %get-tuple-element.11), channel_id=1, source_target_pairs={{1,2},{3,4},{5,6},{7,8},{9,10},{11,12},{13,14},{15,0},{2,1},{4,3},... | collective-permute-start | bytes 491528 | tf_op jit(solution)/shard_map/ppermute | solution.py:289
  17.1 1.9 %collective-permute-start.3 = (f32[5,4,16,256]{3,2,1,0:T(8,128)S(1)}, f32[5,4,16,256]{3,2,1,0:T(8,128)S(1)}, u32[]{:S(2)}, u32[]{:S(2)}) collective-permute-start(f32[5,4,16,256]{3,2,1,0:T(8,128)S(1)} %get-tuple-element.13), channel_id=1, source_target_pairs={{0,16},{32,48},{64,80},{96,112},{128,144},{160,176},{192,208},{224... | collective-permute-start | bytes 983048 | tf_op jit(solution)/shard_map/ppermute | solution.py:289
  19.1 8.5 %collective-permute-start.2 = (f32[5,4,8,256]{3,2,1,0:T(8,128)S(1)}, f32[5,4,8,256]{3,2,1,0:T(8,128)S(1)}, u32[]{:S(2)}, u32[]{:S(2)}) collective-permute-start(f32[5,4,8,256]{3,2,1,0:T(8,128)S(1)} %get-tuple-element.12), channel_id=1, source_target_pairs={{0,1},{2,3},{4,5},{6,7},{8,9},{10,11},{12,13},{14,15},{1,0},{3,2},... | collective-permute-start | bytes 491528 | tf_op jit(solution)/shard_map/ppermute | solution.py:289
  28.2 3.9 %shard_map.50 = (f32[5,8,16,256]{3,2,1,0:T(8,128)S(1)}, f32[8,128]{1,0:T(8,128)S(1)}) custom-call(f32[1,1]{1,0:T(1,128)} %bitcast.10.speed, f32[5,8,16,256]{3,2,1,0:T(8,128)S(1)} %copy-done, f32[5,8,16,256]{3,2,1,0:T(8,128)} %section_far.1), custom_call_target="tpu_custom_call" | custom-call | flops 314572800 | bytes 1048576 | tf_op jit(solution)/shard_map/pallas_call | solution.py:271
  32.1 0.0 collective-permute-done.1.y_rim
  32.1 0.0 collective-permute-done.x_rim
  32.1 0.5 shard_map.53.inner
  32.6 0.0 collective-permute-done.2.y_rim
  32.6 0.3 shard_map.54.inner
  32.9 0.0 collective-permute-done.3.x_rim
  32.9 0.4 shard_map.55
  33.3 13.6 %all_to_all.22 = f32[64,1,128]{2,1,0:T(1,128)S(1)} all-to-all(f32[64,1,128]{2,1,0:T(1,128)S(1)} %bitcast.12), channel_id=1, replica_groups=mesh['z_lo'=4,'y'=8,'z_hi'=2,'x'=4,'core'=2] {'y','x','core'}, dimensions={0} | all-to-all | bytes 65536 | tf_op jit(solution)/shard_map/all_to_all | solution.py:331
  46.9 0.6 %shard_map.56 = f32[8,128]{1,0:T(8,128)} custom-call(f32[64,128]{1,0:T(8,128)S(1)} %bitcast.11), custom_call_target="tpu_custom_call" | custom-call | tf_op jit(solution)/shard_map/pallas_call | solution.py:271
  47.5 3.3 %all-to-all-start.1 = ((f32[8,1,128]{2,1,0:T(1,128)}), f32[8,1,128]{2,1,0:T(1,128)S(1)}, u32[]{:S(2)}, u32[]{:S(2)}) async-start(f32[8,1,128]{2,1,0:T(1,128)} %bitcast.5), calls=%async_computation.1 | async-start | bytes 8192 | tf_op jit(solution)/shard_map/all_to_all | solution.py:333
  50.9 0.8 %copy.7 = f32[5,8,16,256]{3,2,1,0:T(8,128)} copy(f32[5,8,16,256]{3,2,1,0:T(8,128)S(1)} %get-tuple-element.16) | data formatting | bytes 1310720
  51.7 5.6 %all-to-all-done.1 = f32[8,1,128]{2,1,0:T(1,128)S(1)} async-done(((f32[8,1,128]{2,1,0:T(1,128)}), f32[8,1,128]{2,1,0:T(1,128)S(1)}, u32[]{:S(2)}, u32[]{:S(2)}) %all-to-all-start.1) | async-done | bytes 4128 | tf_op jit(solution)/shard_map/all_to_all | solution.py:333
  57.3 0.1 shard_map.57
Async XLA Ops:
  0.6 12.5 %copy-start = (f32[5,8,16,256]{3,2,1,0:T(8,128)S(1)}, f32[5,8,16,256]{3,2,1,0:T(8,128)}, u32[]{:S(2)}) copy-start(f32[5,8,16,256]{3,2,1,0:T(8,128)} %start.3) | copy-start | bytes 1966084
  1.7 30.4 %collective-permute-start = (f32[5,4,16,256]{3,2,1,0:T(8,128)S(1)}, f32[5,4,16,256]{3,2,1,0:T(8,128)S(1)}, u32[]{:S(2)}, u32[]{:S(2)}) collective-permute-start(f32[5,4,16,256]{3,2,1,0:T(8,128)S(1)} %shard_map.51), channel_id=1, source_target_pairs={{16,32},{48,64},{80,96},{112,128},{144,160},{176,192},{208,224},{2... | collective-permute-start | bytes 983048 | tf_op jit(solution)/shard_map/ppermute | solution.py:289
  13.2 18.9 %collective-permute-start.1 = (f32[5,4,8,256]{3,2,1,0:T(8,128)S(1)}, f32[5,4,8,256]{3,2,1,0:T(8,128)S(1)}, u32[]{:S(2)}, u32[]{:S(2)}) collective-permute-start(f32[5,4,8,256]{3,2,1,0:T(8,128)S(1)} %get-tuple-element.11), channel_id=1, source_target_pairs={{1,2},{3,4},{5,6},{7,8},{9,10},{11,12},{13,14},{15,0},{2,1},{4,3},... | collective-permute-start | bytes 491528 | tf_op jit(solution)/shard_map/ppermute | solution.py:289
  17.1 15.8 %collective-permute-start.3 = (f32[5,4,16,256]{3,2,1,0:T(8,128)S(1)}, f32[5,4,16,256]{3,2,1,0:T(8,128)S(1)}, u32[]{:S(2)}, u32[]{:S(2)}) collective-permute-start(f32[5,4,16,256]{3,2,1,0:T(8,128)S(1)} %get-tuple-element.13), channel_id=1, source_target_pairs={{0,16},{32,48},{64,80},{96,112},{128,144},{160,176},{192,208},{224... | collective-permute-start | bytes 983048 | tf_op jit(solution)/shard_map/ppermute | solution.py:289
  19.1 13.5 %collective-permute-start.2 = (f32[5,4,8,256]{3,2,1,0:T(8,128)S(1)}, f32[5,4,8,256]{3,2,1,0:T(8,128)S(1)}, u32[]{:S(2)}, u32[]{:S(2)}) collective-permute-start(f32[5,4,8,256]{3,2,1,0:T(8,128)S(1)} %get-tuple-element.12), channel_id=1, source_target_pairs={{0,1},{2,3},{4,5},{6,7},{8,9},{10,11},{12,13},{14,15},{1,0},{3,2},... | collective-permute-start | bytes 491528 | tf_op jit(solution)/shard_map/ppermute | solution.py:289
  47.5 9.7 %all-to-all-start.1 = ((f32[8,1,128]{2,1,0:T(1,128)}), f32[8,1,128]{2,1,0:T(1,128)S(1)}, u32[]{:S(2)}, u32[]{:S(2)}) async-start(f32[8,1,128]{2,1,0:T(1,128)} %bitcast.5), calls=%async_computation.1 | async-start | bytes 8192 | tf_op jit(solution)/shard_map/all_to_all | solution.py:333
